TPU v7x, 128 devices: a whole 4x4x4 slice. The times are simulated.
128 devices in a mesh: seq: 32 (over y, z, core), batch: 4 (over x).
Axes of the slice: x: 4, y: 4, z: 4, core: 2. Of those that a mesh axis runs over, the one named last changes fastest.
Arguments:
- signal: bfloat16 [4, 4096, 8192], P('batch', 'seq'), may hold values from -6 to 6
- out_grad: bfloat16 [4, 4096, 8192], P('batch', 'seq'), may hold values from -6 to 6
- residues: float32 [8, 8192], replicated, may hold values from -0.3 to 0.3
- log_rates: float32 [8, 512], replicated, as said below
Outputs:
- mixed: bfloat16 [4, 4096, 8192], P('batch', 'seq')
- grad_signal: bfloat16 [4, 4096, 8192], P('batch', 'seq')
- grad_residues: float32 [8, 8192], replicated
- grad_rates: float32 [8, 512], replicated
Inputs may be any that keep to these rules, and one draw needn't show every extreme that they name: Each decay rate exp(log_rates) lies between 0.2 / 4096 and 1 / 30.
All inputs are finite; a program needn't handle non-finite values.
Results may differ from a plain program's by a relative error of at most 0.0012.
Values sent between devices are 32-bit elements; how exact they have to be, the bound alone decides.
No kernel may reach another device: no remote copies, remote signals or barrier semaphores. Data moves between devices by JAX's collectives and lax.ppermute only.
A program may use at most 384 MiB of HBM per device.

v0:
```python
import jax
import jax.numpy as jnp
from jax import lax
from jax.sharding import PartitionSpec as P

M = 8
GROUP = 16


HIGHEST = lax.Precision.HIGHEST
HIGHER = lax.Precision.HIGH


def carried_in(shard, axis, combine, identity, reverse):
    peers, index = (lax.axis_size(axis), lax.axis_index(axis))
    everything = jax.tree.map(lambda part: lax.all_gather(part, axis), shard)
    start = jax.tree.map(
        lambda part, zero: jnp.broadcast_to(jnp.asarray(zero, part.dtype), part.shape),
        shard,
        identity,
    )

    def lap(k, before):
        at = peers - 1 - k if reverse else k
        reached = at > index if reverse else at < index
        new = combine(before, jax.tree.map(lambda part: part[at], everything))
        return jax.tree.map(lambda a, b: jnp.where(reached, a, b), new, before)

    return lax.fori_loop(0, peers, lap, start)


def depthwise(values, kernel, padding, precision):
    return lax.conv_general_dilated(
        values,
        kernel[:, None, :],
        (1,),
        [padding],
        dimension_numbers=("NWC", "WIO", "NWC"),
        feature_group_count=values.shape[2],
        precision=precision,
        preferred_element_type=jnp.float32,
    )


def local(signal, out_grad, residues, log_rates):
    batch_rows, length, channels = signal.shape
    groups = log_rates.shape[1]
    decay_rate = jnp.exp(log_rates)
    offsets = jnp.arange(length + 1, dtype=jnp.float32)
    powers = jnp.exp(-decay_rate[None] * offsets[:, None, None])
    res_group = residues.reshape(M, groups, GROUP)
    kernel = jnp.einsum("kmg,mgi->kgi", powers[:length], res_group, precision=HIGHEST).reshape(
        length, channels
    )
    inputs = signal.astype(jnp.float32)
    cotangent = out_grad.astype(jnp.float32)
    local_out = depthwise(inputs, kernel[::-1], (length - 1, 0), HIGHER)
    local_grad = depthwise(cotangent, kernel, (0, length - 1), HIGHER)
    weights = jnp.stack([powers[:length], offsets[:length, None, None] * powers[:length]])
    starts_table = jnp.stack([powers[:length], offsets[1:, None, None] * powers[1:]])
    input_group = inputs.reshape(batch_rows, length, groups, GROUP)
    grad_group = cotangent.reshape(batch_rows, length, groups, GROUP)
    end_states = jnp.einsum("jsmg,bsgi->jbmgi", weights[:, ::-1], input_group, precision=HIGHER)
    start_sums = jnp.einsum("jtmg,btgi->jbmgi", starts_table, grad_group, precision=HIGHER)
    local_state = end_states[0]
    local_moment = end_states[1]
    start_state = start_sums[0]
    weighted_start = start_sums[1]
    first_pole = powers[1][None, :, :, None]
    start_plain = first_pole * start_state
    empty_state = jnp.zeros_like(local_state)
    span = jnp.full((), float(length), jnp.float32)
    no_span = jnp.zeros((), jnp.float32)

    def join_forward(earlier, later):
        decay = jnp.exp(-decay_rate * later[0])[None, :, :, None]
        return (
            earlier[0] + later[0],
            decay * earlier[1] + later[1],
            decay * (earlier[2] + later[0] * earlier[1]) + later[2],
        )

    def join_backward(earlier, later):
        decay = jnp.exp(-decay_rate * later[0])[None, :, :, None]
        return (earlier[0] + later[0], decay * earlier[1] + later[1])

    forward_out = carried_in(
        (span, local_state, local_moment),
        "seq",
        join_forward,
        (no_span, empty_state, empty_state),
        False,
    )
    carry_state = forward_out[1]
    carry_moment = forward_out[2]
    backward_out = carried_in(
        (span, start_state), "seq", join_backward, (no_span, empty_state), True
    )
    adjoint = backward_out[1]
    out_extra = jnp.einsum(
        "tmg,bmgi->btgi", powers[1:], res_group[None] * carry_state, precision=HIGHEST
    ).reshape(batch_rows, length, channels)
    grad_extra = jnp.einsum(
        "tmg,bmgi->btgi", powers[1:][::-1], res_group[None] * adjoint, precision=HIGHEST
    ).reshape(batch_rows, length, channels)
    mixed = (local_out + out_extra).astype(jnp.bfloat16)
    grad_signal = (local_grad + grad_extra).astype(jnp.bfloat16)
    lag_values = jnp.swapaxes(out_grad, 0, 1).reshape(1, length, batch_rows * channels)
    lag_kernel = jnp.swapaxes(signal, 0, 1).reshape(length, batch_rows * channels)
    lagged = depthwise(lag_values, lag_kernel, (0, length - 1), None)
    lag_sums = jnp.sum(lagged.reshape(length, batch_rows, groups, GROUP), axis=1)
    lag_terms = jnp.einsum("jkmg,kgi->jmgi", weights, lag_sums, precision=HIGHEST)
    residue_part = lag_terms[0] + jnp.sum(carry_state * start_plain, axis=0)
    moment_part = lag_terms[1] + jnp.sum(
        carry_state * weighted_start + carry_moment * start_plain, axis=0
    )
    rate_part = -decay_rate * jnp.sum(res_group * moment_part, axis=2)
    norm_factor = 1.0 / (batch_rows * lax.axis_size("batch") * length * lax.axis_size("seq"))
    grad_residues, grad_rates = lax.psum(
        (residue_part.reshape(M, channels) * norm_factor, rate_part * norm_factor), ("seq", "batch")
    )
    return (mixed, grad_signal, grad_residues, grad_rates)


def solution(mesh):
    placed = (P("batch", "seq", None), P("batch", "seq", None), P(), P())
    return jax.shard_map(
        local,
        mesh=mesh,
        in_specs=placed,
        out_specs=(P("batch", "seq", None), P("batch", "seq", None), P(), P()),
        check_vma=False,
    )
```

profile of v0, /device:TPU:1, one launch (start us, length us, event | category | flops | bytes accessed | tf_op | source)
XLA Modules:
  0.0 932.5 jit_solution(7500349797167476460)
XLA Ops:
  9.6 2.6 multiply_bitcast_fusion.1
  12.2 3.8 pad_maximum_fusion
  16.0 7.2 rev.10
  23.2 3.2 copy.110
  26.4 4.6 fusion.16
  31.0 2.2 fusion.34
  34.0 3.2 copy.120
  37.2 6.4 fusion.9
  43.6 3.0 copy.122
  48.1 55.3 %fusion.7 = f32[1,128,8192]{2,0,1:T(1,128)} fusion(bf16[128,1,8192]{2,0,1:T(8,128)(2,1)} %bitcast.133, bf16[1,128,8192]{2,1,0:T(8,128)(2,1)S(1)} %copy-done.11), kind=kOutput, calls=%fused_computation.16 | convolution fusion | flops 135266304 | bytes 8388608 | tf_op jit(solution)/shard_map/conv_general_dilated | solution.py:33
  103.4 9.8 %copy.129 = f32[1,128,8192]{1,2,0:T(8,128)} copy(f32[1,128,8192]{2,0,1:T(1,128)} %fusion.7) | data formatting | bytes 8388608 | tf_op jit(solution)/shard_map/conv_general_dilated | solution.py:33
  113.2 12.4 %fusion.5 = f32[512,16,2,8]{1,3,2,0:T(8,128)} fusion(f32[128,512,16,1]{0,2,3,1:T(8,128)} %bitcast.123, f32[2,128,8,512]{1,2,3,0:T(8,128)} %get-tuple-element.514), kind=kOutput, calls=%fused_computation.14 | convolution fusion | flops 201326592 | bytes 8912896 | tf_op jit(solution)/shard_map/jkmg,kgi->jmgi/dot_general | solution.py:112
  125.6 3.6 slice.55
  129.9 2.0 broadcast_in_dim_reshape.7
  132.1 2.8 copy.131
  134.9 2.2 copy.132
  138.4 4.2 rev.11
  142.6 11.3 %fusion.23 = f32[512,128,16]{1,2,0:T(8,128)} fusion(f32[8,512,16]{2,1,0:T(8,128)S(1)} %reshape.109, f32[129,8,512]{0,1,2:T(8,128)} %copy-done), kind=kOutput, calls=%fused_computation.31 | convolution fusion | flops 100663296 | bytes 6553600 | tf_op jit(solution)/shard_map/kmg,mgi->kgi/dot_general | solution.py:52
  153.9 9.8 %copy.119 = f32[128,1,8192]{2,1,0:T(1,128)} copy(f32[128,1,8192]{0,2,1:T(8,128)} %bitcast.121) | data formatting | bytes 8388608 | tf_op jit(solution)/shard_map/broadcast_in_dim;reshape | solution.py:35
  163.7 5.7 copy.108
  169.4 33.0 %rev.9 = f32[128,8192]{1,0:T(8,128)} reverse(f32[128,8192]{1,0:T(8,128)} %copy.108), dimensions={0} | reverse | bytes 8388608 | tf_op jit(solution)/shard_map/rev | solution.py:57
  202.4 6.7 broadcast_in_dim.16
  210.4 66.5 %all-reduce = f32[32]{0:T(128)S(1)} all-reduce(f32[32]{0:T(128)S(1)} %dynamic-update-slice), channel_id=1, replica_groups=mesh['seq'=32,'batch'=4] {'seq'}, use_global_device_ids=true, to_apply=%add | all-reduce | flops 32 | bytes 256
  276.9 39.0 %copy.113 = f32[32,1,8,512,16]{3,4,2,1,0:T(8,128)} copy(f32[32,1,8,512,16]{4,2,0,3,1:T(8,128)} %all-gather.4.cloned.1.call-done) | data formatting | bytes 16777216
  316.0 159.4 %all-gather.6.cloned.1.call-done = f32[32,1,8,512,16]{4,2,0,3,1:T(8,128)} async-done(((f32[1,1,8,512,16]{4,2,0,3,1:T(8,128)}), f32[32,1,8,512,16]{4,2,0,3,1:T(8,128)}) %all-gather.6.cloned.1.call-update) | async-done | bytes 8388624 | tf_op jit(solution)/shard_map/all_gather | solution.py:16
  475.4 38.8 %copy.114 = f32[32,1,8,512,16]{3,4,2,1,0:T(8,128)} copy(f32[32,1,8,512,16]{4,2,0,3,1:T(8,128)} %all-gather.6.cloned.1.call-done) | data formatting | bytes 16777216
  514.2 102.5 %while.34 = (s32[]{:T(128)}, f32[1,8,512,16]{2,3,1,0:T(8,128)S(1)}, f32[1,8,512,16]{2,3,1,0:T(8,128)S(1)}, s32[]{:T(128)}, f32[32]{0:T(128)S(1)}, /*index=5*/f32...) while((s32[]{:T(128)}, f32[1,8,512,16]{2,3,1,0:T(8,128)S(1)}, ...), condition=%wide.region_1.2_spmd.clone, body=%wide.region_0.1_spmd.clone.sunk | while | flops 659460 | bytes 1622161 | solution.py:29
  515.4 2.0 fusion.44
  518.6 1.9 fusion.44
  521.9 1.9 fusion.44
  525.1 2.0 fusion.44
  528.3 1.9 fusion.44
  531.5 1.9 fusion.44
  534.7 1.9 fusion.44
  537.9 1.9 fusion.44
  541.1 1.9 fusion.44
  544.3 1.9 fusion.44
  547.5 1.9 fusion.44
  550.7 1.9 fusion.44
  553.9 1.9 fusion.44
  557.1 1.9 fusion.44
  560.3 1.9 fusion.44
  563.5 1.9 fusion.44
  566.7 1.9 fusion.44
  569.9 1.9 fusion.44
  573.1 1.9 fusion.44
  576.3 1.9 fusion.44
  579.5 1.9 fusion.44
  582.7 1.9 fusion.44
  585.9 1.9 fusion.44
  608.3 1.9 fusion.44
  616.7 2.0 copy.115
  621.7 4.0 mul.217
  625.8 78.4 %while.35 = (s32[]{:T(128)}, f32[1,8,512,16]{2,3,1,0:T(8,128)S(1)}, s32[]{:T(128)}, f32[32]{0:T(128)S(1)}, f32[1,8,512,1]{2,1,3,0:T(8,128)S(1)}, /*index=5*/f32[...) while((s32[]{:T(128)}, f32[1,8,512,16]{2,3,1,0:T(8,128)S(1)}, ...), condition=%wide.region_3.4_spmd.clone, body=%wide.region_2.3_spmd.clone.sunk | while | flops 266248 | bytes 835771 | solution.py:29
  706.1 4.0 multiply_bitcast_fusion
  710.2 10.0 %fusion.19 = f32[512,16,128]{2,1,0:T(8,128)} fusion(f32[128,8,512]{0,1,2:T(8,128)S(1)} %copy-done.3, f32[8,512,16]{2,1,0:T(8,128)S(1)} %get-tuple-element.511), kind=kOutput, calls=%fused_computation.27 | convolution fusion | flops 100663296 | bytes 6553600 | tf_op jit(solution)/shard_map/tmg,bmgi->btgi/dot_general | solution.py:103
  720.2 9.8 %copy.126 = f32[1,128,8192]{2,0,1:T(1,128)} copy(f32[1,128,8192]{1,2,0:T(8,128)} %bitcast.124) | data formatting | bytes 8388608 | tf_op jit(solution)/shard_map/reshape | solution.py:105
  730.0 12.3 %fusion.21 = f32[512,16,128]{2,1,0:T(8,128)} fusion(f32[8,512,16]{2,1,0:T(8,128)S(1)} %copy-done.2, f32[129,8,512]{0,1,2:T(8,128)} %copy-done), kind=kOutput, calls=%fused_computation.29 | convolution fusion | flops 100663296 | bytes 6553600 | tf_op jit(solution)/shard_map/tmg,bmgi->btgi/dot_general | solution.py:100
  742.4 9.8 %copy.117 = f32[1,128,8192]{2,0,1:T(1,128)} copy(f32[1,128,8192]{1,2,0:T(8,128)} %bitcast.125) | data formatting | bytes 8388608 | tf_op jit(solution)/shard_map/reshape | solution.py:102
  752.2 47.7 %fusion.3 = bf16[1,128,8192]{2,0,1:T(2,128)(2,1)} fusion(f32[1,128,8192]{2,0,1:T(1,128)} %copy.126, f32[128,1,8192]{2,1,0:T(1,128)} %copy.119, bf16[1,128,8192]{2,1,0:T(8,128)(2,1)S(1)} %copy-done.12), kind=kOutput, calls=%fused_computation.9 | convolution fusion | flops 407896064 | bytes 12582912 | tf_op jit(solution)/shard_map/conv_general_dilated | solution.py:33
  800.0 46.6 %fusion.4 = bf16[1,128,8192]{2,0,1:T(2,128)(2,1)} fusion(f32[1,128,8192]{2,0,1:T(1,128)S(1)} %copy-done.8, f32[128,1,8192]{2,1,0:T(1,128)S(1)} %copy-done.7, bf16[1,128,8192]{2,1,0:T(8,128)(2,1)S(1)} %copy-done.13), kind=kOutput, calls=%fused_computation.11 | convolution fusion | flops 407896064 | bytes 12582912 | tf_op jit(solution)/shard_map/conv_general_dilated | solution.py:33
  846.7 66.9 %psum.15 = f32[8,512]{0,1:T(8,128)S(1)} all-reduce(f32[8,512]{0,1:T(8,128)S(1)} %multiply_multiply_fusion), channel_id=1, replica_groups=mesh['seq'=32,'batch'=4] {'seq','batch'}, use_global_device_ids=true, to_apply=%region_6.7 | all-reduce | flops 4096 | bytes 32768 | tf_op jit(solution)/shard_map/psum | solution.py:119
  914.3 5.9 copy.137
  920.3 3.6 copy.136
  (243 shorter events, 147.7 us)
Async XLA Ops:
  7.2 269.7 %all-gather.4.cloned.1.call-start = ((), (), s32[]{:S(2)}) async-start(), calls=%async_computation | async-start | bytes 69206016 | tf_op jit(solution)/shard_map/all_gather | solution.py:16
  8.1 4.1 copy-start.9
  9.5 2.7 copy-start
  33.2 442.2 %all-gather.6.cloned.1.call-start = ((), (), s32[]{:S(2)}) async-start(), calls=%async_computation.1 | async-start | bytes 69206016 | tf_op jit(solution)/shard_map/all_gather | solution.py:16
  33.9 591.8 %all-gather.8.cloned.1.call-start = ((), (), s32[]{:S(2)}) async-start(), calls=%async_computation.2 | async-start | bytes 8650752 | tf_op jit(solution)/shard_map/all_gather | solution.py:16
  43.6 4.4 copy-start.11
  46.7 56.7 %copy-start.4 = (f32[512,2,8,16]{0,3,2,1:T(8,128)}, f32[512,2,8,16]{0,3,2,1:T(8,128)S(1)}, u32[]{:S(2)}) copy-start(f32[512,2,8,16]{0,3,2,1:T(8,128)S(1)} %copy.122) | copy-start | bytes 1572868
  47.5 876.4 %all-reduce.3.cloned.1.call-start = ((), (), s32[]{:S(2)}) async-start(), calls=%async_computation.3 | async-start | bytes 524288 | tf_op jit(solution)/shard_map/psum | solution.py:119
  125.6 3.7 copy-start.14
  125.6 6.4 copy-start.17
  202.4 6.7 copy-start.18
  514.2 104.5 %copy-start.5 = (f32[512,2,8,16]{0,3,2,1:T(8,128)S(1)}, f32[512,2,8,16]{0,3,2,1:T(8,128)}, u32[]{:S(2)}) copy-start(f32[512,2,8,16]{0,3,2,1:T(8,128)} %copy-done.4) | copy-start | bytes 1572868
  514.2 104.5 %copy-start.15 = (f32[8,512,16]{1,2,0:T(8,128)S(1)}, f32[8,512,16]{1,2,0:T(8,128)}, u32[]{:S(2)}) copy-start(f32[8,512,16]{1,2,0:T(8,128)} %copy.134) | copy-start | bytes 786436
  621.7 84.4 %copy-start.1 = (f32[1,8,512,16]{3,2,1,0:T(8,128)S(1)}, f32[1,8,512,16]{3,2,1,0:T(8,128)}, u32[]{:S(2)}) copy-start(f32[1,8,512,16]{3,2,1,0:T(8,128)} %broadcast_in_dim_reshape.7) | copy-start | bytes 786436
  706.1 4.0 copy-start.3
  720.2 9.8 %copy-start.2 = (f32[8,512,16]{2,1,0:T(8,128)S(1)}, f32[8,512,16]{2,1,0:T(8,128)}, u32[]{:S(2)}) copy-start(f32[8,512,16]{2,1,0:T(8,128)} %get-tuple-element.512) | copy-start | bytes 786436
  742.3 9.8 %copy-start.12 = (bf16[1,128,8192]{2,1,0:T(8,128)(2,1)S(1)}, bf16[1,128,8192]{2,1,0:T(8,128)(2,1)}, u32[]{:S(2)}) copy-start(bf16[1,128,8192]{2,1,0:T(8,128)(2,1)} %param.9) | copy-start | bytes 6291460
  752.2 47.8 %copy-start.7 = (f32[128,1,8192]{2,1,0:T(1,128)S(1)}, f32[128,1,8192]{2,1,0:T(1,128)}, u32[]{:S(2)}) copy-start(f32[128,1,8192]{2,1,0:T(1,128)} %broadcast_in_dim.16) | copy-start | bytes 12582916
  752.2 47.8 %copy-start.8 = (f32[1,128,8192]{2,0,1:T(1,128)S(1)}, f32[1,128,8192]{2,0,1:T(1,128)}, u32[]{:S(2)}) copy-start(f32[1,128,8192]{2,0,1:T(1,128)} %copy.117) | copy-start | bytes 12582916
  752.2 47.8 %copy-start.13 = (bf16[1,128,8192]{2,1,0:T(8,128)(2,1)S(1)}, bf16[1,128,8192]{2,1,0:T(8,128)(2,1)}, u32[]{:S(2)}) copy-start(bf16[1,128,8192]{2,1,0:T(8,128)(2,1)} %param.8) | copy-start | bytes 6291460
  800.0 46.6 %copy-start.10 = (f32[8,512]{0,1:T(8,128)S(1)}, f32[8,512]{0,1:T(8,128)}, u32[]{:S(2)}) copy-start(f32[8,512]{0,1:T(8,128)} %copy-done.9) | copy-start | bytes 49156
  800.0 46.6 %copy-start.16 = (f32[8,512]{0,1:T(8,128)S(1)}, f32[8,512]{0,1:T(8,128)}, u32[]{:S(2)}) copy-start(f32[8,512]{0,1:T(8,128)} %copy.142) | copy-start | bytes 49156
  914.3 6.0 copy-start.6
Sparse Core Ops, SparseCore 0:
  33.3 221.2 all-gather.3
  256.8 218.5 all-gather.5
  477.7 54.0 all-gather.7
  625.9 142.4 all-reduce.2
where the time goes:
time: 947 us; the launch traced here: 932 us
  local copies, waits for them, and re-layouts  262 us (28%)
  matrix products  207 us (22%)
  waiting for transfers between devices  160 us (17%)
  other arithmetic  153 us (16%)
  blocking collectives  133 us (14%)
  between operations  14.4 us (2%)
    all_gather x3, waiting for transfers between devices, carried_in(): everything = jax.tree.map(lambda part: lax.all_gather(part, axis), shard)  159 us
    conv_general_dilated x3, matrix products, depthwise(): lax.conv_general_dilated(values, kernel[:, None, :], (1,), [padding], dim...  150 us
    select_n x64, other arithmetic, lap(): return jax.tree.map(lambda a, b: jnp.where(reached, a, b), new, before)  99.3 us
    unnamed x51, local copies, waits for them, and re-layouts  98.5 us
    psum x1, blocking collectives, local(): lax.psum((residue_part.reshape(M, channels) * norm_factor, rate_part * no...  66.9 us
    unnamed x1, blocking collectives  66.5 us
    dynamic_slice x64, local copies, waits for them, and re-layouts, lap(): new = combine(before, jax.tree.map(lambda part: part[at], everything))  37.5 us
    rev x1, local copies, waits for them, and re-layouts, local(): local_out = depthwise(inputs, kernel[::-1], (length - 1, 0), HIGHER)  33 us
  transfers between devices with their start and end apart: 4, of which 1 were waited for; matrix products, arithmetic and copies ran while one was open for 64% of the time, Pallas kernels for 0%

commit v1 on v0

v1 whole, which is shorter than its diff:
```python
import functools

import jax
import jax.numpy as jnp
import numpy as np
from jax import lax
from jax.experimental import pallas as pl
from jax.experimental.pallas import tpu as pltpu
from jax.sharding import PartitionSpec as P

M = 8
GROUP = 16
SPAN = 128
SLICE = 256
GROUPS = SLICE // GROUP
WIDE = 512
PER = WIDE // SLICE
F32 = jnp.float32
BF16 = jnp.bfloat16


def split_np(values):
    high = values.astype(np.float32).astype(jnp.bfloat16)
    low = (values - high.astype(np.float64)).astype(np.float32).astype(jnp.bfloat16)
    return high, low


def transforms():
    time = np.arange(SPAN)
    angle = 2 * np.pi * np.outer(np.arange(SPAN) + 0.5, time) / (2 * SPAN)
    forward = np.concatenate([np.cos(angle), -np.sin(angle)], 0)
    inverse = np.concatenate([np.cos(angle.T), -np.sin(angle.T)], 1) / SPAN
    fh, fl = split_np(forward)
    ih, il = split_np(inverse)
    return np.concatenate([fh, fl, fh], 1), np.concatenate([ih, il, ih], 1)


def split(values):
    high = values.astype(BF16)
    return high, (values - high.astype(F32)).astype(BF16)


def dot(a, b):
    return jnp.dot(a, b, preferred_element_type=F32)


def twice(values):
    return jnp.concatenate([values, values], 0)


def stacked(values):
    high, low = split(values)
    return jnp.concatenate([high, high, low], 0)


def lane_group(rows, lanes):
    return lax.broadcasted_iota(jnp.int32, (rows, lanes), 1) // GROUP


def spread(values):
    high = values.astype(BF16).astype(F32)
    low = values - high
    owner = lane_group(M, SLICE)

    def rows(part):
        return jnp.concatenate([jnp.where(owner == g, part, 0.0) for g in range(GROUPS)], 0).astype(BF16)

    top = rows(high)
    return jnp.concatenate([top, top, rows(low)], 0)


def powers(rate_row, reverse):
    t = lax.broadcasted_iota(jnp.int32, (SPAN, SPAN), 0)
    t = (SPAN - 1 - t if reverse else t).astype(F32)
    high, low = split(jnp.exp(-rate_row[0:1, :] * t))
    return jnp.concatenate([high, low, high], 1)


def first_kernel(x_ref, g_ref, rate_ref, res_ref, fwd_ref, inv_ref, send_ref):
    x, g = x_ref[0], g_ref[0]
    xx, gg = twice(x), twice(g)
    forward = fwd_ref[:, : 2 * SPAN]
    xf = dot(forward, xx)
    gf = dot(forward, gg)
    xr, xi, gr, gi = xf[:SPAN], xf[SPAN:], gf[:SPAN], gf[SPAN:]
    lags = dot(inv_ref[...], stacked(jnp.concatenate([gr * xr + gi * xi, gi * xr - gr * xi], 0)))
    lag3 = stacked(lags)
    lag = lax.broadcasted_iota(jnp.int32, (SPAN, SPAN), 1).astype(F32)
    back = (SPAN - 1) - lag
    half = SPAN // GROUP
    owner = lane_group(M, SPAN)
    row = lax.broadcasted_iota(jnp.int32, (SPAN, SPAN), 0) // GROUP
    col = lax.broadcasted_iota(jnp.int32, (SPAN, SPAN), 1)

    def pick(values, q):
        at = q * half * M
        chosen = values[at : at + M]
        for k in range(1, half):
            chosen = jnp.where(owner == k, values[at + k * M : at + (k + 1) * M], chosen)
        return chosen

    for s in range(PER):
        rates = jnp.transpose(jnp.broadcast_to(rate_ref[s, 0:1, :], (SPAN, SPAN)))
        early, late = jnp.exp(-rates * lag), jnp.exp(-rates * back)
        rate_sum = jnp.zeros((M, SPAN), F32)
        for h in range(2):
            rows = slice(h * half * M, (h + 1) * half * M)
            cols = slice(s * SLICE + h * SPAN, s * SLICE + (h + 1) * SPAN)
            eh, el = split(jnp.concatenate([early[rows], lag[rows] * early[rows]], 0))
            lh, ll = split(jnp.concatenate([late[rows], back[rows] * late[rows]], 0))
            ends = dot(jnp.concatenate([lh, ll], 1), xx[:, cols])
            starts = dot(jnp.concatenate([eh, el], 1), gg[:, cols])
            sums = dot(jnp.concatenate([eh, el, eh], 1), lag3[:, cols])
            for q, values in enumerate((pick(ends, 0), pick(starts, 0), pick(ends, 1), pick(starts, 1), pick(sums, 0))):
                at = (2 * q + h) * M
                send_ref[s, at : at + M, :] = values
            weighted = res_ref[:, cols] * pick(sums, 1)
            place = jnp.where(row + h * half == col, 1.0, 0.0).astype(BF16)
            wh, wl = split(weighted)
            rate_sum = rate_sum + dot(wh, place) + dot(wl, place)
        send_ref[s, 10 * M : 11 * M, :] = rate_sum


def second_kernel(x_ref, g_ref, rate_ref, res_ref, fwd_ref, inv_ref, mixed_ref, grad_ref):
    forward = fwd_ref[:, : 2 * SPAN]
    for s in range(PER):
        cols = slice(s * SLICE, (s + 1) * SLICE)
        taps = dot(powers(rate_ref[s], False), spread(res_ref[:, cols]))
        kf = dot(fwd_ref[...], stacked(taps))
        xf = dot(forward, twice(x_ref[0, :, cols]))
        gf = dot(forward, twice(g_ref[0, :, cols]))
        kr, ki, xr, xi, gr, gi = kf[:SPAN], kf[SPAN:], xf[:SPAN], xf[SPAN:], gf[:SPAN], gf[SPAN:]
        mixed_ref[:, cols] = dot(inv_ref[...], stacked(jnp.concatenate([kr * xr - ki * xi, kr * xi + ki * xr], 0)))
        grad_ref[:, cols] = dot(inv_ref[...], stacked(jnp.concatenate([kr * gr + ki * gi, kr * gi - ki * gr], 0)))


def middle_kernel(chunks, got_ref, rate_ref, res_ref, back_ref, sums_ref):
    rate_sum = jnp.zeros((M, SPAN), F32)
    for k in range(chunks):
        rate_sum = rate_sum + got_ref[k, 10 * M : 11 * M, :]
    row = lax.broadcasted_iota(jnp.int32, (SPAN, SPAN), 0) // GROUP
    col = lax.broadcasted_iota(jnp.int32, (SPAN, SPAN), 1)
    for h in range(2):
        cols = slice(h * SPAN, (h + 1) * SPAN)
        rate, res = rate_ref[:, cols], res_ref[:, cols]
        pole = jnp.exp(-rate)
        across = jnp.exp(-rate * SPAN)
        handed = res * pole

        def part(k, q):
            at = (2 * q + h) * M
            return got_ref[k, at : at + M, :]

        zero = jnp.zeros((M, SPAN), F32)
        state, moment, res_part, res_carry, rate_carry = zero, zero, zero, zero, zero
        for k in range(chunks):
            back_ref[k, h * M : (h + 1) * M, :] = handed * state
            start = part(k, 1)
            res_part = res_part + part(k, 4)
            res_carry = res_carry + state * start
            rate_carry = rate_carry + state * (part(k, 3) + start) + moment * start
            moment = across * (moment + SPAN * state) + part(k, 2)
            state = across * state + part(k, 0)
        adjoint = zero
        for k in reversed(range(chunks)):
            back_ref[k, (2 + h) * M : (3 + h) * M, :] = handed * adjoint
            adjoint = across * adjoint + part(k, 1)
        sums_ref[h * M : (h + 1) * M, :] = res_part + pole * res_carry
        weighted = handed * rate_carry
        place = jnp.where(row + h * (SPAN // GROUP) == col, 1.0, 0.0).astype(BF16)
        wh, wl = split(weighted)
        rate_sum = rate_sum + dot(wh, place) + dot(wl, place)
    sums_ref[2 * M : 3 * M, :] = rate_sum


def last_kernel(mixed_ref, grad_ref, rate_ref, got_ref, mixed_out, grad_out):
    for s in range(PER):
        cols = slice(s * SLICE, (s + 1) * SLICE)
        state = jnp.concatenate([got_ref[s, 0:M, :], got_ref[s, M : 2 * M, :]], 1)
        adjoint = jnp.concatenate([got_ref[s, 2 * M : 3 * M, :], got_ref[s, 3 * M : 4 * M, :]], 1)
        more = dot(powers(rate_ref[s], False), spread(state))
        mixed_out[0, :, cols] = (mixed_ref[:, cols] + more).astype(BF16)
        more = dot(powers(rate_ref[s], True), spread(adjoint))
        grad_out[0, :, cols] = (grad_ref[:, cols] + more).astype(BF16)


def local(signal, out_grad, residues, log_rates):
    channels = signal.shape[2]
    chunks, rows = lax.axis_size("seq"), lax.axis_size("batch")
    index = lax.axis_index("seq")
    steps = channels // WIDE
    fwd, inv = (jnp.asarray(v) for v in transforms())
    decay_rate = jnp.exp(log_rates)
    rate_rows = jnp.broadcast_to(decay_rate.T.reshape(chunks, 1, SPAN), (chunks, M, SPAN))
    own_rate = jnp.repeat(lax.dynamic_slice_in_dim(decay_rate, index * GROUPS, GROUPS, 1), GROUP, axis=1)
    own_res = lax.dynamic_slice_in_dim(residues, index * SLICE, SLICE, 1)

    seq_block = pl.BlockSpec((1, SPAN, WIDE), lambda i: (0, 0, i))
    flat_block = pl.BlockSpec((SPAN, WIDE), lambda i: (0, i))
    rate_block = pl.BlockSpec((PER, M, SPAN), lambda i: (i, 0, 0))
    res_block = pl.BlockSpec((M, WIDE), lambda i: (0, i))
    whole = lambda a: pl.BlockSpec(a.shape, lambda i: (0,) * a.ndim)
    params = pltpu.CompilerParams(vmem_limit_bytes=32 * 2**20)
    both = 2 * SPAN * channels

    send = pl.pallas_call(
        first_kernel,
        grid=(steps,),
        in_specs=[seq_block, seq_block, rate_block, res_block, whole(fwd), whole(inv)],
        out_specs=pl.BlockSpec((PER, 11 * M, SPAN), lambda i: (i, 0, 0)),
        out_shape=jax.ShapeDtypeStruct((chunks, 11 * M, SPAN), F32),
        compiler_params=params,
        name="ends_and_lags",
    )(signal, out_grad, rate_rows, residues, fwd, inv)
    got = lax.all_to_all(send, "seq", 0, 0, tiled=True)

    mixed_part, grad_part = pl.pallas_call(
        second_kernel,
        grid=(steps,),
        in_specs=[seq_block, seq_block, rate_block, res_block, whole(fwd), whole(inv)],
        out_specs=[flat_block, flat_block],
        out_shape=[jax.ShapeDtypeStruct((SPAN, channels), F32)] * 2,
        compiler_params=params,
        cost_estimate=pl.CostEstimate(flops=both * 3000, bytes_accessed=both * 8, transcendentals=both),
        name="local_convolutions",
    )(signal, out_grad, rate_rows, residues, fwd, inv)

    back, sums = pl.pallas_call(
        functools.partial(middle_kernel, chunks),
        out_shape=[
            jax.ShapeDtypeStruct((chunks, 4 * M, SPAN), F32),
            jax.ShapeDtypeStruct((3 * M, SPAN), F32),
        ],
        name="carries",
    )(got, own_rate, own_res)
    carried = lax.all_to_all(back, "seq", 0, 0, tiled=True)
    total = sums
    for k in range(1, rows):
        total = total + lax.ppermute(sums, "batch", [(i, (i + k) % rows) for i in range(rows)])
    total = total * (1.0 / (rows * chunks * SPAN))
    everyone = lax.all_to_all(jnp.broadcast_to(total[None], (chunks, 3 * M, SPAN)), "seq", 0, 0, tiled=True)

    mixed, grad_signal = pl.pallas_call(
        last_kernel,
        grid=(steps,),
        in_specs=[
            flat_block,
            flat_block,
            rate_block,
            pl.BlockSpec((PER, 4 * M, SPAN), lambda i: (i, 0, 0)),
        ],
        out_specs=[seq_block, seq_block],
        out_shape=[jax.ShapeDtypeStruct(signal.shape, BF16)] * 2,
        compiler_params=params,
        cost_estimate=pl.CostEstimate(flops=both * 800, bytes_accessed=both * 6, transcendentals=both),
        name="add_carries",
    )(mixed_part, grad_part, rate_rows, carried)
    grad_residues = everyone[:, : 2 * M].reshape(chunks, 2, M, SPAN).transpose(2, 0, 1, 3).reshape(M, channels)
    grad_rates = -decay_rate * everyone[:, 2 * M :, :GROUPS].transpose(1, 0, 2).reshape(M, chunks * GROUPS)
    return mixed, grad_signal, grad_residues, grad_rates


def solution(mesh):
    placed = P("batch", "seq", None)
    return jax.shard_map(
        local,
        mesh=mesh,
        in_specs=(placed, placed, P(), P()),
        out_specs=(placed, placed, P(), P()),
        check_vma=False,
    )
```

time: 947 us -> 139 us (0.15); the launches traced: 932 us -> 138 us
  local copies, waits for them, and re-layouts: 262 us -> 21.1 us
  matrix products: 207 us -> 0 us
  other arithmetic: 153 us -> 1.33 us
  waiting for transfers between devices: 160 us -> 23.1 us
  blocking collectives: 133 us -> 16 us
  Pallas kernels: 0 us -> 58.6 us
  starting transfers between devices: 0.68 us -> 17.1 us
  between operations: 14.4 us -> 0.79 us
    all_gather x3 -> x0, waiting for transfers between devices: 159 us -> none  [carried_in(): everything = jax.tree.map(lambda part: lax.all_gather(part, axis), shard)]
    conv_general_dilated x3 -> x0, matrix products: 150 us -> none  [depthwise(): lax.conv_general_dilated(values, kernel[:, None, :], (1,), [padding], dim...]
    select_n x64 -> x0, other arithmetic: 99.3 us -> none  [lap(): return jax.tree.map(lambda a, b: jnp.where(reached, a, b), new, before)]
    unnamed x51 -> x30, local copies, waits for them, and re-layouts: 98.5 us -> 15.9 us
    psum x1 -> x0, blocking collectives: 66.9 us -> none  [local(): lax.psum((residue_part.reshape(M, channels) * norm_factor, rate_part * no...]
    unnamed x1 -> x0, blocking collectives: 66.5 us -> none
    pallas_call x0 -> x4, Pallas kernels: none -> 58.6 us  [the longest x1 24.2 us: local(): pl.pallas_call(first_kernel, grid=(steps,), in_specs=[seq_block, seq_bloc...]
    dot_general x6 -> x0, matrix products: 57.1 us -> none  [the longest x1 12.4 us: local(): jnp.einsum('jkmg,kgi->jmgi', weights, lag_sums, precision=HIGHEST)]
  transfers between devices with their start and end apart: 4 -> 5, of which waited for: 1 -> 3; matrix products, arithmetic and copies ran while one was open for 64% -> 3% of each run, Pallas kernels for 0% -> 17%
where the time goes in v1:
time: 139 us; the launch traced here: 138 us
  Pallas kernels  58.6 us (42%)
  waiting for transfers between devices  23.1 us (17%)
  local copies, waits for them, and re-layouts  21.1 us (15%)
  starting transfers between devices  17.1 us (12%)
  blocking collectives  16 us (12%)
    pallas_call x1, Pallas kernels, local(): pl.pallas_call(first_kernel, grid=(steps,), in_specs=[seq_block, seq_bloc...  24.2 us
    pallas_call x1, Pallas kernels, local(): pl.pallas_call(second_kernel, grid=(steps,), in_specs=[seq_block, seq_blo...  23.2 us
    all_to_all x1, waiting for transfers between devices, local(): got = lax.all_to_all(send, 'seq', 0, 0, tiled=True)  19.8 us
    all_to_all x1, blocking collectives, local(): lax.all_to_all(jnp.broadcast_to(total[None], (chunks, 3 * M, SPAN)), 'seq...  16 us
    unnamed x30, local copies, waits for them, and re-layouts  15.9 us
    all_to_all x1, starting transfers between devices, local(): got = lax.all_to_all(send, 'seq', 0, 0, tiled=True)  9.78 us
    pallas_call x1, Pallas kernels, local(): pl.pallas_call(last_kernel, grid=(steps,), in_specs=[flat_block, flat_blo...  8.82 us
    all_to_all x1, starting transfers between devices, local(): carried = lax.all_to_all(back, 'seq', 0, 0, tiled=True)  3.68 us
  transfers between devices with their start and end apart: 5, of which 3 were waited for; matrix products, arithmetic and copies ran while one was open for 3% of the time, Pallas kernels for 17%

profile of v1, /device:TPU:1, one launch (start us, length us, event | category | flops | bytes accessed | tf_op | source)
XLA Modules:
  0.0 138.1 jit_solution(9978667614985919034)
XLA Ops:
  0.6 0.7 fusion
  1.4 0.1 copy.13
  1.5 0.2 broadcast_in_dim.16
  1.7 0.0 copy-start.4
  1.7 1.6 %copy-done.4 = bf16[1,128,8192]{2,1,0:T(8,128)(2,1)S(1)} copy-done((bf16[1,128,8192]{2,1,0:T(8,128)(2,1)S(1)}, bf16[1,128,8192]{2,1,0:T(8,128)(2,1)}, u32[]{:S(2)}) %copy-start.4) | copy-done | bytes 2097176
  3.3 0.0 copy-start.6
  3.3 1.6 %copy-done.6 = bf16[1,128,8192]{2,1,0:T(8,128)(2,1)S(1)} copy-done((bf16[1,128,8192]{2,1,0:T(8,128)(2,1)S(1)}, bf16[1,128,8192]{2,1,0:T(8,128)(2,1)}, u32[]{:S(2)}) %copy-start.6) | copy-done | bytes 2097176
  4.9 0.0 copy-start.8
  4.9 0.9 copy-done.8
  5.8 0.0 copy-start.10
  5.8 0.9 copy-done.10
  6.7 0.0 copy-start.12
  6.7 0.9 copy-done.12
  7.7 24.2 %ends_and_lags.1 = f32[32,88,128]{2,1,0:T(8,128)} custom-call(bf16[1,128,8192]{2,1,0:T(8,128)(2,1)S(1)} %copy-done.4, bf16[1,128,8192]{2,1,0:T(8,128)(2,1)S(1)} %copy-done.6, f32[32,8,128]{2,1,0:T(8,128)S(1)} %broadcast_in_dim.17.rate_ref, f32[8,8192]{1,0:T(8,128)S(1)} %copy-done.8, bf16[256,384]{1,0:T(8,128)(2,1)S(1)} %copy-done.10, ...), custom_call_target="tpu_custom_call" | custom-call | tf_op jit(solution)/shard_map/ends_and_lags/pallas_call | solution.py:206
  31.9 0.0 copy-start.9
  31.9 9.8 %all-to-all-start = ((f32[32,88,128]{2,1,0:T(8,128)}), f32[32,88,128]{2,1,0:T(8,128)}, u32[]{:S(2)}, u32[]{:S(2)}) async-start(f32[32,88,128]{2,1,0:T(8,128)} %ends_and_lags.1), calls=%async_computation | async-start | bytes 2883584 | tf_op jit(solution)/shard_map/all_to_all | solution.py:215
  41.7 0.0 copy-start.5
  41.7 0.0 copy-start.11
  41.7 0.0 copy-start.13
  41.7 0.1 constant_dynamic-slice_fusion.1
  41.8 0.1 broadcast_in_dim.18
  41.9 0.7 reshape.23.rate_ref
  42.6 0.0 copy-done.9
  42.6 0.6 constant_dynamic-slice_fusion.res_ref
  43.2 19.8 %all-to-all-done.got_ref = f32[32,88,128]{2,1,0:T(8,128)} async-done(((f32[32,88,128]{2,1,0:T(8,128)}), f32[32,88,128]{2,1,0:T(8,128)}, u32[]{:S(2)}, u32[]{:S(2)}) %all-to-all-start) | async-done | bytes 1441824 | tf_op jit(solution)/shard_map/all_to_all | solution.py:215
  63.0 2.4 %carries.1 = (f32[32,32,128]{2,1,0:T(8,128)}, f32[24,128]{1,0:T(8,128)}) custom-call(f32[32,88,128]{2,1,0:T(8,128)} %all-to-all-done.got_ref, f32[8,256]{1,0:T(8,128)} %reshape.23.rate_ref, f32[8,256]{1,0:T(8,128)} %constant_dynamic-slice_fusion.res_ref), custom_call_target="tpu_custom_call" | custom-call | tf_op jit(solution)/shard_map/carries/pallas_call | solution.py:228
  65.3 2.5 %collective-permute-start.2 = (f32[24,128]{1,0:T(8,128)}, f32[24,128]{1,0:T(8,128)S(1)}, u32[]{:S(2)}, u32[]{:S(2)}) collective-permute-start(f32[24,128]{1,0:T(8,128)} %get-tuple-element.15), channel_id=1, source_target_pairs={{0,3},{1,0},{2,1},{3,2},{4,7},{5,4},{6,5},{7,6},{8,11},{9,8},{10,9... | collective-permute-start | bytes 36872 | tf_op jit(solution)/shard_map/ppermute | solution.py:239
  67.8 0.5 collective-permute-start.1
  68.3 0.6 collective-permute-start
  69.0 0.0 collective-permute-done.2
  69.0 3.1 %collective-permute-done.1 = f32[24,128]{1,0:T(8,128)S(1)} collective-permute-done((f32[24,128]{1,0:T(8,128)}, f32[24,128]{1,0:T(8,128)S(1)}, u32[]{:S(2)}, u32[]{:S(2)}) %collective-permute-start.1) | collective-permute-done | bytes 12320 | tf_op jit(solution)/shard_map/ppermute | solution.py:239
  72.1 0.2 collective-permute-done
  72.3 0.7 add_multiply_fusion
  73.1 16.0 %all_to_all.15 = f32[32,24,128]{2,1,0:T(8,128)} all-to-all(f32[32,24,128]{2,1,0:T(8,128)S(1)} %broadcast_in_dim.19), channel_id=1, replica_groups=mesh['seq'=32,'batch'=4] {'seq'}, dimensions={0} | all-to-all | bytes 786432 | tf_op jit(solution)/shard_map/all_to_all | solution.py:241
  89.0 3.7 %all-to-all-start.1 = ((f32[32,32,128]{2,1,0:T(8,128)}), f32[32,32,128]{2,1,0:T(8,128)S(1)}, u32[]{:S(2)}, u32[]{:S(2)}) async-start(f32[32,32,128]{2,1,0:T(8,128)} %get-tuple-element.12), calls=%async_computation.1 | async-start | bytes 1048576 | tf_op jit(solution)/shard_map/all_to_all | solution.py:236
  92.7 0.0 copy-done.5
  92.7 0.0 copy-done.11
  92.7 0.0 copy-done.13
  92.8 0.0 copy-start.7
  92.8 1.6 %copy-done.7 = bf16[1,128,8192]{2,1,0:T(8,128)(2,1)S(1)} copy-done((bf16[1,128,8192]{2,1,0:T(8,128)(2,1)S(1)}, bf16[1,128,8192]{2,1,0:T(8,128)(2,1)}, u32[]{:S(2)}) %copy-start.7) | copy-done | bytes 2097176
  94.4 0.0 copy-start.14
  94.4 23.2 %local_convolutions.1 = (f32[128,8192]{1,0:T(8,128)S(1)}, f32[128,8192]{1,0:T(8,128)S(1)}) custom-call(bf16[1,128,8192]{2,1,0:T(8,128)(2,1)S(1)} %copy-done.5, bf16[1,128,8192]{2,1,0:T(8,128)(2,1)S(1)} %copy-done.7, f32[32,8,128]{2,1,0:T(8,128)S(1)} %broadcast_in_dim.17.rate_ref, f32[8,8192]{1,0:T(8,128)S(1)} %copy-done.9, bf16[256,384]{1,0:T(8,128)(2,1)S(1)} %copy-done.11, ...), custom_call_target="tpu_custom_call" | custom-call | flops 6291456000 | bytes 16777216 | tf_op jit(solution)/shard_map/local_convolutions/pallas_call | solution.py:217
  117.6 0.0 copy-start
  117.6 1.9 %copy-done = f32[128,8192]{1,0:T(8,128)} copy-done((f32[128,8192]{1,0:T(8,128)}, f32[128,8192]{1,0:T(8,128)S(1)}, u32[]{:S(2)}) %copy-start) | copy-done | bytes 4194328
  119.5 0.0 copy-start.2
  119.5 2.0 %copy-done.2 = f32[128,8192]{1,0:T(8,128)} copy-done((f32[128,8192]{1,0:T(8,128)}, f32[128,8192]{1,0:T(8,128)S(1)}, u32[]{:S(2)}) %copy-start.2) | copy-done | bytes 4194328
  121.5 0.9 slice_bitcast_fusion
  122.5 0.1 reshape.26
  122.6 1.7 %slice.8 = f32[32,16,128]{2,1,0:T(8,128)} slice(f32[32,24,128]{2,1,0:T(8,128)} %all_to_all.15), slice={[0:32], [0:16], [0:128]} | slice | bytes 524288 | tf_op jit(solution)/shard_map/slice | solution.py:258
  124.3 0.0 copy-done.14
  124.3 0.6 negate_multiply_fusion
  124.9 0.0 all-to-all-done.1.got_ref
  124.9 0.0 copy-start.1
  124.9 2.2 %copy-done.1 = f32[128,8192]{1,0:T(8,128)S(1)} copy-done((f32[128,8192]{1,0:T(8,128)S(1)}, f32[128,8192]{1,0:T(8,128)}, u32[]{:S(2)}) %copy-start.1) | copy-done | bytes 4194328
  127.1 0.0 copy-start.3
  127.1 2.2 %copy-done.3 = f32[128,8192]{1,0:T(8,128)S(1)} copy-done((f32[128,8192]{1,0:T(8,128)S(1)}, f32[128,8192]{1,0:T(8,128)}, u32[]{:S(2)}) %copy-start.3) | copy-done | bytes 4194328
  129.3 8.8 %add_carries.1 = (bf16[1,128,8192]{2,1,0:T(8,128)(2,1)}, bf16[1,128,8192]{2,1,0:T(8,128)(2,1)}) custom-call(f32[128,8192]{1,0:T(8,128)S(1)} %copy-done.1, f32[128,8192]{1,0:T(8,128)S(1)} %copy-done.3, f32[32,8,128]{2,1,0:T(8,128)S(1)} %broadcast_in_dim.17.rate_ref, f32[32,32,128]{2,1,0:T(8,128)S(1)} %all-to-all-done.1.got_ref), custom_call_target="tpu_custom_call" | custom-call | flops 1677721600 | bytes 12582912 | tf_op jit(solution)/shard_map/add_carries/pallas_call | solution.py:243
  (3 shorter events, 0.1 us)
Async XLA Ops:
  1.7 1.6 %copy-start.4 = (bf16[1,128,8192]{2,1,0:T(8,128)(2,1)S(1)}, bf16[1,128,8192]{2,1,0:T(8,128)(2,1)}, u32[]{:S(2)}) copy-start(bf16[1,128,8192]{2,1,0:T(8,128)(2,1)} %x_ref.3) | copy-start | bytes 6291460
  3.3 1.6 %copy-start.6 = (bf16[1,128,8192]{2,1,0:T(8,128)(2,1)S(1)}, bf16[1,128,8192]{2,1,0:T(8,128)(2,1)}, u32[]{:S(2)}) copy-start(bf16[1,128,8192]{2,1,0:T(8,128)(2,1)} %g_ref.3) | copy-start | bytes 6291460
  4.9 0.9 copy-start.8
  5.8 0.9 copy-start.10
  6.7 0.9 copy-start.12
  31.9 10.7 %copy-start.9 = (f32[8,8192]{1,0:T(8,128)S(1)}, f32[8,8192]{1,0:T(8,128)}, u32[]{:S(2)}) copy-start(f32[8,8192]{1,0:T(8,128)} %res_ref.3) | copy-start | bytes 786436
  31.9 31.1 %all-to-all-start = ((f32[32,88,128]{2,1,0:T(8,128)}), f32[32,88,128]{2,1,0:T(8,128)}, u32[]{:S(2)}, u32[]{:S(2)}) async-start(f32[32,88,128]{2,1,0:T(8,128)} %ends_and_lags.1), calls=%async_computation | async-start | bytes 2883584 | tf_op jit(solution)/shard_map/all_to_all | solution.py:215
  41.7 51.1 %copy-start.5 = (bf16[1,128,8192]{2,1,0:T(8,128)(2,1)S(1)}, bf16[1,128,8192]{2,1,0:T(8,128)(2,1)}, u32[]{:S(2)}) copy-start(bf16[1,128,8192]{2,1,0:T(8,128)(2,1)} %x_ref.3) | copy-start | bytes 6291460
  41.7 51.1 %copy-start.11 = (bf16[256,384]{1,0:T(8,128)(2,1)S(1)}, bf16[256,384]{1,0:T(8,128)(2,1)}, u32[]{:S(2)}) copy-start(bf16[256,384]{1,0:T(8,128)(2,1)} %constant.22.clone.fwd_ref) | copy-start | bytes 589828
  41.7 51.1 %copy-start.13 = (bf16[128,768]{1,0:T(8,128)(2,1)S(1)}, bf16[128,768]{1,0:T(8,128)(2,1)}, u32[]{:S(2)}) copy-start(bf16[128,768]{1,0:T(8,128)(2,1)} %constant.23.clone.inv_ref) | copy-start | bytes 589828
  65.3 3.6 %collective-permute-start.2 = (f32[24,128]{1,0:T(8,128)}, f32[24,128]{1,0:T(8,128)S(1)}, u32[]{:S(2)}, u32[]{:S(2)}) collective-permute-start(f32[24,128]{1,0:T(8,128)} %get-tuple-element.15), channel_id=1, source_target_pairs={{0,3},{1,0},{2,1},{3,2},{4,7},{5,4},{6,5},{7,6},{8,11},{9,8},{10,9... | collective-permute-start | bytes 36872 | tf_op jit(solution)/shard_map/ppermute | solution.py:239
  67.8 4.3 %collective-permute-start.1 = (f32[24,128]{1,0:T(8,128)}, f32[24,128]{1,0:T(8,128)S(1)}, u32[]{:S(2)}, u32[]{:S(2)}) collective-permute-start(f32[24,128]{1,0:T(8,128)} %get-tuple-element.15), channel_id=1, source_target_pairs={{0,2},{1,3},{2,0},{3,1},{4,6},{5,7},{6,4},{7,5},{8,10},{9,11},{10,... | collective-permute-start | bytes 36872 | tf_op jit(solution)/shard_map/ppermute | solution.py:239
  68.3 4.0 %collective-permute-start = (f32[24,128]{1,0:T(8,128)}, f32[24,128]{1,0:T(8,128)S(1)}, u32[]{:S(2)}, u32[]{:S(2)}) collective-permute-start(f32[24,128]{1,0:T(8,128)} %get-tuple-element.15), channel_id=1, source_target_pairs={{0,1},{1,2},{2,3},{3,0},{4,5},{5,6},{6,7},{7,4},{8,9},{9,10},{10,1... | collective-permute-start | bytes 36872 | tf_op jit(solution)/shard_map/ppermute | solution.py:239
  89.0 35.8 %all-to-all-start.1 = ((f32[32,32,128]{2,1,0:T(8,128)}), f32[32,32,128]{2,1,0:T(8,128)S(1)}, u32[]{:S(2)}, u32[]{:S(2)}) async-start(f32[32,32,128]{2,1,0:T(8,128)} %get-tuple-element.12), calls=%async_computation.1 | async-start | bytes 1048576 | tf_op jit(solution)/shard_map/all_to_all | solution.py:236
  92.8 1.6 %copy-start.7 = (bf16[1,128,8192]{2,1,0:T(8,128)(2,1)S(1)}, bf16[1,128,8192]{2,1,0:T(8,128)(2,1)}, u32[]{:S(2)}) copy-start(bf16[1,128,8192]{2,1,0:T(8,128)(2,1)} %g_ref.3) | copy-start | bytes 6291460
  94.4 29.9 %copy-start.14 = (f32[8,512]{1,0:T(8,128)S(1)}, f32[8,512]{1,0:T(8,128)}, u32[]{:S(2)}) copy-start(f32[8,512]{1,0:T(8,128)} %param.9) | copy-start | bytes 49156
  117.6 1.9 %copy-start = (f32[128,8192]{1,0:T(8,128)}, f32[128,8192]{1,0:T(8,128)S(1)}, u32[]{:S(2)}) copy-start(f32[128,8192]{1,0:T(8,128)S(1)} %get-tuple-element.10.mixed_ref) | copy-start | bytes 12582916
  119.5 2.0 %copy-start.2 = (f32[128,8192]{1,0:T(8,128)}, f32[128,8192]{1,0:T(8,128)S(1)}, u32[]{:S(2)}) copy-start(f32[128,8192]{1,0:T(8,128)S(1)} %get-tuple-element.11.grad_ref) | copy-start | bytes 12582916
  124.9 2.2 %copy-start.1 = (f32[128,8192]{1,0:T(8,128)S(1)}, f32[128,8192]{1,0:T(8,128)}, u32[]{:S(2)}) copy-start(f32[128,8192]{1,0:T(8,128)} %copy-done) | copy-start | bytes 12582916
  127.1 2.2 %copy-start.3 = (f32[128,8192]{1,0:T(8,128)S(1)}, f32[128,8192]{1,0:T(8,128)}, u32[]{:S(2)}) copy-start(f32[128,8192]{1,0:T(8,128)} %copy-done.2) | copy-start | bytes 12582916

commit v2 on v1

--- a/solution.py
+++ b/solution.py
@@ -13,8 +13,7 @@
 SPAN = 128
 SLICE = 256
 GROUPS = SLICE // GROUP
-WIDE = 512
-PER = WIDE // SLICE
+WIDE = 2048
 F32 = jnp.float32
 BF16 = jnp.bfloat16
 
@@ -32,7 +31,7 @@
     inverse = np.concatenate([np.cos(angle.T), -np.sin(angle.T)], 1) / SPAN
     fh, fl = split_np(forward)
     ih, il = split_np(inverse)
-    return np.concatenate([fh, fl, fh], 1), np.concatenate([ih, il, ih], 1)
+    return np.concatenate([fh, fl, fh, fl], 1), np.concatenate([ih, il, ih], 1)
 
 
 def split(values):
@@ -42,6 +41,11 @@
 
 def dot(a, b):
     return jnp.dot(a, b, preferred_element_type=F32)
+
+
+def paired(values):
+    high, low = split(values)
+    return jnp.concatenate([high, high, low, low], 0)
 
 
 def twice(values):
@@ -65,15 +69,15 @@
     def rows(part):
         return jnp.concatenate([jnp.where(owner == g, part, 0.0) for g in range(GROUPS)], 0).astype(BF16)
 
-    top = rows(high)
-    return jnp.concatenate([top, top, rows(low)], 0)
+    top, bottom = rows(high), rows(low)
+    return jnp.concatenate([top, top, bottom, bottom], 0)
 
 
 def powers(rate_row, reverse):
     t = lax.broadcasted_iota(jnp.int32, (SPAN, SPAN), 0)
     t = (SPAN - 1 - t if reverse else t).astype(F32)
     high, low = split(jnp.exp(-rate_row[0:1, :] * t))
-    return jnp.concatenate([high, low, high], 1)
+    return jnp.concatenate([high, low, high, low], 1)
 
 
 def first_kernel(x_ref, g_ref, rate_ref, res_ref, fwd_ref, inv_ref, send_ref):
@@ -84,9 +88,11 @@
     gf = dot(forward, gg)
     xr, xi, gr, gi = xf[:SPAN], xf[SPAN:], gf[:SPAN], gf[SPAN:]
     lags = dot(inv_ref[...], stacked(jnp.concatenate([gr * xr + gi * xi, gi * xr - gr * xi], 0)))
-    lag3 = stacked(lags)
+    lag_high, lag_low = split(lags)
+    lag_high, lag_low = twice(lag_high), twice(lag_low)
+    flip = jnp.where(lax.broadcasted_iota(jnp.int32, (SPAN, SPAN), 0) + lax.broadcasted_iota(jnp.int32, (SPAN, SPAN), 1) == SPAN - 1, 1.0, 0.0).astype(BF16)
+    backward = twice(dot(flip, x).astype(BF16))
     lag = lax.broadcasted_iota(jnp.int32, (SPAN, SPAN), 1).astype(F32)
-    back = (SPAN - 1) - lag
     half = SPAN // GROUP
     owner = lane_group(M, SPAN)
     row = lax.broadcasted_iota(jnp.int32, (SPAN, SPAN), 0) // GROUP
@@ -99,18 +105,20 @@
             chosen = jnp.where(owner == k, values[at + k * M : at + (k + 1) * M], chosen)
         return chosen
 
-    for s in range(PER):
+    for s in range(rate_ref.shape[0]):
         rates = jnp.transpose(jnp.broadcast_to(rate_ref[s, 0:1, :], (SPAN, SPAN)))
-        early, late = jnp.exp(-rates * lag), jnp.exp(-rates * back)
+        early = jnp.exp(-rates * lag)
         rate_sum = jnp.zeros((M, SPAN), F32)
         for h in range(2):
             rows = slice(h * half * M, (h + 1) * half * M)
             cols = slice(s * SLICE + h * SPAN, s * SLICE + (h + 1) * SPAN)
             eh, el = split(jnp.concatenate([early[rows], lag[rows] * early[rows]], 0))
-            lh, ll = split(jnp.concatenate([late[rows], back[rows] * late[rows]], 0))
-            ends = dot(jnp.concatenate([lh, ll], 1), xx[:, cols])
-            starts = dot(jnp.concatenate([eh, el], 1), gg[:, cols])
-            sums = dot(jnp.concatenate([eh, el, eh], 1), lag3[:, cols])
+            found = dot(
+                jnp.concatenate([eh, el], 1),
+                jnp.concatenate([backward[:, cols], gg[:, cols], lag_high[:, cols], lag_low[:, cols]], 1),
+            )
+            ends, starts = found[:, :SPAN], found[:, SPAN : 2 * SPAN]
+            sums = found[:, 2 * SPAN : 3 * SPAN] + found[:, 3 * SPAN :]
             for q, values in enumerate((pick(ends, 0), pick(starts, 0), pick(ends, 1), pick(starts, 1), pick(sums, 0))):
                 at = (2 * q + h) * M
                 send_ref[s, at : at + M, :] = values
@@ -123,10 +131,10 @@
 
 def second_kernel(x_ref, g_ref, rate_ref, res_ref, fwd_ref, inv_ref, mixed_ref, grad_ref):
     forward = fwd_ref[:, : 2 * SPAN]
-    for s in range(PER):
+    for s in range(rate_ref.shape[0]):
         cols = slice(s * SLICE, (s + 1) * SLICE)
         taps = dot(powers(rate_ref[s], False), spread(res_ref[:, cols]))
-        kf = dot(fwd_ref[...], stacked(taps))
+        kf = dot(fwd_ref[...], paired(taps))
         xf = dot(forward, twice(x_ref[0, :, cols]))
         gf = dot(forward, twice(g_ref[0, :, cols]))
         kr, ki, xr, xi, gr, gi = kf[:SPAN], kf[SPAN:], xf[:SPAN], xf[SPAN:], gf[:SPAN], gf[SPAN:]
@@ -134,10 +142,12 @@
         grad_ref[:, cols] = dot(inv_ref[...], stacked(jnp.concatenate([kr * gr + ki * gi, kr * gi - ki * gr], 0)))
 
 
-def middle_kernel(chunks, got_ref, rate_ref, res_ref, back_ref, sums_ref):
+def middle_kernel(chunks, index_ref, got_ref, rate_ref, res_ref, back_ref, sums_ref):
+    offset = lax.rem(index_ref[0], SPAN // GROUPS) * GROUPS
     rate_sum = jnp.zeros((M, SPAN), F32)
     for k in range(chunks):
         rate_sum = rate_sum + got_ref[k, 10 * M : 11 * M, :]
+    rate_sum = pltpu.roll(rate_sum, offset, 1)
     row = lax.broadcasted_iota(jnp.int32, (SPAN, SPAN), 0) // GROUP
     col = lax.broadcasted_iota(jnp.int32, (SPAN, SPAN), 1)
     for h in range(2):
@@ -167,14 +177,14 @@
             adjoint = across * adjoint + part(k, 1)
         sums_ref[h * M : (h + 1) * M, :] = res_part + pole * res_carry
         weighted = handed * rate_carry
-        place = jnp.where(row + h * (SPAN // GROUP) == col, 1.0, 0.0).astype(BF16)
+        place = jnp.where(row + (h * (SPAN // GROUP) + offset) == col, 1.0, 0.0).astype(BF16)
         wh, wl = split(weighted)
         rate_sum = rate_sum + dot(wh, place) + dot(wl, place)
     sums_ref[2 * M : 3 * M, :] = rate_sum
 
 
 def last_kernel(mixed_ref, grad_ref, rate_ref, got_ref, mixed_out, grad_out):
-    for s in range(PER):
+    for s in range(rate_ref.shape[0]):
         cols = slice(s * SLICE, (s + 1) * SLICE)
         state = jnp.concatenate([got_ref[s, 0:M, :], got_ref[s, M : 2 * M, :]], 1)
         adjoint = jnp.concatenate([got_ref[s, 2 * M : 3 * M, :], got_ref[s, 3 * M : 4 * M, :]], 1)
@@ -184,30 +194,45 @@
         grad_out[0, :, cols] = (grad_ref[:, cols] + more).astype(BF16)
 
 
+def gather_kernel(chunks, all_ref, log_ref, res_out, rate_out):
+    for k in range(chunks):
+        for h in range(2):
+            res_out[:, k * SLICE + h * SPAN : k * SLICE + (h + 1) * SPAN] = all_ref[k, h * M : (h + 1) * M, :]
+    width = min(SPAN, chunks * GROUPS)
+    per = width // GROUPS
+    for j in range(chunks // per):
+        parts = all_ref[j * per, 2 * M : 3 * M, :]
+        for k in range(j * per + 1, (j + 1) * per):
+            parts = parts + all_ref[k, 2 * M : 3 * M, :]
+        cols = slice(j * width, (j + 1) * width)
+        rate_out[:, cols] = -jnp.exp(log_ref[:, cols]) * parts[:, :width]
+
+
 def local(signal, out_grad, residues, log_rates):
     channels = signal.shape[2]
     chunks, rows = lax.axis_size("seq"), lax.axis_size("batch")
     index = lax.axis_index("seq")
-    steps = channels // WIDE
+    wide = min(WIDE, channels)
+    steps = channels // wide
     fwd, inv = (jnp.asarray(v) for v in transforms())
     decay_rate = jnp.exp(log_rates)
     rate_rows = jnp.broadcast_to(decay_rate.T.reshape(chunks, 1, SPAN), (chunks, M, SPAN))
     own_rate = jnp.repeat(lax.dynamic_slice_in_dim(decay_rate, index * GROUPS, GROUPS, 1), GROUP, axis=1)
     own_res = lax.dynamic_slice_in_dim(residues, index * SLICE, SLICE, 1)
 
-    seq_block = pl.BlockSpec((1, SPAN, WIDE), lambda i: (0, 0, i))
-    flat_block = pl.BlockSpec((SPAN, WIDE), lambda i: (0, i))
-    rate_block = pl.BlockSpec((PER, M, SPAN), lambda i: (i, 0, 0))
-    res_block = pl.BlockSpec((M, WIDE), lambda i: (0, i))
+    seq_block = pl.BlockSpec((1, SPAN, wide), lambda i: (0, 0, i))
+    flat_block = pl.BlockSpec((SPAN, wide), lambda i: (0, i))
+    rate_block = pl.BlockSpec((wide // SLICE, M, SPAN), lambda i: (i, 0, 0))
+    res_block = pl.BlockSpec((M, wide), lambda i: (0, i))
     whole = lambda a: pl.BlockSpec(a.shape, lambda i: (0,) * a.ndim)
-    params = pltpu.CompilerParams(vmem_limit_bytes=32 * 2**20)
+    params = pltpu.CompilerParams(vmem_limit_bytes=58 * 2**20)
     both = 2 * SPAN * channels
 
     send = pl.pallas_call(
         first_kernel,
         grid=(steps,),
         in_specs=[seq_block, seq_block, rate_block, res_block, whole(fwd), whole(inv)],
-        out_specs=pl.BlockSpec((PER, 11 * M, SPAN), lambda i: (i, 0, 0)),
+        out_specs=pl.BlockSpec((wide // SLICE, 11 * M, SPAN), lambda i: (i, 0, 0)),
         out_shape=jax.ShapeDtypeStruct((chunks, 11 * M, SPAN), F32),
         compiler_params=params,
         name="ends_and_lags",
@@ -225,19 +250,23 @@
         name="local_convolutions",
     )(signal, out_grad, rate_rows, residues, fwd, inv)
 
+    got, mixed_part, grad_part = lax.optimization_barrier((got, mixed_part, grad_part))
+    vmem = pl.BlockSpec(memory_space=pltpu.VMEM)
     back, sums = pl.pallas_call(
         functools.partial(middle_kernel, chunks),
         out_shape=[
             jax.ShapeDtypeStruct((chunks, 4 * M, SPAN), F32),
             jax.ShapeDtypeStruct((3 * M, SPAN), F32),
         ],
+        in_specs=[pl.BlockSpec(memory_space=pltpu.SMEM), vmem, vmem, vmem],
         name="carries",
-    )(got, own_rate, own_res)
+    )(index.astype(jnp.int32)[None], got, own_rate, own_res)
     carried = lax.all_to_all(back, "seq", 0, 0, tiled=True)
     total = sums
     for k in range(1, rows):
         total = total + lax.ppermute(sums, "batch", [(i, (i + k) % rows) for i in range(rows)])
     total = total * (1.0 / (rows * chunks * SPAN))
+    carried, total = lax.optimization_barrier((carried, total))
     everyone = lax.all_to_all(jnp.broadcast_to(total[None], (chunks, 3 * M, SPAN)), "seq", 0, 0, tiled=True)
 
     mixed, grad_signal = pl.pallas_call(
@@ -247,7 +276,7 @@
             flat_block,
             flat_block,
             rate_block,
-            pl.BlockSpec((PER, 4 * M, SPAN), lambda i: (i, 0, 0)),
+            pl.BlockSpec((wide // SLICE, 4 * M, SPAN), lambda i: (i, 0, 0)),
         ],
         out_specs=[seq_block, seq_block],
         out_shape=[jax.ShapeDtypeStruct(signal.shape, BF16)] * 2,
@@ -255,8 +284,11 @@
         cost_estimate=pl.CostEstimate(flops=both * 800, bytes_accessed=both * 6, transcendentals=both),
         name="add_carries",
     )(mixed_part, grad_part, rate_rows, carried)
-    grad_residues = everyone[:, : 2 * M].reshape(chunks, 2, M, SPAN).transpose(2, 0, 1, 3).reshape(M, channels)
-    grad_rates = -decay_rate * everyone[:, 2 * M :, :GROUPS].transpose(1, 0, 2).reshape(M, chunks * GROUPS)
+    grad_residues, grad_rates = pl.pallas_call(
+        functools.partial(gather_kernel, chunks),
+        out_shape=[jax.ShapeDtypeStruct(residues.shape, F32), jax.ShapeDtypeStruct(log_rates.shape, F32)],
+        name="unpack",
+    )(everyone, log_rates)
     return mixed, grad_signal, grad_residues, grad_rates
 
 

time: 139 us -> 96.3 us (0.69)
  blocking collectives: 16 us -> 0 us
  local copies, waits for them, and re-layouts: 21.1 us -> 6.5 us
  waiting for transfers between devices: 23.1 us -> 10.5 us
  starting transfers between devices: 17.1 us -> 25.9 us
  Pallas kernels: 58.6 us -> 51.4 us
    all_to_all x1, waiting for transfers between devices: 19.8 us -> 0.01 us  [local(): got = lax.all_to_all(send, 'seq', 0, 0, tiled=True)]
    all_to_all x1 -> x0, blocking collectives: 16 us -> none  [local(): lax.all_to_all(jnp.broadcast_to(total[None], (chunks, 3 * M, SPAN)), 'seq...]
    unnamed x30 -> x6, local copies, waits for them, and re-layouts: 15.9 us -> 1.86 us
    pallas_call x1, Pallas kernels: 24.2 us -> 17.2 us  [local(): pl.pallas_call(first_kernel, grid=(steps,), in_specs=[seq_block, seq_bloc...]
    all_to_all x0 -> x1, starting transfers between devices: none -> 5.24 us  [local(): lax.all_to_all(jnp.broadcast_to(total[None], (chunks, 3 * M, SPAN)), 'seq...]
    all_to_all x1, starting transfers between devices: 3.68 us -> 7.39 us  [local(): carried = lax.all_to_all(back, 'seq', 0, 0, tiled=True)]
    all_to_all x1, waiting for transfers between devices: 0.01 us -> 3.59 us  [local(): carried = lax.all_to_all(back, 'seq', 0, 0, tiled=True)]
    all_to_all x0 -> x1, waiting for transfers between devices: none -> 3.2 us  [local(): lax.all_to_all(jnp.broadcast_to(total[None], (chunks, 3 * M, SPAN)), 'seq...]
  transfers between devices with their start and end apart: 5 -> 6, of which waited for: 3 -> 4; matrix products, arithmetic and copies ran while one was open for 3% -> 3% of each run, Pallas kernels for 17% -> 31%
where the time goes in v2:
time: 96.3 us; the launch traced here: 95.7 us
  Pallas kernels  51.4 us (53%)
  starting transfers between devices  25.9 us (27%)
  waiting for transfers between devices  10.5 us (11%)
  local copies, waits for them, and re-layouts  6.5 us (7%)
    pallas_call x1, Pallas kernels, local(): pl.pallas_call(second_kernel, grid=(steps,), in_specs=[seq_block, seq_blo...  23 us
    pallas_call x1, Pallas kernels, local(): pl.pallas_call(first_kernel, grid=(steps,), in_specs=[seq_block, seq_bloc...  17.2 us
    all_to_all x1, starting transfers between devices, local(): got = lax.all_to_all(send, 'seq', 0, 0, tiled=True)  9.63 us
    all_to_all x1, starting transfers between devices, local(): carried = lax.all_to_all(back, 'seq', 0, 0, tiled=True)  7.39 us
    pallas_call x1, Pallas kernels, local(): pl.pallas_call(last_kernel, grid=(steps,), in_specs=[flat_block, flat_blo...  7.1 us
    all_to_all x1, starting transfers between devices, local(): lax.all_to_all(jnp.broadcast_to(total[None], (chunks, 3 * M, SPAN)), 'seq...  5.24 us
    ppermute x3, waiting for transfers between devices, local(): lax.ppermute(sums, 'batch', [(i, (i + k) % rows) for i in range(rows)])  3.67 us
    ppermute x3, starting transfers between devices, local(): lax.ppermute(sums, 'batch', [(i, (i + k) % rows) for i in range(rows)])  3.64 us
  transfers between devices with their start and end apart: 6, of which 4 were waited for; matrix products, arithmetic and copies ran while one was open for 3% of the time, Pallas kernels for 31%

profile of v2, /device:TPU:1, one launch (start us, length us, event | category | flops | bytes accessed | tf_op | source)
XLA Modules:
  0.0 95.7 jit_solution(11004641469547258342)
XLA Ops:
  0.6 0.7 fusion
  1.4 0.1 copy.10
  1.5 0.2 broadcast_in_dim.19
  1.6 0.7 broadcast_in_dim.20.rate_ref
  2.3 17.2 %ends_and_lags.1 = f32[32,88,128]{2,1,0:T(8,128)} custom-call(bf16[1,128,8192]{2,1,0:T(8,128)(2,1)} %x_ref.3, bf16[1,128,8192]{2,1,0:T(8,128)(2,1)} %g_ref.3, f32[32,8,128]{2,1,0:T(8,128)} %broadcast_in_dim.20.rate_ref, f32[8,8192]{1,0:T(8,128)} %res_ref.3, bf16[256,512]{1,0:T(8,128)(2,1)} %constant.22.clone.fwd_ref, bf16[128,768]{1,0:T(8,128)(2,1)} %constant.23.clone.inv_ref), custom_call_target="tpu_custom_call" | custom-call | tf_op jit(solution)/shard_map/ends_and_lags/pallas_call | solution.py:231
  19.5 9.6 %all-to-all-start = ((f32[32,88,128]{2,1,0:T(8,128)}), f32[32,88,128]{2,1,0:T(8,128)S(1)}, u32[]{:S(2)}, u32[]{:S(2)}) async-start(f32[32,88,128]{2,1,0:T(8,128)} %ends_and_lags.1), calls=%async_computation | async-start | bytes 2883584 | tf_op jit(solution)/shard_map/all_to_all | solution.py:240
  29.1 0.1 constant_dynamic-slice_fusion.1
  29.2 0.1 broadcast_in_dim.22
  29.3 0.7 reshape.14.rate_ref
  29.9 1.3 %constant_dynamic-slice_fusion.res_ref = f32[8,256]{1,0:T(8,128)} fusion(f32[8,8192]{1,0:T(8,128)} %res_ref.3, s32[]{:T(128)S(6)} %select_n.7), kind=kLoop, calls=%fused_computation.1 | loop fusion | bytes 16388 | tf_op jit(solution)/shard_map/dynamic_slice | solution.py:221
  31.2 23.0 %local_convolutions.1 = (f32[128,8192]{1,0:T(8,128)}, f32[128,8192]{1,0:T(8,128)}) custom-call(bf16[1,128,8192]{2,1,0:T(8,128)(2,1)} %x_ref.3, bf16[1,128,8192]{2,1,0:T(8,128)(2,1)} %g_ref.3, f32[32,8,128]{2,1,0:T(8,128)} %broadcast_in_dim.20.rate_ref, f32[8,8192]{1,0:T(8,128)} %res_ref.3, bf16[256,512]{1,0:T(8,128)(2,1)} %constant.22.clone.fwd_ref, ...), custom_call_target="tpu_custom_call" | custom-call | flops 6291456000 | bytes 16777216 | tf_op jit(solution)/shard_map/local_convolutions/pallas_call | solution.py:242
  54.3 0.0 all-to-all-done.got_ref
  54.3 0.0 copy-start
  54.3 1.1 %copy-done = f32[32,88,128]{2,1,0:T(8,128)} copy-done((f32[32,88,128]{2,1,0:T(8,128)}, f32[32,88,128]{2,1,0:T(8,128)S(1)}, u32[]{:S(2)}) %copy-start) | copy-done | bytes 1441816
  55.4 2.4 %carries.1 = (f32[32,32,128]{2,1,0:T(8,128)}, f32[24,128]{1,0:T(8,128)}) custom-call(s32[1]{0:T(128)} %bitcast.1.index_ref, f32[32,88,128]{2,1,0:T(8,128)} %copy-done, f32[8,256]{1,0:T(8,128)} %reshape.14.rate_ref, f32[8,256]{1,0:T(8,128)} %constant_dynamic-slice_fusion.res_ref), custom_call_target="tpu_custom_call" | custom-call | tf_op jit(solution)/shard_map/carries/pallas_call | solution.py:255
  57.8 7.4 %all-to-all-start.1 = ((f32[32,32,128]{2,1,0:T(8,128)}), f32[32,32,128]{2,1,0:T(8,128)S(1)}, u32[]{:S(2)}, u32[]{:S(2)}) async-start(f32[32,32,128]{2,1,0:T(8,128)} %get-tuple-element.22), calls=%async_computation.1 | async-start | bytes 1048576 | tf_op jit(solution)/shard_map/all_to_all | solution.py:264
  65.2 2.5 %collective-permute-start.2 = (f32[24,128]{1,0:T(8,128)}, f32[24,128]{1,0:T(8,128)S(1)}, u32[]{:S(2)}, u32[]{:S(2)}) collective-permute-start(f32[24,128]{1,0:T(8,128)} %get-tuple-element.23), channel_id=1, source_target_pairs={{0,3},{1,0},{2,1},{3,2},{4,7},{5,4},{6,5},{7,6},{8,11},{9,8},{10,9... | collective-permute-start | bytes 36872 | tf_op jit(solution)/shard_map/ppermute | solution.py:267
  67.7 0.5 collective-permute-start.1
  68.2 0.6 collective-permute-start
  68.8 0.0 collective-permute-done.2
  68.8 3.5 %collective-permute-done.1 = f32[24,128]{1,0:T(8,128)S(1)} collective-permute-done((f32[24,128]{1,0:T(8,128)}, f32[24,128]{1,0:T(8,128)S(1)}, u32[]{:S(2)}, u32[]{:S(2)}) %collective-permute-start.1) | collective-permute-done | bytes 12320 | tf_op jit(solution)/shard_map/ppermute | solution.py:267
  72.3 0.2 collective-permute-done
  72.5 0.7 add_multiply_fusion
  73.2 3.6 %all-to-all-done.1.got_ref = f32[32,32,128]{2,1,0:T(8,128)S(1)} async-done(((f32[32,32,128]{2,1,0:T(8,128)}), f32[32,32,128]{2,1,0:T(8,128)S(1)}, u32[]{:S(2)}, u32[]{:S(2)}) %all-to-all-start.1) | async-done | bytes 524320 | tf_op jit(solution)/shard_map/all_to_all | solution.py:264
  76.8 0.0 copy-start.1
  76.8 0.8 broadcast_in_dim.23
  77.6 5.2 %all-to-all-start.2 = ((f32[32,24,128]{2,1,0:T(8,128)}), f32[32,24,128]{2,1,0:T(8,128)S(1)}, u32[]{:S(2)}, u32[]{:S(2)}) async-start(f32[32,24,128]{2,1,0:T(8,128)} %broadcast_in_dim.23), calls=%async_computation.2 | async-start | bytes 786432 | tf_op jit(solution)/shard_map/all_to_all | solution.py:270
  82.9 0.0 copy-done.1
  82.9 7.1 %add_carries.1 = (bf16[1,128,8192]{2,1,0:T(8,128)(2,1)}, bf16[1,128,8192]{2,1,0:T(8,128)(2,1)}) custom-call(f32[128,8192]{1,0:T(8,128)} %get-tuple-element.19.mixed_ref, f32[128,8192]{1,0:T(8,128)} %get-tuple-element.20.grad_ref, f32[32,8,128]{2,1,0:T(8,128)} %broadcast_in_dim.20.rate_ref, f32[32,32,128]{2,1,0:T(8,128)} %copy-done.1), custom_call_target="tpu_custom_call" | custom-call | flops 1677721600 | bytes 12582912 | tf_op jit(solution)/shard_map/add_carries/pallas_call | solution.py:272
  90.0 3.2 %all-to-all-done.2.all_ref = f32[32,24,128]{2,1,0:T(8,128)S(1)} async-done(((f32[32,24,128]{2,1,0:T(8,128)}), f32[32,24,128]{2,1,0:T(8,128)S(1)}, u32[]{:S(2)}, u32[]{:S(2)}) %all-to-all-start.2) | async-done | bytes 393248 | tf_op jit(solution)/shard_map/all_to_all | solution.py:270
  93.2 0.0 copy-start.2
  93.2 0.8 copy-done.2
  93.9 1.7 %unpack.1 = (f32[8,8192]{1,0:T(8,128)}, f32[8,512]{1,0:T(8,128)}) custom-call(f32[32,24,128]{2,1,0:T(8,128)} %copy-done.2, f32[8,512]{1,0:T(8,128)} %log_ref.1), custom_call_target="tpu_custom_call" | custom-call | tf_op jit(solution)/shard_map/unpack/pallas_call | solution.py:287
Async XLA Ops:
  19.5 34.8 %all-to-all-start = ((f32[32,88,128]{2,1,0:T(8,128)}), f32[32,88,128]{2,1,0:T(8,128)S(1)}, u32[]{:S(2)}, u32[]{:S(2)}) async-start(f32[32,88,128]{2,1,0:T(8,128)} %ends_and_lags.1), calls=%async_computation | async-start | bytes 2883584 | tf_op jit(solution)/shard_map/all_to_all | solution.py:240
  54.3 1.1 %copy-start = (f32[32,88,128]{2,1,0:T(8,128)}, f32[32,88,128]{2,1,0:T(8,128)S(1)}, u32[]{:S(2)}) copy-start(f32[32,88,128]{2,1,0:T(8,128)S(1)} %all-to-all-done.got_ref) | copy-start | bytes 4325380
  57.8 19.0 %all-to-all-start.1 = ((f32[32,32,128]{2,1,0:T(8,128)}), f32[32,32,128]{2,1,0:T(8,128)S(1)}, u32[]{:S(2)}, u32[]{:S(2)}) async-start(f32[32,32,128]{2,1,0:T(8,128)} %get-tuple-element.22), calls=%async_computation.1 | async-start | bytes 1048576 | tf_op jit(solution)/shard_map/all_to_all | solution.py:264
  65.2 3.6 %collective-permute-start.2 = (f32[24,128]{1,0:T(8,128)}, f32[24,128]{1,0:T(8,128)S(1)}, u32[]{:S(2)}, u32[]{:S(2)}) collective-permute-start(f32[24,128]{1,0:T(8,128)} %get-tuple-element.23), channel_id=1, source_target_pairs={{0,3},{1,0},{2,1},{3,2},{4,7},{5,4},{6,5},{7,6},{8,11},{9,8},{10,9... | collective-permute-start | bytes 36872 | tf_op jit(solution)/shard_map/ppermute | solution.py:267
  67.7 4.6 %collective-permute-start.1 = (f32[24,128]{1,0:T(8,128)}, f32[24,128]{1,0:T(8,128)S(1)}, u32[]{:S(2)}, u32[]{:S(2)}) collective-permute-start(f32[24,128]{1,0:T(8,128)} %get-tuple-element.23), channel_id=1, source_target_pairs={{0,2},{1,3},{2,0},{3,1},{4,6},{5,7},{6,4},{7,5},{8,10},{9,11},{10,... | collective-permute-start | bytes 36872 | tf_op jit(solution)/shard_map/ppermute | solution.py:267
  68.2 4.3 %collective-permute-start = (f32[24,128]{1,0:T(8,128)}, f32[24,128]{1,0:T(8,128)S(1)}, u32[]{:S(2)}, u32[]{:S(2)}) collective-permute-start(f32[24,128]{1,0:T(8,128)} %get-tuple-element.23), channel_id=1, source_target_pairs={{0,1},{1,2},{2,3},{3,0},{4,5},{5,6},{6,7},{7,4},{8,9},{9,10},{10,1... | collective-permute-start | bytes 36872 | tf_op jit(solution)/shard_map/ppermute | solution.py:267
  76.8 6.1 %copy-start.1 = (f32[32,32,128]{2,1,0:T(8,128)}, f32[32,32,128]{2,1,0:T(8,128)S(1)}, u32[]{:S(2)}) copy-start(f32[32,32,128]{2,1,0:T(8,128)S(1)} %all-to-all-done.1.got_ref) | copy-start | bytes 1572868
  77.6 15.6 %all-to-all-start.2 = ((f32[32,24,128]{2,1,0:T(8,128)}), f32[32,24,128]{2,1,0:T(8,128)S(1)}, u32[]{:S(2)}, u32[]{:S(2)}) async-start(f32[32,24,128]{2,1,0:T(8,128)} %broadcast_in_dim.23), calls=%async_computation.2 | async-start | bytes 786432 | tf_op jit(solution)/shard_map/all_to_all | solution.py:270
  93.2 0.8 copy-start.2

commit v3 on v2

--- a/solution.py
+++ b/solution.py
@@ -31,7 +31,7 @@
     inverse = np.concatenate([np.cos(angle.T), -np.sin(angle.T)], 1) / SPAN
     fh, fl = split_np(forward)
     ih, il = split_np(inverse)
-    return np.concatenate([fh, fl, fh, fl], 1), np.concatenate([ih, il, ih], 1)
+    return np.concatenate([fh, fl], 1), np.concatenate([ih, il, ih], 1)
 
 
 def split(values):
@@ -41,11 +41,6 @@
 
 def dot(a, b):
     return jnp.dot(a, b, preferred_element_type=F32)
-
-
-def paired(values):
-    high, low = split(values)
-    return jnp.concatenate([high, high, low, low], 0)
 
 
 def twice(values):
@@ -80,10 +75,10 @@
     return jnp.concatenate([high, low, high, low], 1)
 
 
-def first_kernel(x_ref, g_ref, rate_ref, res_ref, fwd_ref, inv_ref, send_ref):
+def first_kernel(x_ref, g_ref, log_ref, res_ref, fwd_ref, inv_ref, send_ref):
     x, g = x_ref[0], g_ref[0]
     xx, gg = twice(x), twice(g)
-    forward = fwd_ref[:, : 2 * SPAN]
+    forward = fwd_ref[...]
     xf = dot(forward, xx)
     gf = dot(forward, gg)
     xr, xi, gr, gi = xf[:SPAN], xf[SPAN:], gf[:SPAN], gf[SPAN:]
@@ -105,10 +100,13 @@
             chosen = jnp.where(owner == k, values[at + k * M : at + (k + 1) * M], chosen)
         return chosen
 
-    for s in range(rate_ref.shape[0]):
-        rates = jnp.transpose(jnp.broadcast_to(rate_ref[s, 0:1, :], (SPAN, SPAN)))
+    count = log_ref.shape[1] // GROUPS
+    rate = jnp.exp(log_ref[...])
+    weighted = ([], [])
+    for s in range(count):
+        at = s * GROUPS
+        rates = jnp.concatenate([jnp.broadcast_to(rate[:, k : k + 1], (M, SPAN)) for k in range(at, at + GROUPS)], 0)
         early = jnp.exp(-rates * lag)
-        rate_sum = jnp.zeros((M, SPAN), F32)
         for h in range(2):
             rows = slice(h * half * M, (h + 1) * half * M)
             cols = slice(s * SLICE + h * SPAN, s * SLICE + (h + 1) * SPAN)
@@ -122,27 +120,48 @@
             for q, values in enumerate((pick(ends, 0), pick(starts, 0), pick(ends, 1), pick(starts, 1), pick(sums, 0))):
                 at = (2 * q + h) * M
                 send_ref[s, at : at + M, :] = values
-            weighted = res_ref[:, cols] * pick(sums, 1)
-            place = jnp.where(row + h * half == col, 1.0, 0.0).astype(BF16)
-            wh, wl = split(weighted)
-            rate_sum = rate_sum + dot(wh, place) + dot(wl, place)
-        send_ref[s, 10 * M : 11 * M, :] = rate_sum
+            weighted[h].append(res_ref[:, cols] * pick(sums, 1))
+    total = jnp.zeros((count * M, SPAN), F32)
+    for h in range(2):
+        place = jnp.where(row + h * half == col, 1.0, 0.0).astype(BF16)
+        wh, wl = split(jnp.concatenate(weighted[h], 0))
+        total = total + dot(jnp.concatenate([wh, wl], 1), twice(place))
+    for s in range(count):
+        send_ref[s, 10 * M : 11 * M, :] = total[s * M : (s + 1) * M]
 
 
 def second_kernel(x_ref, g_ref, rate_ref, res_ref, fwd_ref, inv_ref, mixed_ref, grad_ref):
-    forward = fwd_ref[:, : 2 * SPAN]
-    for s in range(rate_ref.shape[0]):
-        cols = slice(s * SLICE, (s + 1) * SLICE)
-        taps = dot(powers(rate_ref[s], False), spread(res_ref[:, cols]))
-        kf = dot(fwd_ref[...], paired(taps))
-        xf = dot(forward, twice(x_ref[0, :, cols]))
-        gf = dot(forward, twice(g_ref[0, :, cols]))
-        kr, ki, xr, xi, gr, gi = kf[:SPAN], kf[SPAN:], xf[:SPAN], xf[SPAN:], gf[:SPAN], gf[SPAN:]
-        mixed_ref[:, cols] = dot(inv_ref[...], stacked(jnp.concatenate([kr * xr - ki * xi, kr * xi + ki * xr], 0)))
-        grad_ref[:, cols] = dot(inv_ref[...], stacked(jnp.concatenate([kr * gr + ki * gi, kr * gi - ki * gr], 0)))
-
-
-def middle_kernel(chunks, index_ref, got_ref, rate_ref, res_ref, back_ref, sums_ref):
+    forward = fwd_ref[...]
+    taps = [
+        dot(powers(rate_ref[s], False), spread(res_ref[:, s * SLICE : (s + 1) * SLICE]))
+        for s in range(rate_ref.shape[0])
+    ]
+    high, low = split(jnp.concatenate(taps, 1))
+    kf = dot(forward, twice(high)) + dot(fwd_ref[:, :SPAN], low)
+    xf = dot(forward, twice(x_ref[0]))
+    gf = dot(forward, twice(g_ref[0]))
+    kr, ki, xr, xi, gr, gi = kf[:SPAN], kf[SPAN:], xf[:SPAN], xf[SPAN:], gf[:SPAN], gf[SPAN:]
+    mixed_ref[...] = dot(inv_ref[...], stacked(jnp.concatenate([kr * xr - ki * xi, kr * xi + ki * xr], 0)))
+    grad_ref[...] = dot(inv_ref[...], stacked(jnp.concatenate([kr * gr + ki * gi, kr * gi - ki * gr], 0)))
+
+
+def carry_kernel(chunks, got_ref, rate_ref, res_ref, back_ref):
+    for h in range(2):
+        cols = slice(h * SPAN, (h + 1) * SPAN)
+        rate = rate_ref[:, cols]
+        across = jnp.exp(-rate * SPAN)
+        handed = res_ref[:, cols] * jnp.exp(-rate)
+        state = jnp.zeros((M, SPAN), F32)
+        adjoint = state
+        for k in range(chunks):
+            last = chunks - 1 - k
+            back_ref[k, h * M : (h + 1) * M, :] = handed * state
+            back_ref[last, (2 + h) * M : (3 + h) * M, :] = handed * adjoint
+            state = across * state + got_ref[k, h * M : (h + 1) * M, :]
+            adjoint = across * adjoint + got_ref[last, (2 + h) * M : (3 + h) * M, :]
+
+
+def sums_kernel(chunks, scale, index_ref, got_ref, rate_ref, res_ref, sums_ref):
     offset = lax.rem(index_ref[0], SPAN // GROUPS) * GROUPS
     rate_sum = jnp.zeros((M, SPAN), F32)
     for k in range(chunks):
@@ -155,7 +174,6 @@
         rate, res = rate_ref[:, cols], res_ref[:, cols]
         pole = jnp.exp(-rate)
         across = jnp.exp(-rate * SPAN)
-        handed = res * pole
 
         def part(k, q):
             at = (2 * q + h) * M
@@ -164,23 +182,17 @@
         zero = jnp.zeros((M, SPAN), F32)
         state, moment, res_part, res_carry, rate_carry = zero, zero, zero, zero, zero
         for k in range(chunks):
-            back_ref[k, h * M : (h + 1) * M, :] = handed * state
             start = part(k, 1)
             res_part = res_part + part(k, 4)
             res_carry = res_carry + state * start
             rate_carry = rate_carry + state * (part(k, 3) + start) + moment * start
             moment = across * (moment + SPAN * state) + part(k, 2)
             state = across * state + part(k, 0)
-        adjoint = zero
-        for k in reversed(range(chunks)):
-            back_ref[k, (2 + h) * M : (3 + h) * M, :] = handed * adjoint
-            adjoint = across * adjoint + part(k, 1)
-        sums_ref[h * M : (h + 1) * M, :] = res_part + pole * res_carry
-        weighted = handed * rate_carry
+        sums_ref[h * M : (h + 1) * M, :] = scale * (res_part + pole * res_carry)
         place = jnp.where(row + (h * (SPAN // GROUP) + offset) == col, 1.0, 0.0).astype(BF16)
-        wh, wl = split(weighted)
+        wh, wl = split(res * pole * rate_carry)
         rate_sum = rate_sum + dot(wh, place) + dot(wl, place)
-    sums_ref[2 * M : 3 * M, :] = rate_sum
+    sums_ref[2 * M : 3 * M, :] = scale * rate_sum
 
 
 def last_kernel(mixed_ref, grad_ref, rate_ref, got_ref, mixed_out, grad_out):
@@ -215,11 +227,7 @@
     wide = min(WIDE, channels)
     steps = channels // wide
     fwd, inv = (jnp.asarray(v) for v in transforms())
-    decay_rate = jnp.exp(log_rates)
-    rate_rows = jnp.broadcast_to(decay_rate.T.reshape(chunks, 1, SPAN), (chunks, M, SPAN))
-    own_rate = jnp.repeat(lax.dynamic_slice_in_dim(decay_rate, index * GROUPS, GROUPS, 1), GROUP, axis=1)
-    own_res = lax.dynamic_slice_in_dim(residues, index * SLICE, SLICE, 1)
-
+    log_block = pl.BlockSpec((M, wide // GROUP), lambda i: (0, i))
     seq_block = pl.BlockSpec((1, SPAN, wide), lambda i: (0, 0, i))
     flat_block = pl.BlockSpec((SPAN, wide), lambda i: (0, i))
     rate_block = pl.BlockSpec((wide // SLICE, M, SPAN), lambda i: (i, 0, 0))
@@ -231,12 +239,18 @@
     send = pl.pallas_call(
         first_kernel,
         grid=(steps,),
-        in_specs=[seq_block, seq_block, rate_block, res_block, whole(fwd), whole(inv)],
+        in_specs=[seq_block, seq_block, log_block, res_block, whole(fwd), whole(inv)],
         out_specs=pl.BlockSpec((wide // SLICE, 11 * M, SPAN), lambda i: (i, 0, 0)),
         out_shape=jax.ShapeDtypeStruct((chunks, 11 * M, SPAN), F32),
         compiler_params=params,
         name="ends_and_lags",
-    )(signal, out_grad, rate_rows, residues, fwd, inv)
+    )(signal, out_grad, log_rates, residues, fwd, inv)
+    send, later_rates, later_res = lax.optimization_barrier((send, log_rates, residues))
+    decay_rate = jnp.exp(later_rates)
+    rate_rows = jnp.broadcast_to(decay_rate.T.reshape(chunks, 1, SPAN), (chunks, M, SPAN))
+    own_rate = jnp.repeat(lax.dynamic_slice_in_dim(decay_rate, index * GROUPS, GROUPS, 1), GROUP, axis=1)
+    own_res = lax.dynamic_slice_in_dim(later_res, index * SLICE, SLICE, 1)
+
     got = lax.all_to_all(send, "seq", 0, 0, tiled=True)
 
     mixed_part, grad_part = pl.pallas_call(
@@ -252,22 +266,27 @@
 
     got, mixed_part, grad_part = lax.optimization_barrier((got, mixed_part, grad_part))
     vmem = pl.BlockSpec(memory_space=pltpu.VMEM)
-    back, sums = pl.pallas_call(
-        functools.partial(middle_kernel, chunks),
-        out_shape=[
-            jax.ShapeDtypeStruct((chunks, 4 * M, SPAN), F32),
-            jax.ShapeDtypeStruct((3 * M, SPAN), F32),
-        ],
+    back = pl.pallas_call(
+        functools.partial(carry_kernel, chunks),
+        out_shape=jax.ShapeDtypeStruct((chunks, 4 * M, SPAN), F32),
+        compiler_params=pltpu.CompilerParams(vmem_limit_bytes=8 * 2**20),
+        name="carries",
+    )(got, own_rate, own_res)
+    back, got = lax.optimization_barrier((back, got))
+    carried = lax.all_to_all(back, "seq", 0, 0, tiled=True)
+    sums = pl.pallas_call(
+        functools.partial(sums_kernel, chunks, 1.0 / (rows * chunks * SPAN)),
+        out_shape=jax.ShapeDtypeStruct((3 * M, SPAN), F32),
         in_specs=[pl.BlockSpec(memory_space=pltpu.SMEM), vmem, vmem, vmem],
-        name="carries",
+        compiler_params=pltpu.CompilerParams(vmem_limit_bytes=8 * 2**20),
+        name="gradient_sums",
     )(index.astype(jnp.int32)[None], got, own_rate, own_res)
-    carried = lax.all_to_all(back, "seq", 0, 0, tiled=True)
     total = sums
     for k in range(1, rows):
         total = total + lax.ppermute(sums, "batch", [(i, (i + k) % rows) for i in range(rows)])
-    total = total * (1.0 / (rows * chunks * SPAN))
+    total = jnp.broadcast_to(total[None], (chunks, 3 * M, SPAN))
     carried, total = lax.optimization_barrier((carried, total))
-    everyone = lax.all_to_all(jnp.broadcast_to(total[None], (chunks, 3 * M, SPAN)), "seq", 0, 0, tiled=True)
+    everyone = lax.all_to_all(total, "seq", 0, 0, tiled=True)
 
     mixed, grad_signal = pl.pallas_call(
         last_kernel,
@@ -287,6 +306,7 @@
     grad_residues, grad_rates = pl.pallas_call(
         functools.partial(gather_kernel, chunks),
         out_shape=[jax.ShapeDtypeStruct(residues.shape, F32), jax.ShapeDtypeStruct(log_rates.shape, F32)],
+        compiler_params=pltpu.CompilerParams(vmem_limit_bytes=8 * 2**20),
         name="unpack",
     )(everyone, log_rates)
     return mixed, grad_signal, grad_residues, grad_rates

time: 96.3 us -> 76.5 us (0.79)
  Pallas kernels: 51.4 us -> 34.5 us
  waiting for transfers between devices: 10.5 us -> 15.9 us
  starting transfers between devices: 25.9 us -> 22 us
  local copies, waits for them, and re-layouts: 6.5 us -> 2.75 us
    pallas_call x1, Pallas kernels: 23 us -> 14.4 us  [local(): pl.pallas_call(second_kernel, grid=(steps,), in_specs=[seq_block, seq_blo...]
    pallas_call x1, Pallas kernels: 17.2 us -> 11.2 us  [local(): pl.pallas_call(first_kernel, grid=(steps,), in_specs=[seq_block, seq_bloc...]
    all_to_all x1, waiting for transfers between devices: 0.01 us -> 4.9 us  [local(): got = lax.all_to_all(send, 'seq', 0, 0, tiled=True)]
    all_to_all x1, starting transfers between devices: 7.39 us -> 4.08 us  [local(): carried = lax.all_to_all(back, 'seq', 0, 0, tiled=True)]
    unnamed x6 -> x4, local copies, waits for them, and re-layouts: 1.86 us -> 0.01 us
    pallas_call x1 -> x2, Pallas kernels: 2.39 us -> 1.15 us  [the longest x1 0.88 us: local(): pl.pallas_call(functools.partial(carry_kernel, chunks), out_shape=jax.Sha...]
    pallas_call x1, Pallas kernels: 1.72 us -> 0.72 us  [local(): pl.pallas_call(functools.partial(gather_kernel, chunks), out_shape=[jax.S...]
  transfers between devices with their start and end apart: 6 -> 6, of which waited for: 4 -> 5; matrix products, arithmetic and copies ran while one was open for 3% -> 3% of each run, Pallas kernels for 31% -> 29%
where the time goes in v3:
time: 76.5 us; the launch traced here: 75.9 us
  Pallas kernels  34.5 us (45%)
  starting transfers between devices  22 us (29%)
  waiting for transfers between devices  15.9 us (21%)
  local copies, waits for them, and re-layouts  2.75 us (4%)
    pallas_call x1, Pallas kernels, local(): pl.pallas_call(second_kernel, grid=(steps,), in_specs=[seq_block, seq_blo...  14.4 us
    pallas_call x1, Pallas kernels, local(): pl.pallas_call(first_kernel, grid=(steps,), in_specs=[seq_block, seq_bloc...  11.2 us
    all_to_all x1, starting transfers between devices, local(): got = lax.all_to_all(send, 'seq', 0, 0, tiled=True)  9.73 us
    pallas_call x1, Pallas kernels, local(): pl.pallas_call(last_kernel, grid=(steps,), in_specs=[flat_block, flat_blo...  7.1 us
    all_to_all x1, waiting for transfers between devices, local(): got = lax.all_to_all(send, 'seq', 0, 0, tiled=True)  4.9 us
    all_to_all x1, starting transfers between devices, local(): everyone = lax.all_to_all(total, 'seq', 0, 0, tiled=True)  4.53 us
    all_to_all x1, waiting for transfers between devices, local(): carried = lax.all_to_all(back, 'seq', 0, 0, tiled=True)  4.4 us
    all_to_all x1, starting transfers between devices, local(): carried = lax.all_to_all(back, 'seq', 0, 0, tiled=True)  4.08 us
  transfers between devices with their start and end apart: 6, of which 5 were waited for; matrix products, arithmetic and copies ran while one was open for 3% of the time, Pallas kernels for 29%

profile of v3, /device:TPU:1, one launch (start us, length us, event | category | flops | bytes accessed | tf_op | source)
XLA Modules:
  0.0 75.9 jit_solution(11959123078127882099)
XLA Ops:
  0.6 11.2 %ends_and_lags.1 = f32[32,88,128]{2,1,0:T(8,128)} custom-call(bf16[1,128,8192]{2,1,0:T(8,128)(2,1)} %x_ref.3, bf16[1,128,8192]{2,1,0:T(8,128)(2,1)} %g_ref.3, f32[8,512]{1,0:T(8,128)} %log_ref.3, f32[8,8192]{1,0:T(8,128)} %res_ref.3, bf16[256,256]{1,0:T(8,128)(2,1)} %constant.20.clone.fwd_ref, bf16[128,768]{1,0:T(8,128)(2,1)} %constant.21.clone.inv_ref), custom_call_target="tpu_custom_call" | custom-call | tf_op jit(solution)/shard_map/ends_and_lags/pallas_call | solution.py:239
  11.8 0.0 copy-start
  11.8 9.7 %all-to-all-start = ((f32[32,88,128]{2,1,0:T(8,128)}), f32[32,88,128]{2,1,0:T(8,128)S(1)}, u32[]{:S(2)}, u32[]{:S(2)}) async-start(f32[32,88,128]{2,1,0:T(8,128)} %ends_and_lags.1), calls=%async_computation | async-start | bytes 2883584 | tf_op jit(solution)/shard_map/all_to_all | solution.py:254
  21.6 0.0 copy-done
  21.6 0.1 constant_dynamic-slice_fusion.1
  21.7 0.1 broadcast_in_dim.21
  21.7 0.1 reshape.14.rate_ref
  21.8 0.1 copy.10
  22.0 0.2 broadcast_in_dim.19
  22.1 0.7 constant_dynamic-slice_fusion.res_ref
  22.8 0.7 broadcast_in_dim.20.rate_ref
  23.5 14.4 %local_convolutions.1 = (f32[128,8192]{1,0:T(8,128)}, f32[128,8192]{1,0:T(8,128)}) custom-call(bf16[1,128,8192]{2,1,0:T(8,128)(2,1)} %x_ref.3, bf16[1,128,8192]{2,1,0:T(8,128)(2,1)} %g_ref.3, f32[32,8,128]{2,1,0:T(8,128)} %broadcast_in_dim.20.rate_ref, f32[8,8192]{1,0:T(8,128)} %res_ref.3, bf16[256,256]{1,0:T(8,128)(2,1)} %constant.20.clone.fwd_ref, ...), custom_call_target="tpu_custom_call" | custom-call | flops 6291456000 | bytes 16777216 | tf_op jit(solution)/shard_map/local_convolutions/pallas_call | solution.py:256
  37.9 4.9 %all-to-all-done.got_ref = f32[32,88,128]{2,1,0:T(8,128)S(1)} async-done(((f32[32,88,128]{2,1,0:T(8,128)}), f32[32,88,128]{2,1,0:T(8,128)S(1)}, u32[]{:S(2)}, u32[]{:S(2)}) %all-to-all-start) | async-done | bytes 1441824 | tf_op jit(solution)/shard_map/all_to_all | solution.py:254
  42.8 0.9 %carries.1 = f32[32,32,128]{2,1,0:T(8,128)} custom-call(f32[32,88,128]{2,1,0:T(8,128)S(1)} %all-to-all-done.got_ref, f32[8,256]{1,0:T(8,128)S(1)} %reshape.14.rate_ref, f32[8,256]{1,0:T(8,128)S(1)} %constant_dynamic-slice_fusion.res_ref), custom_call_target="tpu_custom_call" | custom-call | tf_op jit(solution)/shard_map/carries/pallas_call | solution.py:269
  43.7 4.1 %all-to-all-start.1 = ((f32[32,32,128]{2,1,0:T(8,128)}), f32[32,32,128]{2,1,0:T(8,128)S(1)}, u32[]{:S(2)}, u32[]{:S(2)}) async-start(f32[32,32,128]{2,1,0:T(8,128)} %carries.1), calls=%async_computation.1 | async-start | bytes 1048576 | tf_op jit(solution)/shard_map/all_to_all | solution.py:276
  47.7 0.3 gradient_sums.1
  48.0 2.5 %collective-permute-start.2 = (f32[24,128]{1,0:T(8,128)S(1)}, f32[24,128]{1,0:T(8,128)S(1)}, u32[]{:S(2)}, u32[]{:S(2)}) collective-permute-start(f32[24,128]{1,0:T(8,128)S(1)} %gradient_sums.1), channel_id=1, source_target_pairs={{0,3},{1,0},{2,1},{3,2},{4,7},{5,4},{6,5},{7,6},{8,11},{9,8},{10,9... | collective-permute-start | bytes 36872 | tf_op jit(solution)/shard_map/ppermute | solution.py:286
  50.5 0.5 collective-permute-start.1
  51.0 0.6 collective-permute-start
  51.6 0.0 collective-permute-done.2
  51.6 3.2 %collective-permute-done.1 = f32[24,128]{1,0:T(8,128)S(1)} collective-permute-done((f32[24,128]{1,0:T(8,128)S(1)}, f32[24,128]{1,0:T(8,128)S(1)}, u32[]{:S(2)}, u32[]{:S(2)}) %collective-permute-start.1) | collective-permute-done | bytes 12320 | tf_op jit(solution)/shard_map/ppermute | solution.py:286
  54.8 0.2 collective-permute-done
  55.1 4.4 %all-to-all-done.1.got_ref = f32[32,32,128]{2,1,0:T(8,128)S(1)} async-done(((f32[32,32,128]{2,1,0:T(8,128)}), f32[32,32,128]{2,1,0:T(8,128)S(1)}, u32[]{:S(2)}, u32[]{:S(2)}) %all-to-all-start.1) | async-done | bytes 524320 | tf_op jit(solution)/shard_map/all_to_all | solution.py:276
  59.5 0.0 copy-start.1
  59.5 0.8 %broadcast_in_dim.23 = f32[32,24,128]{2,1,0:T(8,128)} broadcast(f32[24,128]{1,0:T(8,128)S(1)} %add_add_fusion), dimensions={1,2} | broadcast | bytes 405504 | tf_op jit(solution)/shard_map/broadcast_in_dim | solution.py:287
  60.3 4.5 %all-to-all-start.2 = ((f32[32,24,128]{2,1,0:T(8,128)}), f32[32,24,128]{2,1,0:T(8,128)S(1)}, u32[]{:S(2)}, u32[]{:S(2)}) async-start(f32[32,24,128]{2,1,0:T(8,128)} %broadcast_in_dim.23), calls=%async_computation.2 | async-start | bytes 786432 | tf_op jit(solution)/shard_map/all_to_all | solution.py:289
  64.9 0.0 copy-done.1
  64.9 7.1 %add_carries.1 = (bf16[1,128,8192]{2,1,0:T(8,128)(2,1)}, bf16[1,128,8192]{2,1,0:T(8,128)(2,1)}) custom-call(f32[128,8192]{1,0:T(8,128)} %get-tuple-element.24.mixed_ref, f32[128,8192]{1,0:T(8,128)} %get-tuple-element.25.grad_ref, f32[32,8,128]{2,1,0:T(8,128)} %broadcast_in_dim.20.rate_ref, f32[32,32,128]{2,1,0:T(8,128)} %copy-done.1), custom_call_target="tpu_custom_call" | custom-call | flops 1677721600 | bytes 12582912 | tf_op jit(solution)/shard_map/add_carries/pallas_call | solution.py:291
  72.0 3.2 %all-to-all-done.2.all_ref = f32[32,24,128]{2,1,0:T(8,128)S(1)} async-done(((f32[32,24,128]{2,1,0:T(8,128)}), f32[32,24,128]{2,1,0:T(8,128)S(1)}, u32[]{:S(2)}, u32[]{:S(2)}) %all-to-all-start.2) | async-done | bytes 393248 | tf_op jit(solution)/shard_map/all_to_all | solution.py:289
  75.2 0.7 unpack.1
  (2 shorter events, 0.0 us)
Async XLA Ops:
  11.8 9.7 %copy-start = (f32[8,512]{1,0:T(8,128)S(1)}, f32[8,512]{1,0:T(8,128)}, u32[]{:S(2)}) copy-start(f32[8,512]{1,0:T(8,128)} %log_ref.3) | copy-start | bytes 49156
  11.8 31.0 %all-to-all-start = ((f32[32,88,128]{2,1,0:T(8,128)}), f32[32,88,128]{2,1,0:T(8,128)S(1)}, u32[]{:S(2)}, u32[]{:S(2)}) async-start(f32[32,88,128]{2,1,0:T(8,128)} %ends_and_lags.1), calls=%async_computation | async-start | bytes 2883584 | tf_op jit(solution)/shard_map/all_to_all | solution.py:254
  43.7 15.8 %all-to-all-start.1 = ((f32[32,32,128]{2,1,0:T(8,128)}), f32[32,32,128]{2,1,0:T(8,128)S(1)}, u32[]{:S(2)}, u32[]{:S(2)}) async-start(f32[32,32,128]{2,1,0:T(8,128)} %carries.1), calls=%async_computation.1 | async-start | bytes 1048576 | tf_op jit(solution)/shard_map/all_to_all | solution.py:276
  48.0 3.6 %collective-permute-start.2 = (f32[24,128]{1,0:T(8,128)S(1)}, f32[24,128]{1,0:T(8,128)S(1)}, u32[]{:S(2)}, u32[]{:S(2)}) collective-permute-start(f32[24,128]{1,0:T(8,128)S(1)} %gradient_sums.1), channel_id=1, source_target_pairs={{0,3},{1,0},{2,1},{3,2},{4,7},{5,4},{6,5},{7,6},{8,11},{9,8},{10,9... | collective-permute-start | bytes 36872 | tf_op jit(solution)/shard_map/ppermute | solution.py:286
  50.5 4.3 %collective-permute-start.1 = (f32[24,128]{1,0:T(8,128)S(1)}, f32[24,128]{1,0:T(8,128)S(1)}, u32[]{:S(2)}, u32[]{:S(2)}) collective-permute-start(f32[24,128]{1,0:T(8,128)S(1)} %gradient_sums.1), channel_id=1, source_target_pairs={{0,2},{1,3},{2,0},{3,1},{4,6},{5,7},{6,4},{7,5},{8,10},{9,11},{10,... | collective-permute-start | bytes 36872 | tf_op jit(solution)/shard_map/ppermute | solution.py:286
  51.0 4.1 %collective-permute-start = (f32[24,128]{1,0:T(8,128)S(1)}, f32[24,128]{1,0:T(8,128)S(1)}, u32[]{:S(2)}, u32[]{:S(2)}) collective-permute-start(f32[24,128]{1,0:T(8,128)S(1)} %gradient_sums.1), channel_id=1, source_target_pairs={{0,1},{1,2},{2,3},{3,0},{4,5},{5,6},{6,7},{7,4},{8,9},{9,10},{10,1... | collective-permute-start | bytes 36872 | tf_op jit(solution)/shard_map/ppermute | solution.py:286
  59.5 5.4 %copy-start.1 = (f32[32,32,128]{2,1,0:T(8,128)}, f32[32,32,128]{2,1,0:T(8,128)S(1)}, u32[]{:S(2)}) copy-start(f32[32,32,128]{2,1,0:T(8,128)S(1)} %all-to-all-done.1.got_ref) | copy-start | bytes 1572868
  60.3 14.8 %all-to-all-start.2 = ((f32[32,24,128]{2,1,0:T(8,128)}), f32[32,24,128]{2,1,0:T(8,128)S(1)}, u32[]{:S(2)}, u32[]{:S(2)}) async-start(f32[32,24,128]{2,1,0:T(8,128)} %broadcast_in_dim.23), calls=%async_computation.2 | async-start | bytes 786432 | tf_op jit(solution)/shard_map/all_to_all | solution.py:289

commit v4 on v3

v4 whole, which is shorter than its diff:
```python
import functools

import jax
import jax.numpy as jnp
import numpy as np
from jax import lax
from jax.experimental import pallas as pl
from jax.experimental.pallas import tpu as pltpu
from jax.sharding import PartitionSpec as P

M = 8
GROUP = 16
SPAN = 128
SLICE = 256
GROUPS = SLICE // GROUP
WIDE = 2048
F32 = jnp.float32
BF16 = jnp.bfloat16


def split_np(values):
    high = values.astype(np.float32).astype(jnp.bfloat16)
    low = (values - high.astype(np.float64)).astype(np.float32).astype(jnp.bfloat16)
    return high, low


def transforms():
    time = np.arange(SPAN)
    angle = 2 * np.pi * np.outer(np.arange(SPAN) + 0.5, time) / (2 * SPAN)
    forward = np.concatenate([np.cos(angle), -np.sin(angle)], 0)
    inverse = np.concatenate([np.cos(angle.T), -np.sin(angle.T)], 1) / SPAN
    fh, fl = split_np(forward)
    ih, il = split_np(inverse)
    return np.concatenate([fh, fl], 1), np.concatenate([ih, il, ih], 1)


def split(values):
    high = values.astype(BF16)
    return high, (values - high.astype(F32)).astype(BF16)


def dot(a, b):
    return jnp.dot(a, b, preferred_element_type=F32)


def twice(values):
    return jnp.concatenate([values, values], 0)


def stacked(values):
    high, low = split(values)
    return jnp.concatenate([high, high, low], 0)


def lane_group(rows, lanes):
    return lax.broadcasted_iota(jnp.int32, (rows, lanes), 1) // GROUP


def spread(values):
    high = values.astype(BF16).astype(F32)
    low = values - high
    owner = lane_group(M, SLICE)

    def rows(part):
        return jnp.concatenate([jnp.where(owner == g, part, 0.0) for g in range(GROUPS)], 0).astype(BF16)

    top, bottom = rows(high), rows(low)
    return jnp.concatenate([top, top, bottom, bottom], 0)


def powers(rate_row, reverse):
    t = lax.broadcasted_iota(jnp.int32, (SPAN, SPAN), 0)
    t = (SPAN - 1 - t if reverse else t).astype(F32)
    high, low = split(jnp.exp(-rate_row[0:1, :] * t))
    return jnp.concatenate([high, low, high, low], 1)


def first_kernel(half_ref, x_ref, g_ref, log_ref, res_ref, fwd_ref, inv_ref, send_ref):
    x, g = x_ref[0], g_ref[0]
    xx, gg = twice(x), twice(g)
    forward = fwd_ref[...]
    xf = dot(forward, xx)
    gf = dot(forward, gg)
    xr, xi, gr, gi = xf[:SPAN], xf[SPAN:], gf[:SPAN], gf[SPAN:]
    lags = dot(inv_ref[...], stacked(jnp.concatenate([gr * xr + gi * xi, gi * xr - gr * xi], 0)))
    lag_high, lag_low = split(lags)
    lag_high, lag_low = twice(lag_high), twice(lag_low)
    flip = jnp.where(lax.broadcasted_iota(jnp.int32, (SPAN, SPAN), 0) + lax.broadcasted_iota(jnp.int32, (SPAN, SPAN), 1) == SPAN - 1, 1.0, 0.0).astype(BF16)
    backward = twice(dot(flip, x).astype(BF16))
    lag = lax.broadcasted_iota(jnp.int32, (SPAN, SPAN), 1).astype(F32)
    half = SPAN // GROUP
    owner = lane_group(M, SPAN)
    row = lax.broadcasted_iota(jnp.int32, (SPAN, SPAN), 0) // GROUP
    col = lax.broadcasted_iota(jnp.int32, (SPAN, SPAN), 1)

    def pick(values, q):
        at = q * half * M
        chosen = values[at : at + M]
        for k in range(1, half):
            chosen = jnp.where(owner == k, values[at + k * M : at + (k + 1) * M], chosen)
        return chosen

    count = log_ref.shape[1] // GROUPS
    rate = jnp.exp(log_ref[...])
    weighted = ([], [])
    for s in range(count):
        at = s * GROUPS
        rates = jnp.concatenate([jnp.broadcast_to(rate[:, k : k + 1], (M, SPAN)) for k in range(at, at + GROUPS)], 0)
        early = jnp.exp(-rates * lag)
        for h in range(2):
            rows = slice(h * half * M, (h + 1) * half * M)
            cols = slice(s * SLICE + h * SPAN, s * SLICE + (h + 1) * SPAN)
            eh, el = split(jnp.concatenate([early[rows], lag[rows] * early[rows]], 0))
            found = dot(
                jnp.concatenate([eh, el], 1),
                jnp.concatenate([backward[:, cols], gg[:, cols], lag_high[:, cols], lag_low[:, cols]], 1),
            )
            ends, starts = found[:, :SPAN], found[:, SPAN : 2 * SPAN]
            sums = found[:, 2 * SPAN : 3 * SPAN] + found[:, 3 * SPAN :]
            for q, values in enumerate((pick(ends, 0), pick(starts, 0), pick(ends, 1), pick(starts, 1), pick(sums, 0))):
                at = (2 * q + h) * M
                send_ref[s, at : at + M, :] = values
            weighted[h].append(res_ref[:, cols] * pick(sums, 1))
    total = jnp.zeros((count * M, SPAN), F32)
    for h in range(2):
        place = jnp.where(row + h * half == col, 1.0, 0.0).astype(BF16)
        wh, wl = split(jnp.concatenate(weighted[h], 0))
        total = total + dot(jnp.concatenate([wh, wl], 1), twice(place))
    for s in range(count):
        send_ref[s, 10 * M : 11 * M, :] = total[s * M : (s + 1) * M]


def second_kernel(x_ref, g_ref, rate_ref, res_ref, fwd_ref, inv_ref, *rest):
    mixed_ref, grad_ref = rest[-2:]
    forward = fwd_ref[...]
    taps = [
        dot(powers(rate_ref[s], False), spread(res_ref[:, s * SLICE : (s + 1) * SLICE]))
        for s in range(rate_ref.shape[0])
    ]
    high, low = split(jnp.concatenate(taps, 1))
    kf = dot(forward, twice(high)) + dot(fwd_ref[:, :SPAN], low)
    xf = dot(forward, twice(x_ref[0]))
    gf = dot(forward, twice(g_ref[0]))
    kr, ki, xr, xi, gr, gi = kf[:SPAN], kf[SPAN:], xf[:SPAN], xf[SPAN:], gf[:SPAN], gf[SPAN:]
    mixed_ref[...] = dot(inv_ref[...], stacked(jnp.concatenate([kr * xr - ki * xi, kr * xi + ki * xr], 0)))
    grad_ref[...] = dot(inv_ref[...], stacked(jnp.concatenate([kr * gr + ki * gi, kr * gi - ki * gr], 0)))


def per_channel(values, at):
    owner = lane_group(M, SPAN)
    chosen = jnp.broadcast_to(values[:, at : at + 1], (M, SPAN))
    for k in range(1, SPAN // GROUP):
        chosen = jnp.where(owner == k, values[:, at + k : at + k + 1], chosen)
    return chosen


def placed(parts, h, offset):
    row = lax.broadcasted_iota(jnp.int32, (SPAN, SPAN), 0) // GROUP
    col = lax.broadcasted_iota(jnp.int32, (SPAN, SPAN), 1)
    place = jnp.where(row + (h * (SPAN // GROUP) + offset) == col, 1.0, 0.0).astype(BF16)
    high, low = split(parts)
    return dot(jnp.concatenate([high, low], 1), twice(place))


def pair_kernel(core_ref, kept_ref, arrived_ref, log_ref, res_ref, pair_ref):
    even = core_ref[0] == 0
    count = kept_ref.shape[0]
    rate = jnp.exp(log_ref[...])
    pole, across = jnp.exp(-rate), jnp.exp(-rate * SPAN)
    weighted = ([], [])
    for s in range(count):
        for h in range(2):

            def both(q):
                rows = slice((2 * q + h) * M, (2 * q + h + 1) * M)
                kept, arrived = kept_ref[s, rows, :], arrived_ref[s, rows, :]
                return jnp.where(even, kept, arrived), jnp.where(even, arrived, kept)

            def put(q, values):
                pair_ref[s, (2 * q + h) * M : (2 * q + h + 1) * M, :] = values

            lanes = s * GROUPS + h * (SPAN // GROUP)
            p, far = per_channel(pole, lanes), per_channel(across, lanes)
            (s1, s2), (t1, t2), (u1, u2), (w1, w2), (r1, r2) = (both(q) for q in range(5))
            put(0, far * s1 + s2)
            put(1, t1 + far * t2)
            put(2, far * (u1 + SPAN * s1) + u2)
            put(3, w1 + far * (w2 + SPAN * t2))
            put(4, r1 + r2 + p * s1 * t2)
            cols = slice(s * SLICE + h * SPAN, s * SLICE + (h + 1) * SPAN)
            weighted[h].append(res_ref[:, cols] * p * (s1 * (w2 + t2) + u1 * t2))
    total = placed(jnp.concatenate(weighted[0], 0), 0, 0) + placed(jnp.concatenate(weighted[1], 0), 1, 0)
    for s in range(count):
        rows = slice(10 * M, 11 * M)
        pair_ref[s, rows, :] = kept_ref[s, rows, :] + arrived_ref[s, rows, :] + total[s * M : (s + 1) * M]


def carry_kernel(pairs, got_ref, rate_ref, res_ref, back_ref):
    for h in range(2):
        cols = slice(h * SPAN, (h + 1) * SPAN)
        rate = rate_ref[:, cols]
        across = jnp.exp(-rate * (2 * SPAN))
        handed = res_ref[:, cols] * jnp.exp(-rate)
        state = jnp.zeros((M, SPAN), F32)
        adjoint = state
        for k in range(pairs):
            last = pairs - 1 - k
            back_ref[k, h * M : (h + 1) * M, :] = handed * state
            back_ref[last, (2 + h) * M : (3 + h) * M, :] = handed * adjoint
            state = across * state + got_ref[k, h * M : (h + 1) * M, :]
            adjoint = across * adjoint + got_ref[last, (2 + h) * M : (3 + h) * M, :]


def sums_kernel(pairs, scale, index_ref, got_ref, rate_ref, res_ref, sums_ref):
    offset = lax.rem(index_ref[0], SPAN // GROUPS) * GROUPS
    rate_sum = jnp.zeros((M, SPAN), F32)
    for k in range(pairs):
        rate_sum = rate_sum + got_ref[k, 10 * M : 11 * M, :]
    rate_sum = pltpu.roll(rate_sum, offset, 1)
    for h in range(2):
        cols = slice(h * SPAN, (h + 1) * SPAN)
        rate, res = rate_ref[:, cols], res_ref[:, cols]
        pole = jnp.exp(-rate)
        across = jnp.exp(-rate * (2 * SPAN))

        def part(k, q):
            at = (2 * q + h) * M
            return got_ref[k, at : at + M, :]

        zero = jnp.zeros((M, SPAN), F32)
        state, moment, res_part, res_carry, rate_carry = zero, zero, zero, zero, zero
        for k in range(pairs):
            start = part(k, 1)
            res_part = res_part + part(k, 4)
            res_carry = res_carry + state * start
            rate_carry = rate_carry + state * (part(k, 3) + start) + moment * start
            moment = across * (moment + 2 * SPAN * state) + part(k, 2)
            state = across * state + part(k, 0)
        sums_ref[h * M : (h + 1) * M, :] = scale * (res_part + pole * res_carry)
        rate_sum = rate_sum + placed(res * pole * rate_carry, h, offset)
    sums_ref[2 * M : 3 * M, :] = scale * rate_sum


def last_kernel(
    core_ref, mixed_ref, grad_ref, rate_ref, log_ref, res_ref, mine_ref, other_ref, near_ref, far_ref, mixed_out, grad_out
):
    core = core_ref[0]
    even = core == 0
    here = pl.program_id(0) // (pl.num_programs(0) // 2) == core
    rate = jnp.exp(log_ref[...])
    pole, across = jnp.exp(-rate), jnp.exp(-rate * SPAN)
    for s in range(rate_ref.shape[0]):
        cols = slice(s * SLICE, (s + 1) * SLICE)
        states, adjoints = [], []
        for h in range(2):

            def chosen(a_ref, b_ref, q):
                rows = slice((2 * q + h) * M, (2 * q + h + 1) * M)
                return jnp.where(here, a_ref[s, rows, :], b_ref[s, rows, :])

            lanes = s * GROUPS + h * (SPAN // GROUP)
            p, far = per_channel(pole, lanes), per_channel(across, lanes)
            handed = res_ref[:, s * SLICE + h * SPAN : s * SLICE + (h + 1) * SPAN] * p
            state, adjoint = chosen(mine_ref, other_ref, 0), chosen(mine_ref, other_ref, 1)
            end, start = chosen(near_ref, far_ref, 0), chosen(near_ref, far_ref, 1)
            states.append(jnp.where(even, state, far * state + handed * end))
            adjoints.append(jnp.where(even, far * adjoint + handed * start, adjoint))
        more = dot(powers(rate_ref[s], False), spread(jnp.concatenate(states, 1)))
        mixed_out[0, :, cols] = (mixed_ref[:, cols] + more).astype(BF16)
        more = dot(powers(rate_ref[s], True), spread(jnp.concatenate(adjoints, 1)))
        grad_out[0, :, cols] = (grad_ref[:, cols] + more).astype(BF16)


def gather_kernel(pairs, core_ref, mine_ref, other_ref, log_ref, res_out, rate_out):
    chunks = 2 * pairs

    def part(k, rows):
        return jnp.where(core_ref[0] == k // pairs, mine_ref[k % pairs, rows, :], other_ref[k % pairs, rows, :])

    for k in range(chunks):
        for h in range(2):
            res_out[:, k * SLICE + h * SPAN : k * SLICE + (h + 1) * SPAN] = part(k, slice(h * M, (h + 1) * M))
    width = min(SPAN, chunks * GROUPS)
    per = width // GROUPS
    rows = slice(2 * M, 3 * M)
    for j in range(chunks // per):
        parts = part(j * per, rows)
        for k in range(j * per + 1, (j + 1) * per):
            parts = parts + part(k, rows)
        cols = slice(j * width, (j + 1) * width)
        rate_out[:, cols] = -jnp.exp(log_ref[:, cols]) * parts[:, :width]


def local(signal, out_grad, residues, log_rates):
    channels = signal.shape[2]
    chunks, rows = lax.axis_size("seq"), lax.axis_size("batch")
    index = lax.axis_index("seq").astype(jnp.int32)
    pairs = chunks // 2
    core = lax.rem(index, 2)
    own = core * pairs + index // 2
    swap = [(i, i ^ 1) for i in range(chunks)]
    same_core = [[2 * j + c for j in range(pairs)] for c in range(2)]
    wide = min(WIDE, channels // 2)
    steps = channels // wide
    part = steps // 2
    block = wide // SLICE
    fwd, inv = (jnp.asarray(v) for v in transforms())
    params = pltpu.CompilerParams(vmem_limit_bytes=58 * 2**20)
    little = pltpu.CompilerParams(vmem_limit_bytes=8 * 2**20)
    vmem, smem = pl.BlockSpec(memory_space=pltpu.VMEM), pl.BlockSpec(memory_space=pltpu.SMEM)
    states_shape = jax.ShapeDtypeStruct((pairs, 11 * M, SPAN), F32)
    core_scalar = core[None]

    def whole(a):
        return pl.BlockSpec(a.shape, lambda i, *_: (0,) * a.ndim)

    def exchange(values):
        return lax.all_to_all(values, "seq", 0, 0, axis_index_groups=same_core, tiled=True)

    def other_core(values):
        return lax.ppermute(values, "seq", swap)

    def ends_and_lags(half, x, g):
        return pl.pallas_call(
            first_kernel,
            grid_spec=pltpu.PrefetchScalarGridSpec(
                num_scalar_prefetch=1,
                grid=(part,),
                in_specs=[
                    pl.BlockSpec((1, SPAN, wide), lambda i, at: (0, 0, at[0] * part + i)),
                    pl.BlockSpec((1, SPAN, wide), lambda i, at: (0, 0, at[0] * part + i)),
                    pl.BlockSpec((M, wide // GROUP), lambda i, at: (0, at[0] * part + i)),
                    pl.BlockSpec((M, wide), lambda i, at: (0, at[0] * part + i)),
                    whole(fwd),
                    whole(inv),
                ],
                out_specs=pl.BlockSpec((block, 11 * M, SPAN), lambda i, at: (i, 0, 0)),
            ),
            out_shape=states_shape,
            compiler_params=params,
            name="ends_and_lags",
        )(half, x, g, log_rates, residues, fwd, inv)

    away = ends_and_lags(1 - core_scalar, signal, out_grad)
    away, x2, g2 = lax.optimization_barrier((away, signal, out_grad))
    arrived = other_core(away)
    kept = ends_and_lags(core_scalar, x2, g2)
    state_block = pl.BlockSpec((block, 11 * M, SPAN), lambda i, at: (i, 0, 0))
    pair = pl.pallas_call(
        pair_kernel,
        grid_spec=pltpu.PrefetchScalarGridSpec(
            num_scalar_prefetch=1,
            grid=(part,),
            in_specs=[
                state_block,
                state_block,
                pl.BlockSpec((M, wide // GROUP), lambda i, at: (0, at[0] * part + i)),
                pl.BlockSpec((M, wide), lambda i, at: (0, at[0] * part + i)),
            ],
            out_specs=state_block,
        ),
        out_shape=states_shape,
        compiler_params=little,
        name="join_pair",
    )(core_scalar, kept, arrived, log_rates, residues)
    pair, later_rates, later_res, kept = lax.optimization_barrier((pair, log_rates, residues, kept))
    got = exchange(pair)
    arrived_far = other_core(kept)

    decay_rate = jnp.exp(later_rates)
    rate_rows = jnp.broadcast_to(decay_rate.T.reshape(chunks, 1, SPAN), (chunks, M, SPAN))
    own_rate = jnp.repeat(lax.dynamic_slice_in_dim(decay_rate, own * GROUPS, GROUPS, 1), GROUP, axis=1)
    own_res = lax.dynamic_slice_in_dim(later_res, own * SLICE, SLICE, 1)

    work = SPAN * channels

    def convolutions(half, x, g, *earlier):
        at = half * part
        kernel_blocks = [
            pl.BlockSpec((1, SPAN, wide), lambda i: (0, 0, at + i)),
            pl.BlockSpec((1, SPAN, wide), lambda i: (0, 0, at + i)),
            pl.BlockSpec((block, M, SPAN), lambda i: (at + i, 0, 0)),
            pl.BlockSpec((M, wide), lambda i: (0, at + i)),
            whole(fwd),
            whole(inv),
        ]
        return pl.pallas_call(
            second_kernel,
            grid=(part,),
            in_specs=kernel_blocks + [pl.BlockSpec(memory_space=pl.ANY)] * len(earlier),
            out_specs=[pl.BlockSpec((SPAN, wide), lambda i: (0, at + i))] * 2,
            out_shape=[jax.ShapeDtypeStruct((SPAN, channels), F32)] * 2,
            input_output_aliases={6: 0, 7: 1} if earlier else {},
            compiler_params=params,
            cost_estimate=pl.CostEstimate(flops=work * 300, bytes_accessed=work * 2, transcendentals=0),
            name="local_convolutions",
        )(x, g, rate_rows, residues, fwd, inv, *earlier)

    mixed_part, grad_part = convolutions(0, signal, out_grad)
    got, mixed_part, grad_part, arrived_far = lax.optimization_barrier((got, mixed_part, grad_part, arrived_far))
    back = pl.pallas_call(
        functools.partial(carry_kernel, pairs),
        out_shape=jax.ShapeDtypeStruct((pairs, 4 * M, SPAN), F32),
        compiler_params=little,
        name="carries",
    )(got, own_rate, own_res)
    back, got, x3, g3 = lax.optimization_barrier((back, got, signal, out_grad))
    carried = exchange(back)
    sums = pl.pallas_call(
        functools.partial(sums_kernel, pairs, 1.0 / (rows * chunks * SPAN)),
        out_shape=jax.ShapeDtypeStruct((3 * M, SPAN), F32),
        in_specs=[smem, vmem, vmem, vmem],
        compiler_params=little,
        cost_estimate=pl.CostEstimate(flops=10**10, bytes_accessed=10**7, transcendentals=0),
        name="gradient_sums",
    )(own[None], got, own_rate, own_res)
    arriving = [lax.ppermute(sums, "batch", [(i, (i + k) % rows) for i in range(rows)]) for k in range(1, rows)]
    mixed_part, grad_part = convolutions(1, x3, g3, mixed_part, grad_part)

    def total_kernel(*refs):
        total = refs[0][...]
        for ref in refs[1:-1]:
            total = total + ref[...]
        for k in range(pairs):
            refs[-1][k] = total

    total = pl.pallas_call(
        total_kernel,
        out_shape=jax.ShapeDtypeStruct((pairs, 3 * M, SPAN), F32),
        compiler_params=little,
        name="total",
    )(sums, *arriving)
    carried, total, mixed_part, grad_part = lax.optimization_barrier((carried, total, mixed_part, grad_part))
    carried_far = other_core(carried)
    everyone = exchange(total)

    flat_block = pl.BlockSpec((SPAN, wide), lambda i, at: (0, i))
    seq_block = pl.BlockSpec((1, SPAN, wide), lambda i, at: (0, 0, i))
    half_block = pl.BlockSpec((block, 4 * M, SPAN), lambda i, at: (lax.rem(i, part), 0, 0))
    mixed, grad_signal = pl.pallas_call(
        last_kernel,
        grid_spec=pltpu.PrefetchScalarGridSpec(
            num_scalar_prefetch=1,
            grid=(steps,),
            in_specs=[
                flat_block,
                flat_block,
                pl.BlockSpec((block, M, SPAN), lambda i, at: (i, 0, 0)),
                pl.BlockSpec((M, wide // GROUP), lambda i, at: (0, i)),
                pl.BlockSpec((M, wide), lambda i, at: (0, i)),
                half_block,
                half_block,
                half_block,
                half_block,
            ],
            out_specs=[seq_block, seq_block],
        ),
        out_shape=[jax.ShapeDtypeStruct(signal.shape, BF16)] * 2,
        compiler_params=params,
        cost_estimate=pl.CostEstimate(flops=work * 1600, bytes_accessed=work * 12, transcendentals=work),
        name="add_carries",
    )(core_scalar, mixed_part, grad_part, rate_rows, log_rates, residues, carried, carried_far, arrived, arrived_far)
    everyone, mixed, grad_signal = lax.optimization_barrier((everyone, mixed, grad_signal))
    grad_residues, grad_rates = pl.pallas_call(
        functools.partial(gather_kernel, pairs),
        out_shape=[jax.ShapeDtypeStruct(residues.shape, F32), jax.ShapeDtypeStruct(log_rates.shape, F32)],
        in_specs=[smem, vmem, vmem, vmem],
        compiler_params=little,
        name="unpack",
    )(core_scalar, everyone, other_core(everyone), log_rates)
    return mixed, grad_signal, grad_residues, grad_rates


def solution(mesh):
    sharded = P("batch", "seq", None)
    return jax.shard_map(
        local,
        mesh=mesh,
        in_specs=(sharded, sharded, P(), P()),
        out_specs=(sharded, sharded, P(), P()),
        check_vma=False,
    )
```

time: 76.5 us -> 78 us (1.020)
  waiting for transfers between devices: 15.9 us -> 2.9 us
  Pallas kernels: 34.5 us -> 43.7 us
  starting transfers between devices: 22 us -> 27.4 us
    all_to_all x3, waiting for transfers between devices: 12.5 us -> 1.73 us  [exchange(): lax.all_to_all(values, 'seq', 0, 0, axis_index_groups=same_core, tiled=True)]
    pallas_call x6 -> x10, Pallas kernels: 34.5 us -> 43.7 us  [the longest x2 16.8 us: convolutions(): pl.pallas_call(second_kernel, grid=(part,), in_specs=kernel_blocks + [pl....]
    ppermute x0 -> x4, starting transfers between devices: none -> 4 us  [other_core(): return lax.ppermute(values, 'seq', swap)]
    ppermute x3, waiting for transfers between devices: 3.44 us -> 0.01 us  [local(): lax.ppermute(sums, 'batch', [(i, (i + k) % rows) for i in range(rows)])]
    all_to_all x3, starting transfers between devices: 18.3 us -> 19.7 us  [exchange(): lax.all_to_all(values, 'seq', 0, 0, axis_index_groups=same_core, tiled=True)]
    ppermute x0 -> x4, waiting for transfers between devices: none -> 1.15 us  [other_core(): return lax.ppermute(values, 'seq', swap)]
    broadcast_in_dim x2 -> x1, local copies, waits for them, and re-layouts: 0.92 us -> 0.08 us  [local(): jnp.repeat(lax.dynamic_slice_in_dim(decay_rate, own * GROUPS, GROUPS, 1),...]
  transfers between devices with their start and end apart: 6 -> 10, of which waited for: 5 -> 2; matrix products, arithmetic and copies ran while one was open for 3% -> 2% of each run, Pallas kernels for 29% -> 42%
where the time goes in v4:
time: 78 us; the launch traced here: 77.4 us
  Pallas kernels  43.7 us (56%)
  starting transfers between devices  27.4 us (35%)
  waiting for transfers between devices  2.9 us (4%)
  local copies, waits for them, and re-layouts  2.63 us (3%)
  between operations  0.82 us (1%)
    all_to_all x3, starting transfers between devices, exchange(): lax.all_to_all(values, 'seq', 0, 0, axis_index_groups=same_core, tiled=True)  19.7 us
    pallas_call x2, Pallas kernels, convolutions(): pl.pallas_call(second_kernel, grid=(part,), in_specs=kernel_blocks + [pl....  16.8 us
    pallas_call x2, Pallas kernels, ends_and_lags(): pl.pallas_call(first_kernel, grid_spec=pltpu.PrefetchScalarGridSpec(num_s...  13.4 us
    pallas_call x1, Pallas kernels, local(): pl.pallas_call(last_kernel, grid_spec=pltpu.PrefetchScalarGridSpec(num_sc...  7.81 us
    ppermute x4, starting transfers between devices, other_core(): return lax.ppermute(values, 'seq', swap)  4 us
    ppermute x3, starting transfers between devices, local(): lax.ppermute(sums, 'batch', [(i, (i + k) % rows) for i in range(rows)])  3.68 us
    pallas_call x1, Pallas kernels, local(): pl.pallas_call(pair_kernel, grid_spec=pltpu.PrefetchScalarGridSpec(num_sc...  3.17 us
    all_to_all x3, waiting for transfers between devices, exchange(): lax.all_to_all(values, 'seq', 0, 0, axis_index_groups=same_core, tiled=True)  1.73 us
  transfers between devices with their start and end apart: 10, of which 2 were waited for; matrix products, arithmetic and copies ran while one was open for 2% of the time, Pallas kernels for 42%

profile of v4, /device:TPU:1, one launch (start us, length us, event | category | flops | bytes accessed | tf_op | source)
XLA Modules:
  0.0 77.4 jit_solution(5007949504471414041)
XLA Ops:
  0.6 0.0 copy-start
  0.6 0.0 copy-start.2
  0.7 6.8 %ends_and_lags.2 = f32[16,88,128]{2,1,0:T(8,128)} custom-call(s32[1]{0:T(128)S(6)} %sub.7.half_ref, bf16[1,128,8192]{2,1,0:T(8,128)(2,1)} %x_ref.5, bf16[1,128,8192]{2,1,0:T(8,128)(2,1)} %g_ref.5, f32[8,512]{1,0:T(8,128)} %log_ref.9, f32[8,8192]{1,0:T(8,128)} %res_ref.11, bf16[256,256]{1,0:T(8,128)(2,1)} %constant.35.clone.fwd_ref, ...), custom_call_target="tpu_custom_call" | custom-call | tf_op jit(solution)/shard_map/ends_and_lags/pallas_call | solution.py:324
  7.4 1.4 %collective-permute-start = (f32[16,88,128]{2,1,0:T(8,128)}, f32[16,88,128]{2,1,0:T(8,128)S(1)}, u32[]{:S(2)}, u32[]{:S(2)}) collective-permute-start(f32[16,88,128]{2,1,0:T(8,128)} %ends_and_lags.2), channel_id=1, source_target_pairs={{0,4},{4,0},{8,12},{12,8},{16,20},{20,16},{24,28},{28,24},{32,36},... | collective-permute-start | bytes 2162696 | tf_op jit(solution)/shard_map/ppermute | solution.py:321
  8.8 6.7 %ends_and_lags.3.kept_ref = f32[16,88,128]{2,1,0:T(8,128)} custom-call(s32[1]{0:T(128)} %bitcast.half_ref.core_ref, bf16[1,128,8192]{2,1,0:T(8,128)(2,1)} %x_ref.5, bf16[1,128,8192]{2,1,0:T(8,128)(2,1)} %g_ref.5, f32[8,512]{1,0:T(8,128)} %log_ref.9, f32[8,8192]{1,0:T(8,128)} %res_ref.11, bf16[256,256]{1,0:T(8,128)(2,1)} %constant.35.clone.fwd_ref, ...), custom_call_target="tpu_custom_call" | custom-call | tf_op jit(solution)/shard_map/ends_and_lags/pallas_call | solution.py:324
  15.5 0.0 collective-permute-done.arrived_ref.near_ref
  15.5 0.0 copy-done
  15.5 0.0 copy-done.2
  15.5 0.0 copy-start.1
  15.6 3.2 %join_pair.1 = f32[16,88,128]{2,1,0:T(8,128)} custom-call(s32[1]{0:T(128)} %bitcast.half_ref.core_ref, f32[16,88,128]{2,1,0:T(8,128)} %ends_and_lags.3.kept_ref, f32[16,88,128]{2,1,0:T(8,128)S(1)} %collective-permute-done.arrived_ref.near_ref, f32[8,512]{1,0:T(8,128)S(1)} %copy-done.2, f32[8,8192]{1,0:T(8,128)S(1)} %copy-done), custom_call_target="tpu_custom_call" | custom-call | tf_op jit(solution)/shard_map/join_pair/pallas_call | solution.py:349
  18.7 0.0 collective-permute-start.1
  18.8 7.8 %all-to-all-start = ((f32[16,88,128]{2,1,0:T(8,128)}), f32[16,88,128]{2,1,0:T(8,128)S(1)}, u32[]{:S(2)}, u32[]{:S(2)}) async-start(f32[16,88,128]{2,1,0:T(8,128)} %join_pair.1), calls=%async_computation | async-start | bytes 1441792 | tf_op jit(solution)/shard_map/all_to_all | solution.py:318
  26.7 0.1 constant_dynamic-slice_fusion.1
  26.7 0.1 broadcast_in_dim.19
  26.8 0.1 reshape.13.rate_ref
  26.9 0.1 copy.12
  27.0 0.2 broadcast_in_dim.17
  27.2 0.7 broadcast_in_dim.18.rate_ref
  27.9 8.4 %local_convolutions.2 = (f32[128,8192]{1,0:T(8,128)}, f32[128,8192]{1,0:T(8,128)}) custom-call(bf16[1,128,8192]{2,1,0:T(8,128)(2,1)} %x_ref.5, bf16[1,128,8192]{2,1,0:T(8,128)(2,1)} %g_ref.5, f32[32,8,128]{2,1,0:T(8,128)} %broadcast_in_dim.18.rate_ref, f32[8,8192]{1,0:T(8,128)} %res_ref.11, bf16[256,256]{1,0:T(8,128)(2,1)} %constant.35.clone.fwd_ref, ...), custom_call_target="tpu_custom_call" | custom-call | flops 314572800 | bytes 2097152 | tf_op jit(solution)/shard_map/local_convolutions/pallas_call | solution.py:387
  36.3 0.0 copy-done.1
  36.3 0.7 constant_dynamic-slice_fusion.res_ref
  37.0 1.7 %all-to-all-done.got_ref = f32[16,88,128]{2,1,0:T(8,128)S(1)} async-done(((f32[16,88,128]{2,1,0:T(8,128)}), f32[16,88,128]{2,1,0:T(8,128)S(1)}, u32[]{:S(2)}, u32[]{:S(2)}) %all-to-all-start) | async-done | bytes 720928 | tf_op jit(solution)/shard_map/all_to_all | solution.py:318
  38.7 0.0 collective-permute-done.1.far_ref
  38.7 0.0 copy-start.5
  38.7 0.8 %carries.1 = f32[16,32,128]{2,1,0:T(8,128)} custom-call(f32[16,88,128]{2,1,0:T(8,128)S(1)} %all-to-all-done.got_ref, f32[8,256]{1,0:T(8,128)S(1)} %reshape.13.rate_ref, f32[8,256]{1,0:T(8,128)S(1)} %constant_dynamic-slice_fusion.res_ref), custom_call_target="tpu_custom_call" | custom-call | tf_op jit(solution)/shard_map/carries/pallas_call | solution.py:401
  39.5 4.9 %all-to-all-start.1 = ((f32[16,32,128]{2,1,0:T(8,128)}), f32[16,32,128]{2,1,0:T(8,128)S(1)}, u32[]{:S(2)}, u32[]{:S(2)}) async-start(f32[16,32,128]{2,1,0:T(8,128)} %carries.1), calls=%async_computation.1 | async-start | bytes 524288 | tf_op jit(solution)/shard_map/all_to_all | solution.py:318
  44.4 0.2 gradient_sums.1.refs_0_
  44.6 0.0 copy-done.5
  44.6 2.5 %collective-permute-start.4 = (f32[24,128]{1,0:T(8,128)S(1)}, f32[24,128]{1,0:T(8,128)S(1)}, u32[]{:S(2)}, u32[]{:S(2)}) collective-permute-start(f32[24,128]{1,0:T(8,128)S(1)} %gradient_sums.1.refs_0_), channel_id=1, source_target_pairs={{0,3},{1,0},{2,1},{3,2},{4,7},{5,4},{6,5},{7,6},{8,11},{9,8},{10,9... | collective-permute-start | bytes 36872 | tf_op jit(solution)/shard_map/ppermute | solution.py:417
  47.2 0.5 collective-permute-start.3
  47.7 0.6 collective-permute-start.2
  48.3 8.4 %local_convolutions.3 = (f32[128,8192]{1,0:T(8,128)}, f32[128,8192]{1,0:T(8,128)}) custom-call(bf16[1,128,8192]{2,1,0:T(8,128)(2,1)} %x_ref.5, bf16[1,128,8192]{2,1,0:T(8,128)(2,1)} %g_ref.5, f32[32,8,128]{2,1,0:T(8,128)} %broadcast_in_dim.18.rate_ref, f32[8,8192]{1,0:T(8,128)} %res_ref.11, ...), custom_call_target="tpu_custom_call", output_to_operand_aliasing={{0}: (6, {}), {1}: (7, {})} | custom-call | flops 314572800 | bytes 2097152 | tf_op jit(solution)/shard_map/local_convolutions/pallas_call | solution.py:387
  56.7 0.0 collective-permute-done.4.refs_3_
  56.7 0.0 collective-permute-done.3.refs_2_
  56.7 0.0 collective-permute-done.2.refs_1_
  56.7 0.7 total.1
  57.5 0.0 all-to-all-done.1.mine_ref
  57.5 0.0 copy-start.4
  57.5 2.2 %collective-permute-start.5 = (f32[16,32,128]{2,1,0:T(8,128)S(1)}, f32[16,32,128]{2,1,0:T(8,128)S(1)}, u32[]{:S(2)}, u32[]{:S(2)}) collective-permute-start(f32[16,32,128]{2,1,0:T(8,128)S(1)} %all-to-all-done.1.mine_ref), channel_id=1, source_target_pairs={{0,4},{4,0},{8,12},{12,8},{16,20},{20,16},{24,28},{28,24},{32,36},... | collective-permute-start | bytes 786440 | tf_op jit(solution)/shard_map/ppermute | solution.py:321
  59.6 6.9 %all-to-all-start.2 = ((f32[16,24,128]{2,1,0:T(8,128)}), f32[16,24,128]{2,1,0:T(8,128)S(1)}, u32[]{:S(2)}, u32[]{:S(2)}) async-start(f32[16,24,128]{2,1,0:T(8,128)} %total.1), calls=%async_computation.2 | async-start | bytes 393216 | tf_op jit(solution)/shard_map/all_to_all | solution.py:318
  66.6 0.0 copy-start.3
  66.6 0.0 collective-permute-done.5.other_ref
  66.6 0.0 copy-done.4
  66.6 0.0 copy-start.6
  66.6 0.7 copy-done.6
  67.3 7.8 %add_carries.1 = (bf16[1,128,8192]{2,1,0:T(8,128)(2,1)}, bf16[1,128,8192]{2,1,0:T(8,128)(2,1)}) custom-call(s32[1]{0:T(128)} %bitcast.half_ref.core_ref, f32[128,8192]{1,0:T(8,128)} %get-tuple-element.53.mixed_ref, f32[128,8192]{1,0:T(8,128)} %get-tuple-element.54.grad_ref, f32[32,8,128]{2,1,0:T(8,128)} %broadcast_in_dim.18.rate_ref, f32[8,512]{1,0:T(8,128)} %log_ref.9, ...), custom_call_target="tpu_custom_call" | custom-call | flops 1677721600 | bytes 12582912 | tf_op jit(solution)/shard_map/add_carries/pallas_call | solution.py:440
  75.1 0.0 all-to-all-done.2.mine_ref
  75.1 0.4 collective-permute-start.6
  75.5 1.1 %collective-permute-done.6.other_ref = f32[16,24,128]{2,1,0:T(8,128)S(1)} collective-permute-done((f32[16,24,128]{2,1,0:T(8,128)S(1)}, f32[16,24,128]{2,1,0:T(8,128)S(1)}, u32[]{:S(2)}, u32[]{:S(2)}) %collective-permute-start.6) | collective-permute-done | bytes 196640 | tf_op jit(solution)/shard_map/ppermute | solution.py:321
  76.7 0.0 copy-done.3
  76.7 0.7 unpack.1
  (1 shorter events, 0.0 us)
Async XLA Ops:
  0.6 14.9 %copy-start = (f32[8,8192]{1,0:T(8,128)S(1)}, f32[8,8192]{1,0:T(8,128)}, u32[]{:S(2)}) copy-start(f32[8,8192]{1,0:T(8,128)} %res_ref.11) | copy-start | bytes 786436
  0.6 14.9 %copy-start.2 = (f32[8,512]{1,0:T(8,128)S(1)}, f32[8,512]{1,0:T(8,128)}, u32[]{:S(2)}) copy-start(f32[8,512]{1,0:T(8,128)} %log_ref.9) | copy-start | bytes 49156
  7.4 8.1 %collective-permute-start = (f32[16,88,128]{2,1,0:T(8,128)}, f32[16,88,128]{2,1,0:T(8,128)S(1)}, u32[]{:S(2)}, u32[]{:S(2)}) collective-permute-start(f32[16,88,128]{2,1,0:T(8,128)} %ends_and_lags.2), channel_id=1, source_target_pairs={{0,4},{4,0},{8,12},{12,8},{16,20},{20,16},{24,28},{28,24},{32,36},... | collective-permute-start | bytes 2162696 | tf_op jit(solution)/shard_map/ppermute | solution.py:321
  15.5 20.7 %copy-start.1 = (f32[16,88,128]{2,1,0:T(8,128)}, f32[16,88,128]{2,1,0:T(8,128)S(1)}, u32[]{:S(2)}) copy-start(f32[16,88,128]{2,1,0:T(8,128)S(1)} %collective-permute-done.arrived_ref.near_ref) | copy-start | bytes 2162692
  18.7 20.0 %collective-permute-start.1 = (f32[16,88,128]{2,1,0:T(8,128)}, f32[16,88,128]{2,1,0:T(8,128)S(1)}, u32[]{:S(2)}, u32[]{:S(2)}) collective-permute-start(f32[16,88,128]{2,1,0:T(8,128)} %ends_and_lags.3.kept_ref), channel_id=1, source_target_pairs={{0,4},{4,0},{8,12},{12,8},{16,20},{20,16},{24,28},{28,24},{32,36},... | collective-permute-start | bytes 2162696 | tf_op jit(solution)/shard_map/ppermute | solution.py:321
  18.8 19.9 %all-to-all-start = ((f32[16,88,128]{2,1,0:T(8,128)}), f32[16,88,128]{2,1,0:T(8,128)S(1)}, u32[]{:S(2)}, u32[]{:S(2)}) async-start(f32[16,88,128]{2,1,0:T(8,128)} %join_pair.1), calls=%async_computation | async-start | bytes 1441792 | tf_op jit(solution)/shard_map/all_to_all | solution.py:318
  38.7 5.9 %copy-start.5 = (f32[16,88,128]{2,1,0:T(8,128)}, f32[16,88,128]{2,1,0:T(8,128)S(1)}, u32[]{:S(2)}) copy-start(f32[16,88,128]{2,1,0:T(8,128)S(1)} %collective-permute-done.1.far_ref) | copy-start | bytes 2162692
  39.5 17.9 %all-to-all-start.1 = ((f32[16,32,128]{2,1,0:T(8,128)}), f32[16,32,128]{2,1,0:T(8,128)S(1)}, u32[]{:S(2)}, u32[]{:S(2)}) async-start(f32[16,32,128]{2,1,0:T(8,128)} %carries.1), calls=%async_computation.1 | async-start | bytes 524288 | tf_op jit(solution)/shard_map/all_to_all | solution.py:318
  44.6 12.1 %collective-permute-start.4 = (f32[24,128]{1,0:T(8,128)S(1)}, f32[24,128]{1,0:T(8,128)S(1)}, u32[]{:S(2)}, u32[]{:S(2)}) collective-permute-start(f32[24,128]{1,0:T(8,128)S(1)} %gradient_sums.1.refs_0_), channel_id=1, source_target_pairs={{0,3},{1,0},{2,1},{3,2},{4,7},{5,4},{6,5},{7,6},{8,11},{9,8},{10,9... | collective-permute-start | bytes 36872 | tf_op jit(solution)/shard_map/ppermute | solution.py:417
  47.2 9.6 %collective-permute-start.3 = (f32[24,128]{1,0:T(8,128)S(1)}, f32[24,128]{1,0:T(8,128)S(1)}, u32[]{:S(2)}, u32[]{:S(2)}) collective-permute-start(f32[24,128]{1,0:T(8,128)S(1)} %gradient_sums.1.refs_0_), channel_id=1, source_target_pairs={{0,2},{1,3},{2,0},{3,1},{4,6},{5,7},{6,4},{7,5},{8,10},{9,11},{10,... | collective-permute-start | bytes 36872 | tf_op jit(solution)/shard_map/ppermute | solution.py:417
  47.7 9.0 %collective-permute-start.2 = (f32[24,128]{1,0:T(8,128)S(1)}, f32[24,128]{1,0:T(8,128)S(1)}, u32[]{:S(2)}, u32[]{:S(2)}) collective-permute-start(f32[24,128]{1,0:T(8,128)S(1)} %gradient_sums.1.refs_0_), channel_id=1, source_target_pairs={{0,1},{1,2},{2,3},{3,0},{4,5},{5,6},{6,7},{7,4},{8,9},{9,10},{10,1... | collective-permute-start | bytes 36872 | tf_op jit(solution)/shard_map/ppermute | solution.py:417
  57.5 9.1 %copy-start.4 = (f32[16,32,128]{2,1,0:T(8,128)}, f32[16,32,128]{2,1,0:T(8,128)S(1)}, u32[]{:S(2)}) copy-start(f32[16,32,128]{2,1,0:T(8,128)S(1)} %all-to-all-done.1.mine_ref) | copy-start | bytes 786436
  57.5 9.1 %collective-permute-start.5 = (f32[16,32,128]{2,1,0:T(8,128)S(1)}, f32[16,32,128]{2,1,0:T(8,128)S(1)}, u32[]{:S(2)}, u32[]{:S(2)}) collective-permute-start(f32[16,32,128]{2,1,0:T(8,128)S(1)} %all-to-all-done.1.mine_ref), channel_id=1, source_target_pairs={{0,4},{4,0},{8,12},{12,8},{16,20},{20,16},{24,28},{28,24},{32,36},... | collective-permute-start | bytes 786440 | tf_op jit(solution)/shard_map/ppermute | solution.py:321
  59.6 15.5 %all-to-all-start.2 = ((f32[16,24,128]{2,1,0:T(8,128)}), f32[16,24,128]{2,1,0:T(8,128)S(1)}, u32[]{:S(2)}, u32[]{:S(2)}) async-start(f32[16,24,128]{2,1,0:T(8,128)} %total.1), calls=%async_computation.2 | async-start | bytes 393216 | tf_op jit(solution)/shard_map/all_to_all | solution.py:318
  66.6 10.1 %copy-start.3 = (f32[8,512]{1,0:T(8,128)S(1)}, f32[8,512]{1,0:T(8,128)}, u32[]{:S(2)}) copy-start(f32[8,512]{1,0:T(8,128)} %log_ref.9) | copy-start | bytes 49156
  66.6 0.7 copy-start.6
  75.1 1.5 %collective-permute-start.6 = (f32[16,24,128]{2,1,0:T(8,128)S(1)}, f32[16,24,128]{2,1,0:T(8,128)S(1)}, u32[]{:S(2)}, u32[]{:S(2)}) collective-permute-start(f32[16,24,128]{2,1,0:T(8,128)S(1)} %all-to-all-done.2.mine_ref), channel_id=1, source_target_pairs={{0,4},{4,0},{8,12},{12,8},{16,20},{20,16},{24,28},{28,24},{32,36},... | collective-permute-start | bytes 589832 | tf_op jit(solution)/shard_map/ppermute | solution.py:321

commit v5 on v4

--- a/solution.py
+++ b/solution.py
@@ -75,7 +75,7 @@
     return jnp.concatenate([high, low, high, low], 1)
 
 
-def first_kernel(half_ref, x_ref, g_ref, log_ref, res_ref, fwd_ref, inv_ref, send_ref):
+def first_kernel(half_ref, x_ref, g_ref, log_ref, res_ref, fwd_ref, inv_ref, send_ref, rate_out):
     x, g = x_ref[0], g_ref[0]
     xx, gg = twice(x), twice(g)
     forward = fwd_ref[...]
@@ -107,6 +107,8 @@
         at = s * GROUPS
         rates = jnp.concatenate([jnp.broadcast_to(rate[:, k : k + 1], (M, SPAN)) for k in range(at, at + GROUPS)], 0)
         early = jnp.exp(-rates * lag)
+        for h in range(2):
+            rate_out[s, h * M : (h + 1) * M, :] = pick(rates[h * half * M : (h + 1) * half * M], 0)
         for h in range(2):
             rows = slice(h * half * M, (h + 1) * half * M)
             cols = slice(s * SLICE + h * SPAN, s * SLICE + (h + 1) * SPAN)
@@ -162,11 +164,9 @@
     return dot(jnp.concatenate([high, low], 1), twice(place))
 
 
-def pair_kernel(core_ref, kept_ref, arrived_ref, log_ref, res_ref, pair_ref):
+def pair_kernel(core_ref, kept_ref, arrived_ref, rate_ref, res_ref, pair_ref):
     even = core_ref[0] == 0
     count = kept_ref.shape[0]
-    rate = jnp.exp(log_ref[...])
-    pole, across = jnp.exp(-rate), jnp.exp(-rate * SPAN)
     weighted = ([], [])
     for s in range(count):
         for h in range(2):
@@ -179,8 +179,8 @@
             def put(q, values):
                 pair_ref[s, (2 * q + h) * M : (2 * q + h + 1) * M, :] = values
 
-            lanes = s * GROUPS + h * (SPAN // GROUP)
-            p, far = per_channel(pole, lanes), per_channel(across, lanes)
+            rate = rate_ref[s, h * M : (h + 1) * M, :]
+            p, far = jnp.exp(-rate), jnp.exp(-rate * SPAN)
             (s1, s2), (t1, t2), (u1, u2), (w1, w2), (r1, r2) = (both(q) for q in range(5))
             put(0, far * s1 + s2)
             put(1, t1 + far * t2)
@@ -205,8 +205,9 @@
         adjoint = state
         for k in range(pairs):
             last = pairs - 1 - k
-            back_ref[k, h * M : (h + 1) * M, :] = handed * state
-            back_ref[last, (2 + h) * M : (3 + h) * M, :] = handed * adjoint
+            for c in range(2):
+                back_ref[2 * k + c, h * M : (h + 1) * M, :] = handed * state
+                back_ref[2 * last + c, (2 + h) * M : (3 + h) * M, :] = handed * adjoint
             state = across * state + got_ref[k, h * M : (h + 1) * M, :]
             adjoint = across * adjoint + got_ref[last, (2 + h) * M : (3 + h) * M, :]
 
@@ -242,7 +243,7 @@
 
 
 def last_kernel(
-    core_ref, mixed_ref, grad_ref, rate_ref, log_ref, res_ref, mine_ref, other_ref, near_ref, far_ref, mixed_out, grad_out
+    core_ref, mixed_ref, grad_ref, rate_ref, log_ref, res_ref, got_ref, near_ref, far_ref, mixed_out, grad_out
 ):
     core = core_ref[0]
     even = core == 0
@@ -254,15 +255,15 @@
         states, adjoints = [], []
         for h in range(2):
 
-            def chosen(a_ref, b_ref, q):
+            def chosen(q):
                 rows = slice((2 * q + h) * M, (2 * q + h + 1) * M)
-                return jnp.where(here, a_ref[s, rows, :], b_ref[s, rows, :])
+                return jnp.where(here, near_ref[s, rows, :], far_ref[s, rows, :])
 
             lanes = s * GROUPS + h * (SPAN // GROUP)
             p, far = per_channel(pole, lanes), per_channel(across, lanes)
             handed = res_ref[:, s * SLICE + h * SPAN : s * SLICE + (h + 1) * SPAN] * p
-            state, adjoint = chosen(mine_ref, other_ref, 0), chosen(mine_ref, other_ref, 1)
-            end, start = chosen(near_ref, far_ref, 0), chosen(near_ref, far_ref, 1)
+            state, adjoint = got_ref[s, h * M : (h + 1) * M, :], got_ref[s, (2 + h) * M : (3 + h) * M, :]
+            end, start = chosen(0), chosen(1)
             states.append(jnp.where(even, state, far * state + handed * end))
             adjoints.append(jnp.where(even, far * adjoint + handed * start, adjoint))
         more = dot(powers(rate_ref[s], False), spread(jnp.concatenate(states, 1)))
@@ -271,11 +272,11 @@
         grad_out[0, :, cols] = (grad_ref[:, cols] + more).astype(BF16)
 
 
-def gather_kernel(pairs, core_ref, mine_ref, other_ref, log_ref, res_out, rate_out):
+def gather_kernel(pairs, all_ref, log_ref, res_out, rate_out):
     chunks = 2 * pairs
 
     def part(k, rows):
-        return jnp.where(core_ref[0] == k // pairs, mine_ref[k % pairs, rows, :], other_ref[k % pairs, rows, :])
+        return all_ref[2 * (k % pairs) + k // pairs, rows, :]
 
     for k in range(chunks):
         for h in range(2):
@@ -334,17 +335,20 @@
                     whole(fwd),
                     whole(inv),
                 ],
-                out_specs=pl.BlockSpec((block, 11 * M, SPAN), lambda i, at: (i, 0, 0)),
+                out_specs=[
+                    pl.BlockSpec((block, 11 * M, SPAN), lambda i, at: (i, 0, 0)),
+                    pl.BlockSpec((block, 2 * M, SPAN), lambda i, at: (i, 0, 0)),
+                ],
             ),
-            out_shape=states_shape,
+            out_shape=[states_shape, jax.ShapeDtypeStruct((pairs, 2 * M, SPAN), F32)],
             compiler_params=params,
             name="ends_and_lags",
         )(half, x, g, log_rates, residues, fwd, inv)
 
-    away = ends_and_lags(1 - core_scalar, signal, out_grad)
+    away, _ = ends_and_lags(1 - core_scalar, signal, out_grad)
     away, x2, g2 = lax.optimization_barrier((away, signal, out_grad))
     arrived = other_core(away)
-    kept = ends_and_lags(core_scalar, x2, g2)
+    kept, channel_rates = ends_and_lags(core_scalar, x2, g2)
     state_block = pl.BlockSpec((block, 11 * M, SPAN), lambda i, at: (i, 0, 0))
     pair = pl.pallas_call(
         pair_kernel,
@@ -354,7 +358,7 @@
             in_specs=[
                 state_block,
                 state_block,
-                pl.BlockSpec((M, wide // GROUP), lambda i, at: (0, at[0] * part + i)),
+                pl.BlockSpec((block, 2 * M, SPAN), lambda i, at: (i, 0, 0)),
                 pl.BlockSpec((M, wide), lambda i, at: (0, at[0] * part + i)),
             ],
             out_specs=state_block,
@@ -362,7 +366,7 @@
         out_shape=states_shape,
         compiler_params=little,
         name="join_pair",
-    )(core_scalar, kept, arrived, log_rates, residues)
+    )(core_scalar, kept, arrived, channel_rates, residues)
     pair, later_rates, later_res, kept = lax.optimization_barrier((pair, log_rates, residues, kept))
     got = exchange(pair)
     arrived_far = other_core(kept)
@@ -400,12 +404,12 @@
     got, mixed_part, grad_part, arrived_far = lax.optimization_barrier((got, mixed_part, grad_part, arrived_far))
     back = pl.pallas_call(
         functools.partial(carry_kernel, pairs),
-        out_shape=jax.ShapeDtypeStruct((pairs, 4 * M, SPAN), F32),
+        out_shape=jax.ShapeDtypeStruct((chunks, 4 * M, SPAN), F32),
         compiler_params=little,
         name="carries",
     )(got, own_rate, own_res)
     back, got, x3, g3 = lax.optimization_barrier((back, got, signal, out_grad))
-    carried = exchange(back)
+    carried = lax.all_to_all(back, "seq", 0, 0, tiled=True).reshape(pairs, 2, 4 * M, SPAN)
     sums = pl.pallas_call(
         functools.partial(sums_kernel, pairs, 1.0 / (rows * chunks * SPAN)),
         out_shape=jax.ShapeDtypeStruct((3 * M, SPAN), F32),
@@ -421,18 +425,17 @@
         total = refs[0][...]
         for ref in refs[1:-1]:
             total = total + ref[...]
-        for k in range(pairs):
+        for k in range(chunks):
             refs[-1][k] = total
 
     total = pl.pallas_call(
         total_kernel,
-        out_shape=jax.ShapeDtypeStruct((pairs, 3 * M, SPAN), F32),
+        out_shape=jax.ShapeDtypeStruct((chunks, 3 * M, SPAN), F32),
         compiler_params=little,
         name="total",
     )(sums, *arriving)
     carried, total, mixed_part, grad_part = lax.optimization_barrier((carried, total, mixed_part, grad_part))
-    carried_far = other_core(carried)
-    everyone = exchange(total)
+    everyone = lax.all_to_all(total, "seq", 0, 0, tiled=True)
 
     flat_block = pl.BlockSpec((SPAN, wide), lambda i, at: (0, i))
     seq_block = pl.BlockSpec((1, SPAN, wide), lambda i, at: (0, 0, i))
@@ -448,8 +451,7 @@
                 pl.BlockSpec((block, M, SPAN), lambda i, at: (i, 0, 0)),
                 pl.BlockSpec((M, wide // GROUP), lambda i, at: (0, i)),
                 pl.BlockSpec((M, wide), lambda i, at: (0, i)),
-                half_block,
-                half_block,
+                pl.BlockSpec((block, None, 4 * M, SPAN), lambda i, at: (lax.rem(i, part), i // part, 0, 0)),
                 half_block,
                 half_block,
             ],
@@ -459,15 +461,13 @@
         compiler_params=params,
         cost_estimate=pl.CostEstimate(flops=work * 1600, bytes_accessed=work * 12, transcendentals=work),
         name="add_carries",
-    )(core_scalar, mixed_part, grad_part, rate_rows, log_rates, residues, carried, carried_far, arrived, arrived_far)
-    everyone, mixed, grad_signal = lax.optimization_barrier((everyone, mixed, grad_signal))
+    )(core_scalar, mixed_part, grad_part, rate_rows, log_rates, residues, carried, arrived, arrived_far)
     grad_residues, grad_rates = pl.pallas_call(
         functools.partial(gather_kernel, pairs),
         out_shape=[jax.ShapeDtypeStruct(residues.shape, F32), jax.ShapeDtypeStruct(log_rates.shape, F32)],
-        in_specs=[smem, vmem, vmem, vmem],
         compiler_params=little,
         name="unpack",
-    )(core_scalar, everyone, other_core(everyone), log_rates)
+    )(everyone, log_rates)
     return mixed, grad_signal, grad_residues, grad_rates
 
 

time: 78 us -> 79.1 us (1.014)
  waiting for transfers between devices: 2.9 us -> 4.22 us
  Pallas kernels: 43.7 us -> 42.8 us
    all_to_all x0 -> x2, starting transfers between devices: none -> 14.5 us  [the longest x1 8.22 us: local(): everyone = lax.all_to_all(total, 'seq', 0, 0, tiled=True)]
    all_to_all x3 -> x1, starting transfers between devices: 19.7 us -> 7.85 us  [exchange(): lax.all_to_all(values, 'seq', 0, 0, axis_index_groups=same_core, tiled=True)]
    all_to_all x0 -> x2, waiting for transfers between devices: none -> 2.5 us  [the longest x1 2.5 us: local(): everyone = lax.all_to_all(total, 'seq', 0, 0, tiled=True)]
    ppermute x4 -> x2, starting transfers between devices: 4 us -> 1.54 us  [other_core(): return lax.ppermute(values, 'seq', swap)]
    ppermute x4 -> x2, waiting for transfers between devices: 1.15 us -> 0.01 us  [other_core(): return lax.ppermute(values, 'seq', swap)]
    pallas_call x1, Pallas kernels: 3.17 us -> 2.17 us  [local(): pl.pallas_call(pair_kernel, grid_spec=pltpu.PrefetchScalarGridSpec(num_sc...]
    all_to_all x3 -> x1, waiting for transfers between devices: 1.73 us -> 1.7 us  [exchange(): lax.all_to_all(values, 'seq', 0, 0, axis_index_groups=same_core, tiled=True)]
  transfers between devices with their start and end apart: 10 -> 8, of which waited for: 2 -> 2; matrix products, arithmetic and copies ran while one was open for 2% -> 2% of each run, Pallas kernels for 42% -> 41%
where the time goes in v5:
time: 79.1 us; the launch traced here: 78.4 us
  Pallas kernels  42.8 us (54%)
  starting transfers between devices  27.6 us (35%)
  waiting for transfers between devices  4.22 us (5%)
  local copies, waits for them, and re-layouts  2.99 us (4%)
  between operations  0.81 us (1%)
    pallas_call x2, Pallas kernels, convolutions(): pl.pallas_call(second_kernel, grid=(part,), in_specs=kernel_blocks + [pl....  16.8 us
    pallas_call x2, Pallas kernels, ends_and_lags(): pl.pallas_call(first_kernel, grid_spec=pltpu.PrefetchScalarGridSpec(num_s...  13.5 us
    all_to_all x1, starting transfers between devices, local(): everyone = lax.all_to_all(total, 'seq', 0, 0, tiled=True)  8.22 us
    all_to_all x1, starting transfers between devices, exchange(): lax.all_to_all(values, 'seq', 0, 0, axis_index_groups=same_core, tiled=True)  7.85 us
    pallas_call x1, Pallas kernels, local(): pl.pallas_call(last_kernel, grid_spec=pltpu.PrefetchScalarGridSpec(num_sc...  7.78 us
    all_to_all x1, starting transfers between devices, local(): lax.all_to_all(back, 'seq', 0, 0, tiled=True).reshape(pairs, 2, 4 * M, SPAN)  6.27 us
    ppermute x3, starting transfers between devices, local(): lax.ppermute(sums, 'batch', [(i, (i + k) % rows) for i in range(rows)])  3.67 us
    all_to_all x1, waiting for transfers between devices, local(): everyone = lax.all_to_all(total, 'seq', 0, 0, tiled=True)  2.5 us
  transfers between devices with their start and end apart: 8, of which 2 were waited for; matrix products, arithmetic and copies ran while one was open for 2% of the time, Pallas kernels for 41%

profile of v5, /device:TPU:1, one launch (start us, length us, event | category | flops | bytes accessed | tf_op | source)
XLA Modules:
  0.0 78.4 jit_solution(4498788798007332274)
XLA Ops:
  0.6 0.0 copy-start
  0.6 6.8 %ends_and_lags.2 = (f32[16,88,128]{2,1,0:T(8,128)}, f32[16,16,128]{2,1,0:T(8,128)}) custom-call(s32[1]{0:T(128)S(6)} %sub.7.half_ref, bf16[1,128,8192]{2,1,0:T(8,128)(2,1)} %x_ref.5, bf16[1,128,8192]{2,1,0:T(8,128)(2,1)} %g_ref.5, f32[8,512]{1,0:T(8,128)} %log_ref.7, f32[8,8192]{1,0:T(8,128)} %res_ref.11, bf16[256,256]{1,0:T(8,128)(2,1)} %constant.35.clone.fwd_ref, ...), custom_call_target="tpu_custom_call" | custom-call | tf_op jit(solution)/shard_map/ends_and_lags/pallas_call | solution.py:325
  7.4 0.0 copy-start.2
  7.4 1.5 %collective-permute-start = (f32[16,88,128]{2,1,0:T(8,128)}, f32[16,88,128]{2,1,0:T(8,128)S(1)}, u32[]{:S(2)}, u32[]{:S(2)}) collective-permute-start(f32[16,88,128]{2,1,0:T(8,128)} %get-tuple-element.38), channel_id=1, source_target_pairs={{0,4},{4,0},{8,12},{12,8},{16,20},{20,16},{24,28},{28,24},{32,36},... | collective-permute-start | bytes 2162696 | tf_op jit(solution)/shard_map/ppermute | solution.py:322
  8.9 6.7 %ends_and_lags.3 = (f32[16,88,128]{2,1,0:T(8,128)}, f32[16,16,128]{2,1,0:T(8,128)}) custom-call(s32[1]{0:T(128)} %bitcast.half_ref.core_ref, bf16[1,128,8192]{2,1,0:T(8,128)(2,1)} %x_ref.5, bf16[1,128,8192]{2,1,0:T(8,128)(2,1)} %g_ref.5, f32[8,512]{1,0:T(8,128)} %log_ref.7, f32[8,8192]{1,0:T(8,128)} %res_ref.11, bf16[256,256]{1,0:T(8,128)(2,1)} %constant.35.clone.fwd_ref, ...), custom_call_target="tpu_custom_call" | custom-call | tf_op jit(solution)/shard_map/ends_and_lags/pallas_call | solution.py:325
  15.6 0.0 collective-permute-done.arrived_ref.near_ref
  15.6 0.0 copy-start.1
  15.6 0.0 copy-done
  15.6 0.0 copy-start.4
  15.7 1.1 %copy-done.4 = f32[16,16,128]{2,1,0:T(8,128)S(1)} copy-done((f32[16,16,128]{2,1,0:T(8,128)S(1)}, f32[16,16,128]{2,1,0:T(8,128)}, u32[]{:S(2)}) %copy-start.4) | copy-done | bytes 131096
  16.7 2.2 %join_pair.1 = f32[16,88,128]{2,1,0:T(8,128)} custom-call(s32[1]{0:T(128)} %bitcast.half_ref.core_ref, f32[16,88,128]{2,1,0:T(8,128)} %get-tuple-element.44.kept_ref, f32[16,88,128]{2,1,0:T(8,128)S(1)} %collective-permute-done.arrived_ref.near_ref, f32[16,16,128]{2,1,0:T(8,128)S(1)} %copy-done.4, f32[8,8192]{1,0:T(8,128)S(1)} %copy-done), custom_call_target="tpu_custom_call" | custom-call | tf_op jit(solution)/shard_map/join_pair/pallas_call | solution.py:353
  18.9 0.0 collective-permute-start.1
  18.9 7.9 %all-to-all-start = ((f32[16,88,128]{2,1,0:T(8,128)}), f32[16,88,128]{2,1,0:T(8,128)S(1)}, u32[]{:S(2)}, u32[]{:S(2)}) async-start(f32[16,88,128]{2,1,0:T(8,128)} %join_pair.1), calls=%async_computation | async-start | bytes 1441792 | tf_op jit(solution)/shard_map/all_to_all | solution.py:319
  26.8 0.0 copy-done.2
  26.8 0.1 constant_dynamic-slice_fusion.1
  26.9 0.1 broadcast_in_dim.19
  27.0 0.1 reshape.16.rate_ref
  27.1 0.1 copy.12
  27.2 0.2 broadcast_in_dim.17
  27.4 0.7 broadcast_in_dim.18.rate_ref
  28.0 8.4 %local_convolutions.2 = (f32[128,8192]{1,0:T(8,128)}, f32[128,8192]{1,0:T(8,128)}) custom-call(bf16[1,128,8192]{2,1,0:T(8,128)(2,1)} %x_ref.5, bf16[1,128,8192]{2,1,0:T(8,128)(2,1)} %g_ref.5, f32[32,8,128]{2,1,0:T(8,128)} %broadcast_in_dim.18.rate_ref, f32[8,8192]{1,0:T(8,128)} %res_ref.11, bf16[256,256]{1,0:T(8,128)(2,1)} %constant.35.clone.fwd_ref, ...), custom_call_target="tpu_custom_call" | custom-call | flops 314572800 | bytes 2097152 | tf_op jit(solution)/shard_map/local_convolutions/pallas_call | solution.py:391
  36.5 0.0 copy-done.1
  36.5 0.7 constant_dynamic-slice_fusion.res_ref
  37.2 1.7 %all-to-all-done.got_ref = f32[16,88,128]{2,1,0:T(8,128)S(1)} async-done(((f32[16,88,128]{2,1,0:T(8,128)}), f32[16,88,128]{2,1,0:T(8,128)S(1)}, u32[]{:S(2)}, u32[]{:S(2)}) %all-to-all-start) | async-done | bytes 720928 | tf_op jit(solution)/shard_map/all_to_all | solution.py:319
  38.9 0.0 collective-permute-done.1.far_ref
  38.9 0.0 copy-start.6
  38.9 0.9 %carries.1 = f32[32,32,128]{2,1,0:T(8,128)} custom-call(f32[16,88,128]{2,1,0:T(8,128)S(1)} %all-to-all-done.got_ref, f32[8,256]{1,0:T(8,128)S(1)} %reshape.16.rate_ref, f32[8,256]{1,0:T(8,128)S(1)} %constant_dynamic-slice_fusion.res_ref), custom_call_target="tpu_custom_call" | custom-call | tf_op jit(solution)/shard_map/carries/pallas_call | solution.py:405
  39.8 6.3 %all-to-all-start.1 = ((f32[32,32,128]{2,1,0:T(8,128)}), f32[32,32,128]{2,1,0:T(8,128)S(1)}, u32[]{:S(2)}, u32[]{:S(2)}) async-start(f32[32,32,128]{2,1,0:T(8,128)} %carries.1), calls=%async_computation.1 | async-start | bytes 1048576 | tf_op jit(solution)/shard_map/all_to_all | solution.py:412
  46.1 0.2 gradient_sums.1.refs_0_
  46.2 0.0 copy-done.6
  46.2 2.5 %collective-permute-start.4 = (f32[24,128]{1,0:T(8,128)S(1)}, f32[24,128]{1,0:T(8,128)S(1)}, u32[]{:S(2)}, u32[]{:S(2)}) collective-permute-start(f32[24,128]{1,0:T(8,128)S(1)} %gradient_sums.1.refs_0_), channel_id=1, source_target_pairs={{0,3},{1,0},{2,1},{3,2},{4,7},{5,4},{6,5},{7,6},{8,11},{9,8},{10,9... | collective-permute-start | bytes 36872 | tf_op jit(solution)/shard_map/ppermute | solution.py:421
  48.8 0.5 collective-permute-start.3
  49.3 0.6 collective-permute-start.2
  49.9 8.4 %local_convolutions.3 = (f32[128,8192]{1,0:T(8,128)}, f32[128,8192]{1,0:T(8,128)}) custom-call(bf16[1,128,8192]{2,1,0:T(8,128)(2,1)} %x_ref.5, bf16[1,128,8192]{2,1,0:T(8,128)(2,1)} %g_ref.5, f32[32,8,128]{2,1,0:T(8,128)} %broadcast_in_dim.18.rate_ref, f32[8,8192]{1,0:T(8,128)} %res_ref.11, ...), custom_call_target="tpu_custom_call", output_to_operand_aliasing={{0}: (6, {}), {1}: (7, {})} | custom-call | flops 314572800 | bytes 2097152 | tf_op jit(solution)/shard_map/local_convolutions/pallas_call | solution.py:391
  58.3 0.0 collective-permute-done.4.refs_3_
  58.3 0.0 collective-permute-done.3.refs_2_
  58.4 0.0 collective-permute-done.2.refs_1_
  58.4 0.8 %total.1 = f32[32,24,128]{2,1,0:T(8,128)} custom-call(f32[24,128]{1,0:T(8,128)S(1)} %gradient_sums.1.refs_0_, f32[24,128]{1,0:T(8,128)S(1)} %collective-permute-done.2.refs_1_, f32[24,128]{1,0:T(8,128)S(1)} %collective-permute-done.3.refs_2_, f32[24,128]{1,0:T(8,128)S(1)} %collective-permute-done.4.refs_3_), custom_call_target="tpu_custom_call" | custom-call | tf_op jit(solution)/shard_map/total/pallas_call | solution.py:431
  59.2 0.0 all-to-all-done.1
  59.2 0.0 copy-start.5
  59.2 8.2 %all-to-all-start.2 = ((f32[32,24,128]{2,1,0:T(8,128)}), f32[32,24,128]{2,1,0:T(8,128)S(1)}, u32[]{:S(2)}, u32[]{:S(2)}) async-start(f32[32,24,128]{2,1,0:T(8,128)} %total.1), calls=%async_computation.2 | async-start | bytes 786432 | tf_op jit(solution)/shard_map/all_to_all | solution.py:438
  67.4 0.0 copy-done.5
  67.4 0.0 copy-start.3
  67.4 7.8 %add_carries.1 = (bf16[1,128,8192]{2,1,0:T(8,128)(2,1)}, bf16[1,128,8192]{2,1,0:T(8,128)(2,1)}) custom-call(s32[1]{0:T(128)} %bitcast.half_ref.core_ref, f32[128,8192]{1,0:T(8,128)} %get-tuple-element.55.mixed_ref, f32[128,8192]{1,0:T(8,128)} %get-tuple-element.56.grad_ref, f32[32,8,128]{2,1,0:T(8,128)} %broadcast_in_dim.18.rate_ref, f32[8,512]{1,0:T(8,128)} %log_ref.7, ...), custom_call_target="tpu_custom_call" | custom-call | flops 1677721600 | bytes 12582912 | tf_op jit(solution)/shard_map/add_carries/pallas_call | solution.py:443
  75.2 2.5 %all-to-all-done.2.all_ref = f32[32,24,128]{2,1,0:T(8,128)S(1)} async-done(((f32[32,24,128]{2,1,0:T(8,128)}), f32[32,24,128]{2,1,0:T(8,128)S(1)}, u32[]{:S(2)}, u32[]{:S(2)}) %all-to-all-start.2) | async-done | bytes 393248 | tf_op jit(solution)/shard_map/all_to_all | solution.py:438
  77.7 0.0 copy-done.3
  77.7 0.7 unpack.1
  (1 shorter events, 0.0 us)
Async XLA Ops:
  0.6 15.0 %copy-start = (f32[8,8192]{1,0:T(8,128)S(1)}, f32[8,8192]{1,0:T(8,128)}, u32[]{:S(2)}) copy-start(f32[8,8192]{1,0:T(8,128)} %res_ref.11) | copy-start | bytes 786436
  7.4 19.4 %copy-start.2 = (f32[8,512]{1,0:T(8,128)S(1)}, f32[8,512]{1,0:T(8,128)}, u32[]{:S(2)}) copy-start(f32[8,512]{1,0:T(8,128)} %log_ref.7) | copy-start | bytes 49156
  7.4 8.2 %collective-permute-start = (f32[16,88,128]{2,1,0:T(8,128)}, f32[16,88,128]{2,1,0:T(8,128)S(1)}, u32[]{:S(2)}, u32[]{:S(2)}) collective-permute-start(f32[16,88,128]{2,1,0:T(8,128)} %get-tuple-element.38), channel_id=1, source_target_pairs={{0,4},{4,0},{8,12},{12,8},{16,20},{20,16},{24,28},{28,24},{32,36},... | collective-permute-start | bytes 2162696 | tf_op jit(solution)/shard_map/ppermute | solution.py:322
  15.6 20.8 %copy-start.1 = (f32[16,88,128]{2,1,0:T(8,128)}, f32[16,88,128]{2,1,0:T(8,128)S(1)}, u32[]{:S(2)}) copy-start(f32[16,88,128]{2,1,0:T(8,128)S(1)} %collective-permute-done.arrived_ref.near_ref) | copy-start | bytes 2162692
  15.6 1.1 %copy-start.4 = (f32[16,16,128]{2,1,0:T(8,128)S(1)}, f32[16,16,128]{2,1,0:T(8,128)}, u32[]{:S(2)}) copy-start(f32[16,16,128]{2,1,0:T(8,128)} %get-tuple-element.39.rate_ref) | copy-start | bytes 393220
  18.9 20.0 %collective-permute-start.1 = (f32[16,88,128]{2,1,0:T(8,128)}, f32[16,88,128]{2,1,0:T(8,128)S(1)}, u32[]{:S(2)}, u32[]{:S(2)}) collective-permute-start(f32[16,88,128]{2,1,0:T(8,128)} %get-tuple-element.44.kept_ref), channel_id=1, source_target_pairs={{0,4},{4,0},{8,12},{12,8},{16,20},{20,16},{24,28},{28,24},{32,36},... | collective-permute-start | bytes 2162696 | tf_op jit(solution)/shard_map/ppermute | solution.py:322
  18.9 19.9 %all-to-all-start = ((f32[16,88,128]{2,1,0:T(8,128)}), f32[16,88,128]{2,1,0:T(8,128)S(1)}, u32[]{:S(2)}, u32[]{:S(2)}) async-start(f32[16,88,128]{2,1,0:T(8,128)} %join_pair.1), calls=%async_computation | async-start | bytes 1441792 | tf_op jit(solution)/shard_map/all_to_all | solution.py:319
  38.9 7.4 %copy-start.6 = (f32[16,88,128]{2,1,0:T(8,128)}, f32[16,88,128]{2,1,0:T(8,128)S(1)}, u32[]{:S(2)}) copy-start(f32[16,88,128]{2,1,0:T(8,128)S(1)} %collective-permute-done.1.far_ref) | copy-start | bytes 2162692
  39.8 19.4 %all-to-all-start.1 = ((f32[32,32,128]{2,1,0:T(8,128)}), f32[32,32,128]{2,1,0:T(8,128)S(1)}, u32[]{:S(2)}, u32[]{:S(2)}) async-start(f32[32,32,128]{2,1,0:T(8,128)} %carries.1), calls=%async_computation.1 | async-start | bytes 1048576 | tf_op jit(solution)/shard_map/all_to_all | solution.py:412
  46.2 12.1 %collective-permute-start.4 = (f32[24,128]{1,0:T(8,128)S(1)}, f32[24,128]{1,0:T(8,128)S(1)}, u32[]{:S(2)}, u32[]{:S(2)}) collective-permute-start(f32[24,128]{1,0:T(8,128)S(1)} %gradient_sums.1.refs_0_), channel_id=1, source_target_pairs={{0,3},{1,0},{2,1},{3,2},{4,7},{5,4},{6,5},{7,6},{8,11},{9,8},{10,9... | collective-permute-start | bytes 36872 | tf_op jit(solution)/shard_map/ppermute | solution.py:421
  48.8 9.6 %collective-permute-start.3 = (f32[24,128]{1,0:T(8,128)S(1)}, f32[24,128]{1,0:T(8,128)S(1)}, u32[]{:S(2)}, u32[]{:S(2)}) collective-permute-start(f32[24,128]{1,0:T(8,128)S(1)} %gradient_sums.1.refs_0_), channel_id=1, source_target_pairs={{0,2},{1,3},{2,0},{3,1},{4,6},{5,7},{6,4},{7,5},{8,10},{9,11},{10,... | collective-permute-start | bytes 36872 | tf_op jit(solution)/shard_map/ppermute | solution.py:421
  49.3 9.0 %collective-permute-start.2 = (f32[24,128]{1,0:T(8,128)S(1)}, f32[24,128]{1,0:T(8,128)S(1)}, u32[]{:S(2)}, u32[]{:S(2)}) collective-permute-start(f32[24,128]{1,0:T(8,128)S(1)} %gradient_sums.1.refs_0_), channel_id=1, source_target_pairs={{0,1},{1,2},{2,3},{3,0},{4,5},{5,6},{6,7},{7,4},{8,9},{9,10},{10,1... | collective-permute-start | bytes 36872 | tf_op jit(solution)/shard_map/ppermute | solution.py:421
  59.2 8.2 %copy-start.5 = (f32[32,32,128]{2,1,0:T(8,128)}, f32[32,32,128]{2,1,0:T(8,128)S(1)}, u32[]{:S(2)}) copy-start(f32[32,32,128]{2,1,0:T(8,128)S(1)} %all-to-all-done.1) | copy-start | bytes 1572868
  59.2 18.5 %all-to-all-start.2 = ((f32[32,24,128]{2,1,0:T(8,128)}), f32[32,24,128]{2,1,0:T(8,128)S(1)}, u32[]{:S(2)}, u32[]{:S(2)}) async-start(f32[32,24,128]{2,1,0:T(8,128)} %total.1), calls=%async_computation.2 | async-start | bytes 786432 | tf_op jit(solution)/shard_map/all_to_all | solution.py:438
  67.4 10.3 %copy-start.3 = (f32[8,512]{1,0:T(8,128)S(1)}, f32[8,512]{1,0:T(8,128)}, u32[]{:S(2)}) copy-start(f32[8,512]{1,0:T(8,128)} %log_ref.7) | copy-start | bytes 49156

commit v6 on v3

--- a/solution.py
+++ b/solution.py
@@ -281,10 +281,21 @@
         compiler_params=pltpu.CompilerParams(vmem_limit_bytes=8 * 2**20),
         name="gradient_sums",
     )(index.astype(jnp.int32)[None], got, own_rate, own_res)
-    total = sums
-    for k in range(1, rows):
-        total = total + lax.ppermute(sums, "batch", [(i, (i + k) % rows) for i in range(rows)])
-    total = jnp.broadcast_to(total[None], (chunks, 3 * M, SPAN))
+    arriving = [lax.ppermute(sums, "batch", [(i, (i + k) % rows) for i in range(rows)]) for k in range(1, rows)]
+
+    def total_kernel(*refs):
+        total = refs[0][...]
+        for ref in refs[1:-1]:
+            total = total + ref[...]
+        for k in range(chunks):
+            refs[-1][k] = total
+
+    total = pl.pallas_call(
+        total_kernel,
+        out_shape=jax.ShapeDtypeStruct((chunks, 3 * M, SPAN), F32),
+        compiler_params=pltpu.CompilerParams(vmem_limit_bytes=8 * 2**20),
+        name="total",
+    )(sums, *arriving)
     carried, total = lax.optimization_barrier((carried, total))
     everyone = lax.all_to_all(total, "seq", 0, 0, tiled=True)
 

time: 76.5 us -> 76.4 us (level)
  local copies, waits for them, and re-layouts: 2.75 us -> 1.91 us
  waiting for transfers between devices: 15.9 us -> 15.1 us
  Pallas kernels: 34.5 us -> 35.3 us
    broadcast_in_dim x1 -> x0, local copies, waits for them, and re-layouts: 0.85 us -> none  [local(): total = jnp.broadcast_to(total[None], (chunks, 3 * M, SPAN))]
    pallas_call x0 -> x1, Pallas kernels: none -> 0.81 us  [local(): pl.pallas_call(total_kernel, out_shape=jax.ShapeDtypeStruct((chunks, 3 *...]
    all_to_all x1, waiting for transfers between devices: 4.4 us -> 3.59 us  [local(): carried = lax.all_to_all(back, 'seq', 0, 0, tiled=True)]
    all_to_all x1, starting transfers between devices: 4.53 us -> 5.32 us  [local(): everyone = lax.all_to_all(total, 'seq', 0, 0, tiled=True)]
  transfers between devices with their start and end apart: 6 -> 6, of which waited for: 5 -> 5; matrix products, arithmetic and copies ran while one was open for 3% -> 3% of each run, Pallas kernels for 29% -> 30%
where the time goes in v6:
time: 76.4 us; the launch traced here: 75.8 us
  Pallas kernels  35.3 us (46%)
  starting transfers between devices  22.7 us (30%)
  waiting for transfers between devices  15.1 us (20%)
  local copies, waits for them, and re-layouts  1.91 us (2%)
    pallas_call x1, Pallas kernels, local(): pl.pallas_call(second_kernel, grid=(steps,), in_specs=[seq_block, seq_blo...  14.4 us
    pallas_call x1, Pallas kernels, local(): pl.pallas_call(first_kernel, grid=(steps,), in_specs=[seq_block, seq_bloc...  11.2 us
    all_to_all x1, starting transfers between devices, local(): got = lax.all_to_all(send, 'seq', 0, 0, tiled=True)  9.73 us
    pallas_call x1, Pallas kernels, local(): pl.pallas_call(last_kernel, grid=(steps,), in_specs=[flat_block, flat_blo...  7.1 us
    all_to_all x1, starting transfers between devices, local(): everyone = lax.all_to_all(total, 'seq', 0, 0, tiled=True)  5.32 us
    all_to_all x1, waiting for transfers between devices, local(): got = lax.all_to_all(send, 'seq', 0, 0, tiled=True)  4.9 us
    all_to_all x1, starting transfers between devices, local(): carried = lax.all_to_all(back, 'seq', 0, 0, tiled=True)  4.08 us
    ppermute x3, starting transfers between devices, local(): lax.ppermute(sums, 'batch', [(i, (i + k) % rows) for i in range(rows)])  3.61 us
  transfers between devices with their start and end apart: 6, of which 5 were waited for; matrix products, arithmetic and copies ran while one was open for 3% of the time, Pallas kernels for 30%

profile of v6, /device:TPU:1, one launch (start us, length us, event | category | flops | bytes accessed | tf_op | source)
XLA Modules:
  0.0 75.8 jit_solution(14181453401598139984)
XLA Ops:
  0.6 11.2 %ends_and_lags.1 = f32[32,88,128]{2,1,0:T(8,128)} custom-call(bf16[1,128,8192]{2,1,0:T(8,128)(2,1)} %x_ref.3, bf16[1,128,8192]{2,1,0:T(8,128)(2,1)} %g_ref.3, f32[8,512]{1,0:T(8,128)} %log_ref.3, f32[8,8192]{1,0:T(8,128)} %res_ref.3, bf16[256,256]{1,0:T(8,128)(2,1)} %constant.20.clone.fwd_ref, bf16[128,768]{1,0:T(8,128)(2,1)} %constant.21.clone.inv_ref), custom_call_target="tpu_custom_call" | custom-call | tf_op jit(solution)/shard_map/ends_and_lags/pallas_call | solution.py:239
  11.8 0.0 copy-start
  11.8 9.7 %all-to-all-start = ((f32[32,88,128]{2,1,0:T(8,128)}), f32[32,88,128]{2,1,0:T(8,128)S(1)}, u32[]{:S(2)}, u32[]{:S(2)}) async-start(f32[32,88,128]{2,1,0:T(8,128)} %ends_and_lags.1), calls=%async_computation | async-start | bytes 2883584 | tf_op jit(solution)/shard_map/all_to_all | solution.py:254
  21.6 0.0 copy-done
  21.6 0.1 constant_dynamic-slice_fusion.1
  21.7 0.1 broadcast_in_dim.15
  21.7 0.1 reshape.13.rate_ref
  21.8 0.1 copy.10
  22.0 0.2 broadcast_in_dim.13
  22.1 0.7 constant_dynamic-slice_fusion.res_ref
  22.8 0.7 broadcast_in_dim.14.rate_ref
  23.5 14.4 %local_convolutions.1 = (f32[128,8192]{1,0:T(8,128)}, f32[128,8192]{1,0:T(8,128)}) custom-call(bf16[1,128,8192]{2,1,0:T(8,128)(2,1)} %x_ref.3, bf16[1,128,8192]{2,1,0:T(8,128)(2,1)} %g_ref.3, f32[32,8,128]{2,1,0:T(8,128)} %broadcast_in_dim.14.rate_ref, f32[8,8192]{1,0:T(8,128)} %res_ref.3, bf16[256,256]{1,0:T(8,128)(2,1)} %constant.20.clone.fwd_ref, ...), custom_call_target="tpu_custom_call" | custom-call | flops 6291456000 | bytes 16777216 | tf_op jit(solution)/shard_map/local_convolutions/pallas_call | solution.py:256
  37.9 4.9 %all-to-all-done.got_ref = f32[32,88,128]{2,1,0:T(8,128)S(1)} async-done(((f32[32,88,128]{2,1,0:T(8,128)}), f32[32,88,128]{2,1,0:T(8,128)S(1)}, u32[]{:S(2)}, u32[]{:S(2)}) %all-to-all-start) | async-done | bytes 1441824 | tf_op jit(solution)/shard_map/all_to_all | solution.py:254
  42.8 0.9 %carries.1 = f32[32,32,128]{2,1,0:T(8,128)} custom-call(f32[32,88,128]{2,1,0:T(8,128)S(1)} %all-to-all-done.got_ref, f32[8,256]{1,0:T(8,128)S(1)} %reshape.13.rate_ref, f32[8,256]{1,0:T(8,128)S(1)} %constant_dynamic-slice_fusion.res_ref), custom_call_target="tpu_custom_call" | custom-call | tf_op jit(solution)/shard_map/carries/pallas_call | solution.py:269
  43.7 4.1 %all-to-all-start.1 = ((f32[32,32,128]{2,1,0:T(8,128)}), f32[32,32,128]{2,1,0:T(8,128)S(1)}, u32[]{:S(2)}, u32[]{:S(2)}) async-start(f32[32,32,128]{2,1,0:T(8,128)} %carries.1), calls=%async_computation.1 | async-start | bytes 1048576 | tf_op jit(solution)/shard_map/all_to_all | solution.py:276
  47.7 0.3 gradient_sums.1.refs_0_
  48.0 2.5 %collective-permute-start.2 = (f32[24,128]{1,0:T(8,128)S(1)}, f32[24,128]{1,0:T(8,128)S(1)}, u32[]{:S(2)}, u32[]{:S(2)}) collective-permute-start(f32[24,128]{1,0:T(8,128)S(1)} %gradient_sums.1.refs_0_), channel_id=1, source_target_pairs={{0,3},{1,0},{2,1},{3,2},{4,7},{5,4},{6,5},{7,6},{8,11},{9,8},{10,9... | collective-permute-start | bytes 36872 | tf_op jit(solution)/shard_map/ppermute | solution.py:284
  50.5 0.5 collective-permute-start.1
  51.0 0.6 collective-permute-start
  51.6 0.0 collective-permute-done.2.refs_3_
  51.6 3.2 %collective-permute-done.1.refs_2_ = f32[24,128]{1,0:T(8,128)S(1)} collective-permute-done((f32[24,128]{1,0:T(8,128)S(1)}, f32[24,128]{1,0:T(8,128)S(1)}, u32[]{:S(2)}, u32[]{:S(2)}) %collective-permute-start.1) | collective-permute-done | bytes 12320 | tf_op jit(solution)/shard_map/ppermute | solution.py:284
  54.8 0.2 collective-permute-done.refs_1_
  55.1 0.8 %total.1 = f32[32,24,128]{2,1,0:T(8,128)} custom-call(f32[24,128]{1,0:T(8,128)S(1)} %gradient_sums.1.refs_0_, f32[24,128]{1,0:T(8,128)S(1)} %collective-permute-done.refs_1_, f32[24,128]{1,0:T(8,128)S(1)} %collective-permute-done.1.refs_2_, f32[24,128]{1,0:T(8,128)S(1)} %collective-permute-done.2.refs_3_), custom_call_target="tpu_custom_call" | custom-call | tf_op jit(solution)/shard_map/total/pallas_call | solution.py:293
  55.9 3.6 %all-to-all-done.1.got_ref = f32[32,32,128]{2,1,0:T(8,128)S(1)} async-done(((f32[32,32,128]{2,1,0:T(8,128)}), f32[32,32,128]{2,1,0:T(8,128)S(1)}, u32[]{:S(2)}, u32[]{:S(2)}) %all-to-all-start.1) | async-done | bytes 524320 | tf_op jit(solution)/shard_map/all_to_all | solution.py:276
  59.5 0.0 copy-start.1
  59.5 5.3 %all-to-all-start.2 = ((f32[32,24,128]{2,1,0:T(8,128)}), f32[32,24,128]{2,1,0:T(8,128)S(1)}, u32[]{:S(2)}, u32[]{:S(2)}) async-start(f32[32,24,128]{2,1,0:T(8,128)} %total.1), calls=%async_computation.2 | async-start | bytes 786432 | tf_op jit(solution)/shard_map/all_to_all | solution.py:300
  64.8 0.0 copy-done.1
  64.8 7.1 %add_carries.1 = (bf16[1,128,8192]{2,1,0:T(8,128)(2,1)}, bf16[1,128,8192]{2,1,0:T(8,128)(2,1)}) custom-call(f32[128,8192]{1,0:T(8,128)} %get-tuple-element.24.mixed_ref, f32[128,8192]{1,0:T(8,128)} %get-tuple-element.25.grad_ref, f32[32,8,128]{2,1,0:T(8,128)} %broadcast_in_dim.14.rate_ref, f32[32,32,128]{2,1,0:T(8,128)} %copy-done.1), custom_call_target="tpu_custom_call" | custom-call | flops 1677721600 | bytes 12582912 | tf_op jit(solution)/shard_map/add_carries/pallas_call | solution.py:302
  71.9 3.2 %all-to-all-done.2.all_ref = f32[32,24,128]{2,1,0:T(8,128)S(1)} async-done(((f32[32,24,128]{2,1,0:T(8,128)}), f32[32,24,128]{2,1,0:T(8,128)S(1)}, u32[]{:S(2)}, u32[]{:S(2)}) %all-to-all-start.2) | async-done | bytes 393248 | tf_op jit(solution)/shard_map/all_to_all | solution.py:300
  75.1 0.7 unpack.1
  (1 shorter events, 0.0 us)
Async XLA Ops:
  11.8 9.7 %copy-start = (f32[8,512]{1,0:T(8,128)S(1)}, f32[8,512]{1,0:T(8,128)}, u32[]{:S(2)}) copy-start(f32[8,512]{1,0:T(8,128)} %log_ref.3) | copy-start | bytes 49156
  11.8 31.0 %all-to-all-start = ((f32[32,88,128]{2,1,0:T(8,128)}), f32[32,88,128]{2,1,0:T(8,128)S(1)}, u32[]{:S(2)}, u32[]{:S(2)}) async-start(f32[32,88,128]{2,1,0:T(8,128)} %ends_and_lags.1), calls=%async_computation | async-start | bytes 2883584 | tf_op jit(solution)/shard_map/all_to_all | solution.py:254
  43.7 15.8 %all-to-all-start.1 = ((f32[32,32,128]{2,1,0:T(8,128)}), f32[32,32,128]{2,1,0:T(8,128)S(1)}, u32[]{:S(2)}, u32[]{:S(2)}) async-start(f32[32,32,128]{2,1,0:T(8,128)} %carries.1), calls=%async_computation.1 | async-start | bytes 1048576 | tf_op jit(solution)/shard_map/all_to_all | solution.py:276
  48.0 3.6 %collective-permute-start.2 = (f32[24,128]{1,0:T(8,128)S(1)}, f32[24,128]{1,0:T(8,128)S(1)}, u32[]{:S(2)}, u32[]{:S(2)}) collective-permute-start(f32[24,128]{1,0:T(8,128)S(1)} %gradient_sums.1.refs_0_), channel_id=1, source_target_pairs={{0,3},{1,0},{2,1},{3,2},{4,7},{5,4},{6,5},{7,6},{8,11},{9,8},{10,9... | collective-permute-start | bytes 36872 | tf_op jit(solution)/shard_map/ppermute | solution.py:284
  50.5 4.3 %collective-permute-start.1 = (f32[24,128]{1,0:T(8,128)S(1)}, f32[24,128]{1,0:T(8,128)S(1)}, u32[]{:S(2)}, u32[]{:S(2)}) collective-permute-start(f32[24,128]{1,0:T(8,128)S(1)} %gradient_sums.1.refs_0_), channel_id=1, source_target_pairs={{0,2},{1,3},{2,0},{3,1},{4,6},{5,7},{6,4},{7,5},{8,10},{9,11},{10,... | collective-permute-start | bytes 36872 | tf_op jit(solution)/shard_map/ppermute | solution.py:284
  51.0 4.1 %collective-permute-start = (f32[24,128]{1,0:T(8,128)S(1)}, f32[24,128]{1,0:T(8,128)S(1)}, u32[]{:S(2)}, u32[]{:S(2)}) collective-permute-start(f32[24,128]{1,0:T(8,128)S(1)} %gradient_sums.1.refs_0_), channel_id=1, source_target_pairs={{0,1},{1,2},{2,3},{3,0},{4,5},{5,6},{6,7},{7,4},{8,9},{9,10},{10,1... | collective-permute-start | bytes 36872 | tf_op jit(solution)/shard_map/ppermute | solution.py:284
  59.5 5.3 %copy-start.1 = (f32[32,32,128]{2,1,0:T(8,128)}, f32[32,32,128]{2,1,0:T(8,128)S(1)}, u32[]{:S(2)}) copy-start(f32[32,32,128]{2,1,0:T(8,128)S(1)} %all-to-all-done.1.got_ref) | copy-start | bytes 1572868
  59.5 15.6 %all-to-all-start.2 = ((f32[32,24,128]{2,1,0:T(8,128)}), f32[32,24,128]{2,1,0:T(8,128)S(1)}, u32[]{:S(2)}, u32[]{:S(2)}) async-start(f32[32,24,128]{2,1,0:T(8,128)} %total.1), calls=%async_computation.2 | async-start | bytes 786432 | tf_op jit(solution)/shard_map/all_to_all | solution.py:300

commit v7 on v5

--- a/solution.py
+++ b/solution.py
@@ -75,7 +75,7 @@
     return jnp.concatenate([high, low, high, low], 1)
 
 
-def first_kernel(half_ref, x_ref, g_ref, log_ref, res_ref, fwd_ref, inv_ref, send_ref, rate_out):
+def first_kernel(half_ref, x_ref, g_ref, log_ref, res_ref, fwd_ref, inv_ref, send_ref):
     x, g = x_ref[0], g_ref[0]
     xx, gg = twice(x), twice(g)
     forward = fwd_ref[...]
@@ -108,7 +108,7 @@
         rates = jnp.concatenate([jnp.broadcast_to(rate[:, k : k + 1], (M, SPAN)) for k in range(at, at + GROUPS)], 0)
         early = jnp.exp(-rates * lag)
         for h in range(2):
-            rate_out[s, h * M : (h + 1) * M, :] = pick(rates[h * half * M : (h + 1) * half * M], 0)
+            send_ref[s, (11 + h) * M : (12 + h) * M, :] = pick(rates[h * half * M : (h + 1) * half * M], 0)
         for h in range(2):
             rows = slice(h * half * M, (h + 1) * half * M)
             cols = slice(s * SLICE + h * SPAN, s * SLICE + (h + 1) * SPAN)
@@ -164,7 +164,7 @@
     return dot(jnp.concatenate([high, low], 1), twice(place))
 
 
-def pair_kernel(core_ref, kept_ref, arrived_ref, rate_ref, res_ref, pair_ref):
+def pair_kernel(core_ref, kept_ref, arrived_ref, res_ref, pair_ref):
     even = core_ref[0] == 0
     count = kept_ref.shape[0]
     weighted = ([], [])
@@ -179,7 +179,7 @@
             def put(q, values):
                 pair_ref[s, (2 * q + h) * M : (2 * q + h + 1) * M, :] = values
 
-            rate = rate_ref[s, h * M : (h + 1) * M, :]
+            rate = kept_ref[s, (11 + h) * M : (12 + h) * M, :]
             p, far = jnp.exp(-rate), jnp.exp(-rate * SPAN)
             (s1, s2), (t1, t2), (u1, u2), (w1, w2), (r1, r2) = (both(q) for q in range(5))
             put(0, far * s1 + s2)
@@ -321,7 +321,7 @@
     def other_core(values):
         return lax.ppermute(values, "seq", swap)
 
-    def ends_and_lags(half, x, g):
+    def ends_and_lags(half, x, g, room):
         return pl.pallas_call(
             first_kernel,
             grid_spec=pltpu.PrefetchScalarGridSpec(
@@ -335,20 +335,17 @@
                     whole(fwd),
                     whole(inv),
                 ],
-                out_specs=[
-                    pl.BlockSpec((block, 11 * M, SPAN), lambda i, at: (i, 0, 0)),
-                    pl.BlockSpec((block, 2 * M, SPAN), lambda i, at: (i, 0, 0)),
-                ],
+                out_specs=pl.BlockSpec((block, 13 * M, SPAN), lambda i, at: (i, 0, 0)),
             ),
-            out_shape=[states_shape, jax.ShapeDtypeStruct((pairs, 2 * M, SPAN), F32)],
-            compiler_params=params,
+            out_shape=jax.ShapeDtypeStruct((pairs, 13 * M, SPAN), F32),
+            compiler_params=room,
             name="ends_and_lags",
         )(half, x, g, log_rates, residues, fwd, inv)
 
-    away, _ = ends_and_lags(1 - core_scalar, signal, out_grad)
+    away = ends_and_lags(1 - core_scalar, signal, out_grad, params)
     away, x2, g2 = lax.optimization_barrier((away, signal, out_grad))
     arrived = other_core(away)
-    kept, channel_rates = ends_and_lags(core_scalar, x2, g2)
+    kept = ends_and_lags(core_scalar, x2, g2, pltpu.CompilerParams(vmem_limit_bytes=40 * 2**20))
     state_block = pl.BlockSpec((block, 11 * M, SPAN), lambda i, at: (i, 0, 0))
     pair = pl.pallas_call(
         pair_kernel,
@@ -356,9 +353,8 @@
             num_scalar_prefetch=1,
             grid=(part,),
             in_specs=[
-                state_block,
-                state_block,
-                pl.BlockSpec((block, 2 * M, SPAN), lambda i, at: (i, 0, 0)),
+                pl.BlockSpec((block, 13 * M, SPAN), lambda i, at: (i, 0, 0)),
+                pl.BlockSpec((block, 11 * M, SPAN), lambda i, at: (i, 0, 0)),
                 pl.BlockSpec((M, wide), lambda i, at: (0, at[0] * part + i)),
             ],
             out_specs=state_block,
@@ -366,10 +362,9 @@
         out_shape=states_shape,
         compiler_params=little,
         name="join_pair",
-    )(core_scalar, kept, arrived, channel_rates, residues)
+    )(core_scalar, kept, arrived, residues)
     pair, later_rates, later_res, kept = lax.optimization_barrier((pair, log_rates, residues, kept))
     got = exchange(pair)
-    arrived_far = other_core(kept)
 
     decay_rate = jnp.exp(later_rates)
     rate_rows = jnp.broadcast_to(decay_rate.T.reshape(chunks, 1, SPAN), (chunks, M, SPAN))
@@ -378,8 +373,7 @@
 
     work = SPAN * channels
 
-    def convolutions(half, x, g, *earlier):
-        at = half * part
+    def convolutions(at, count, x, g, *earlier):
         kernel_blocks = [
             pl.BlockSpec((1, SPAN, wide), lambda i: (0, 0, at + i)),
             pl.BlockSpec((1, SPAN, wide), lambda i: (0, 0, at + i)),
@@ -390,7 +384,7 @@
         ]
         return pl.pallas_call(
             second_kernel,
-            grid=(part,),
+            grid=(count,),
             in_specs=kernel_blocks + [pl.BlockSpec(memory_space=pl.ANY)] * len(earlier),
             out_specs=[pl.BlockSpec((SPAN, wide), lambda i: (0, at + i))] * 2,
             out_shape=[jax.ShapeDtypeStruct((SPAN, channels), F32)] * 2,
@@ -400,15 +394,16 @@
             name="local_convolutions",
         )(x, g, rate_rows, residues, fwd, inv, *earlier)
 
-    mixed_part, grad_part = convolutions(0, signal, out_grad)
-    got, mixed_part, grad_part, arrived_far = lax.optimization_barrier((got, mixed_part, grad_part, arrived_far))
+    early = steps - max(1, steps // 4)
+    mixed_part, grad_part = convolutions(0, early, signal, out_grad)
+    got, mixed_part, grad_part = lax.optimization_barrier((got, mixed_part, grad_part))
     back = pl.pallas_call(
         functools.partial(carry_kernel, pairs),
         out_shape=jax.ShapeDtypeStruct((chunks, 4 * M, SPAN), F32),
         compiler_params=little,
         name="carries",
     )(got, own_rate, own_res)
-    back, got, x3, g3 = lax.optimization_barrier((back, got, signal, out_grad))
+    back, got, x3, g3, kept = lax.optimization_barrier((back, got, signal, out_grad, kept))
     carried = lax.all_to_all(back, "seq", 0, 0, tiled=True).reshape(pairs, 2, 4 * M, SPAN)
     sums = pl.pallas_call(
         functools.partial(sums_kernel, pairs, 1.0 / (rows * chunks * SPAN)),
@@ -419,7 +414,8 @@
         name="gradient_sums",
     )(own[None], got, own_rate, own_res)
     arriving = [lax.ppermute(sums, "batch", [(i, (i + k) % rows) for i in range(rows)]) for k in range(1, rows)]
-    mixed_part, grad_part = convolutions(1, x3, g3, mixed_part, grad_part)
+    arrived_far = other_core(kept)
+    mixed_part, grad_part = convolutions(early, steps - early, x3, g3, mixed_part, grad_part)
 
     def total_kernel(*refs):
         total = refs[0][...]
@@ -434,7 +430,9 @@
         compiler_params=little,
         name="total",
     )(sums, *arriving)
-    carried, total, mixed_part, grad_part = lax.optimization_barrier((carried, total, mixed_part, grad_part))
+    carried, total, mixed_part, grad_part, arrived_far = lax.optimization_barrier(
+        (carried, total, mixed_part, grad_part, arrived_far)
+    )
     everyone = lax.all_to_all(total, "seq", 0, 0, tiled=True)
 
     flat_block = pl.BlockSpec((SPAN, wide), lambda i, at: (0, i))

time: 79.1 us -> 75.4 us (0.953)
  Pallas kernels: 42.8 us -> 39.7 us
    pallas_call x2, Pallas kernels: 13.5 us -> 11.6 us  [ends_and_lags(): pl.pallas_call(first_kernel, grid_spec=pltpu.PrefetchScalarGridSpec(num_s...]
    all_to_all x1, waiting for transfers between devices: 1.7 us -> 0.01 us  [exchange(): lax.all_to_all(values, 'seq', 0, 0, axis_index_groups=same_core, tiled=True)]
    all_to_all x1, starting transfers between devices: 8.22 us -> 6.73 us  [local(): everyone = lax.all_to_all(total, 'seq', 0, 0, tiled=True)]
    all_to_all x1, waiting for transfers between devices: 0.01 us -> 1.45 us  [local(): lax.all_to_all(back, 'seq', 0, 0, tiled=True).reshape(pairs, 2, 4 * M, SPAN)]
    all_to_all x1, starting transfers between devices: 6.27 us -> 7.53 us  [local(): lax.all_to_all(back, 'seq', 0, 0, tiled=True).reshape(pairs, 2, 4 * M, SPAN)]
    pallas_call x1, Pallas kernels: 2.17 us -> 1.26 us  [local(): pl.pallas_call(pair_kernel, grid_spec=pltpu.PrefetchScalarGridSpec(num_sc...]
  transfers between devices with their start and end apart: 8 -> 8, of which waited for: 2 -> 2; matrix products, arithmetic and copies ran while one was open for 2% -> 3% of each run, Pallas kernels for 41% -> 40%
where the time goes in v7:
time: 75.4 us; the launch traced here: 74.9 us
  Pallas kernels  39.7 us (53%)
  starting transfers between devices  27.5 us (36%)
  waiting for transfers between devices  3.95 us (5%)
  local copies, waits for them, and re-layouts  2.95 us (4%)
  between operations  0.83 us (1%)
    pallas_call x2, Pallas kernels, convolutions(): pl.pallas_call(second_kernel, grid=(count,), in_specs=kernel_blocks + [pl...  16.6 us
    pallas_call x2, Pallas kernels, ends_and_lags(): pl.pallas_call(first_kernel, grid_spec=pltpu.PrefetchScalarGridSpec(num_s...  11.6 us
    all_to_all x1, starting transfers between devices, exchange(): lax.all_to_all(values, 'seq', 0, 0, axis_index_groups=same_core, tiled=True)  7.85 us
    pallas_call x1, Pallas kernels, local(): pl.pallas_call(last_kernel, grid_spec=pltpu.PrefetchScalarGridSpec(num_sc...  7.78 us
    all_to_all x1, starting transfers between devices, local(): lax.all_to_all(back, 'seq', 0, 0, tiled=True).reshape(pairs, 2, 4 * M, SPAN)  7.53 us
    all_to_all x1, starting transfers between devices, local(): everyone = lax.all_to_all(total, 'seq', 0, 0, tiled=True)  6.73 us
    ppermute x3, starting transfers between devices, local(): lax.ppermute(sums, 'batch', [(i, (i + k) % rows) for i in range(rows)])  3.63 us
    all_to_all x1, waiting for transfers between devices, local(): everyone = lax.all_to_all(total, 'seq', 0, 0, tiled=True)  2.49 us
  transfers between devices with their start and end apart: 8, of which 2 were waited for; matrix products, arithmetic and copies ran while one was open for 3% of the time, Pallas kernels for 40%

profile of v7, /device:TPU:1, one launch (start us, length us, event | category | flops | bytes accessed | tf_op | source)
XLA Modules:
  0.0 74.9 jit_solution(7499609681549660493)
XLA Ops:
  0.6 0.0 copy-start.4
  0.6 0.0 copy-start.5
  0.7 0.0 copy-start.2
  0.7 0.0 copy-start.6
  0.7 0.0 copy-start
  0.7 0.0 copy-start.1
  0.7 6.9 %ends_and_lags.2 = f32[16,104,128]{2,1,0:T(8,128)} custom-call(s32[1]{0:T(128)S(6)} %sub.7.half_ref, bf16[1,128,8192]{2,1,0:T(8,128)(2,1)} %x_ref.5, bf16[1,128,8192]{2,1,0:T(8,128)(2,1)} %g_ref.5, f32[8,512]{1,0:T(8,128)} %log_ref.7, f32[8,8192]{1,0:T(8,128)} %res_ref.11, bf16[256,256]{1,0:T(8,128)(2,1)} %constant.35.clone.fwd_ref, ...), custom_call_target="tpu_custom_call" | custom-call | tf_op jit(solution)/shard_map/ends_and_lags/pallas_call | solution.py:325
  7.6 1.4 %collective-permute-start = (f32[16,104,128]{2,1,0:T(8,128)}, f32[16,104,128]{2,1,0:T(8,128)S(1)}, u32[]{:S(2)}, u32[]{:S(2)}) collective-permute-start(f32[16,104,128]{2,1,0:T(8,128)} %ends_and_lags.2), channel_id=1, source_target_pairs={{0,4},{4,0},{8,12},{12,8},{16,20},{20,16},{24,28},{28,24},{32,36},... | collective-permute-start | bytes 2555912 | tf_op jit(solution)/shard_map/ppermute | solution.py:322
  9.0 0.0 copy-done.4
  9.0 0.0 copy-done.5
  9.0 0.0 copy-done.2
  9.0 0.0 copy-done.6
  9.0 0.0 copy-done
  9.0 0.0 copy-done.1
  9.1 4.7 %ends_and_lags.3.kept_ref = f32[16,104,128]{2,1,0:T(8,128)S(1)} custom-call(s32[1]{0:T(128)} %bitcast.half_ref.core_ref, bf16[1,128,8192]{2,1,0:T(8,128)(2,1)S(1)} %copy-done, bf16[1,128,8192]{2,1,0:T(8,128)(2,1)S(1)} %copy-done.1, f32[8,512]{1,0:T(8,128)S(1)} %copy-done.6, f32[8,8192]{1,0:T(8,128)S(1)} %copy-done.2, bf16[256,256]{1,0:T(8,128)(2,1)S(1)} %copy-done.5, ...), custom_call_target="tpu_custom_call" | custom-call | tf_op jit(solution)/shard_map/ends_and_lags/pallas_call | solution.py:325
  13.7 0.0 collective-permute-done.arrived_ref.near_ref
  13.7 1.3 %join_pair.1 = f32[16,88,128]{2,1,0:T(8,128)} custom-call(s32[1]{0:T(128)} %bitcast.half_ref.core_ref, f32[16,104,128]{2,1,0:T(8,128)S(1)} %ends_and_lags.3.kept_ref, f32[16,104,128]{2,1,0:T(8,128)S(1)} %collective-permute-done.arrived_ref.near_ref, f32[8,8192]{1,0:T(8,128)S(1)} %copy-done.2), custom_call_target="tpu_custom_call" | custom-call | tf_op jit(solution)/shard_map/join_pair/pallas_call | solution.py:350
  15.0 0.0 copy-start.3
  15.0 1.0 %copy-done.3 = f32[16,104,128]{2,1,0:T(8,128)} copy-done((f32[16,104,128]{2,1,0:T(8,128)}, f32[16,104,128]{2,1,0:T(8,128)S(1)}, u32[]{:S(2)}) %copy-start.3) | copy-done | bytes 851992
  16.0 7.9 %all-to-all-start = ((f32[16,88,128]{2,1,0:T(8,128)}), f32[16,88,128]{2,1,0:T(8,128)S(1)}, u32[]{:S(2)}, u32[]{:S(2)}) async-start(f32[16,88,128]{2,1,0:T(8,128)} %join_pair.1), calls=%async_computation | async-start | bytes 1441792 | tf_op jit(solution)/shard_map/all_to_all | solution.py:319
  23.9 0.1 constant_dynamic-slice_fusion.1
  24.0 0.1 broadcast_in_dim.19
  24.1 0.1 reshape.16.rate_ref
  24.2 0.1 copy.12
  24.3 0.2 broadcast_in_dim.17
  24.4 0.7 broadcast_in_dim.18.rate_ref
  25.1 11.3 %local_convolutions.2 = (f32[128,8192]{1,0:T(8,128)}, f32[128,8192]{1,0:T(8,128)}) custom-call(bf16[1,128,8192]{2,1,0:T(8,128)(2,1)} %x_ref.5, bf16[1,128,8192]{2,1,0:T(8,128)(2,1)} %g_ref.5, f32[32,8,128]{2,1,0:T(8,128)} %broadcast_in_dim.18.rate_ref, f32[8,8192]{1,0:T(8,128)} %res_ref.11, bf16[256,256]{1,0:T(8,128)(2,1)} %constant.35.clone.fwd_ref, ...), custom_call_target="tpu_custom_call" | custom-call | flops 314572800 | bytes 2097152 | tf_op jit(solution)/shard_map/local_convolutions/pallas_call | solution.py:385
  36.4 0.7 constant_dynamic-slice_fusion.res_ref
  37.1 0.0 all-to-all-done.got_ref
  37.1 0.8 %carries.1 = f32[32,32,128]{2,1,0:T(8,128)} custom-call(f32[16,88,128]{2,1,0:T(8,128)S(1)} %all-to-all-done.got_ref, f32[8,256]{1,0:T(8,128)S(1)} %reshape.16.rate_ref, f32[8,256]{1,0:T(8,128)S(1)} %constant_dynamic-slice_fusion.res_ref), custom_call_target="tpu_custom_call" | custom-call | tf_op jit(solution)/shard_map/carries/pallas_call | solution.py:400
  38.0 7.5 %all-to-all-start.1 = ((f32[32,32,128]{2,1,0:T(8,128)}), f32[32,32,128]{2,1,0:T(8,128)S(1)}, u32[]{:S(2)}, u32[]{:S(2)}) async-start(f32[32,32,128]{2,1,0:T(8,128)} %carries.1), calls=%async_computation.1 | async-start | bytes 1048576 | tf_op jit(solution)/shard_map/all_to_all | solution.py:407
  45.5 0.3 collective-permute-start.4
  45.8 0.2 gradient_sums.1.refs_0_
  46.0 2.5 %collective-permute-start.3 = (f32[24,128]{1,0:T(8,128)S(1)}, f32[24,128]{1,0:T(8,128)S(1)}, u32[]{:S(2)}, u32[]{:S(2)}) collective-permute-start(f32[24,128]{1,0:T(8,128)S(1)} %gradient_sums.1.refs_0_), channel_id=1, source_target_pairs={{0,3},{1,0},{2,1},{3,2},{4,7},{5,4},{6,5},{7,6},{8,11},{9,8},{10,9... | collective-permute-start | bytes 36872 | tf_op jit(solution)/shard_map/ppermute | solution.py:416
  48.5 0.5 collective-permute-start.2
  49.1 0.6 collective-permute-start.1
  49.7 5.2 %local_convolutions.3 = (f32[128,8192]{1,0:T(8,128)}, f32[128,8192]{1,0:T(8,128)}) custom-call(bf16[1,128,8192]{2,1,0:T(8,128)(2,1)} %x_ref.5, bf16[1,128,8192]{2,1,0:T(8,128)(2,1)} %g_ref.5, f32[32,8,128]{2,1,0:T(8,128)} %broadcast_in_dim.18.rate_ref, f32[8,8192]{1,0:T(8,128)} %res_ref.11, ...), custom_call_target="tpu_custom_call", output_to_operand_aliasing={{0}: (6, {}), {1}: (7, {})} | custom-call | flops 314572800 | bytes 2097152 | tf_op jit(solution)/shard_map/local_convolutions/pallas_call | solution.py:385
  54.9 0.0 collective-permute-done.3.refs_3_
  54.9 0.0 collective-permute-done.2.refs_2_
  54.9 0.0 collective-permute-done.1.refs_1_
  54.9 0.8 %total.1 = f32[32,24,128]{2,1,0:T(8,128)} custom-call(f32[24,128]{1,0:T(8,128)S(1)} %gradient_sums.1.refs_0_, f32[24,128]{1,0:T(8,128)S(1)} %collective-permute-done.1.refs_1_, f32[24,128]{1,0:T(8,128)S(1)} %collective-permute-done.2.refs_2_, f32[24,128]{1,0:T(8,128)S(1)} %collective-permute-done.3.refs_3_), custom_call_target="tpu_custom_call" | custom-call | tf_op jit(solution)/shard_map/total/pallas_call | solution.py:427
  55.7 1.4 %all-to-all-done.1 = f32[32,32,128]{2,1,0:T(8,128)S(1)} async-done(((f32[32,32,128]{2,1,0:T(8,128)}), f32[32,32,128]{2,1,0:T(8,128)S(1)}, u32[]{:S(2)}, u32[]{:S(2)}) %all-to-all-start.1) | async-done | bytes 524320 | tf_op jit(solution)/shard_map/all_to_all | solution.py:407
  57.2 0.0 copy-start.8
  57.2 0.0 collective-permute-done.4.far_ref
  57.2 0.0 copy-start.9
  57.2 6.7 %all-to-all-start.2 = ((f32[32,24,128]{2,1,0:T(8,128)}), f32[32,24,128]{2,1,0:T(8,128)S(1)}, u32[]{:S(2)}, u32[]{:S(2)}) async-start(f32[32,24,128]{2,1,0:T(8,128)} %total.1), calls=%async_computation.2 | async-start | bytes 786432 | tf_op jit(solution)/shard_map/all_to_all | solution.py:436
  63.9 0.0 copy-done.8
  63.9 0.0 copy-done.9
  63.9 0.0 copy-start.7
  63.9 7.8 %add_carries.1 = (bf16[1,128,8192]{2,1,0:T(8,128)(2,1)}, bf16[1,128,8192]{2,1,0:T(8,128)(2,1)}) custom-call(s32[1]{0:T(128)} %bitcast.half_ref.core_ref, f32[128,8192]{1,0:T(8,128)} %get-tuple-element.51.mixed_ref, f32[128,8192]{1,0:T(8,128)} %get-tuple-element.52.grad_ref, f32[32,8,128]{2,1,0:T(8,128)} %broadcast_in_dim.18.rate_ref, f32[8,512]{1,0:T(8,128)} %log_ref.7, ...), custom_call_target="tpu_custom_call" | custom-call | flops 1677721600 | bytes 12582912 | tf_op jit(solution)/shard_map/add_carries/pallas_call | solution.py:441
  71.7 2.5 %all-to-all-done.2.all_ref = f32[32,24,128]{2,1,0:T(8,128)S(1)} async-done(((f32[32,24,128]{2,1,0:T(8,128)}), f32[32,24,128]{2,1,0:T(8,128)S(1)}, u32[]{:S(2)}, u32[]{:S(2)}) %all-to-all-start.2) | async-done | bytes 393248 | tf_op jit(solution)/shard_map/all_to_all | solution.py:436
  74.2 0.0 copy-done.7
  74.2 0.7 unpack.1
  (1 shorter events, 0.0 us)
Async XLA Ops:
  0.6 8.4 %copy-start.4 = (bf16[128,768]{1,0:T(8,128)(2,1)S(1)}, bf16[128,768]{1,0:T(8,128)(2,1)}, u32[]{:S(2)}) copy-start(bf16[128,768]{1,0:T(8,128)(2,1)} %constant.36.clone.inv_ref) | copy-start | bytes 589828
  0.6 8.4 %copy-start.5 = (bf16[256,256]{1,0:T(8,128)(2,1)S(1)}, bf16[256,256]{1,0:T(8,128)(2,1)}, u32[]{:S(2)}) copy-start(bf16[256,256]{1,0:T(8,128)(2,1)} %constant.35.clone.fwd_ref) | copy-start | bytes 393220
  0.7 8.4 %copy-start.2 = (f32[8,8192]{1,0:T(8,128)S(1)}, f32[8,8192]{1,0:T(8,128)}, u32[]{:S(2)}) copy-start(f32[8,8192]{1,0:T(8,128)} %res_ref.11) | copy-start | bytes 786436
  0.7 8.4 %copy-start.6 = (f32[8,512]{1,0:T(8,128)S(1)}, f32[8,512]{1,0:T(8,128)}, u32[]{:S(2)}) copy-start(f32[8,512]{1,0:T(8,128)} %log_ref.7) | copy-start | bytes 49156
  0.7 8.4 %copy-start = (bf16[1,128,8192]{2,1,0:T(8,128)(2,1)S(1)}, bf16[1,128,8192]{2,1,0:T(8,128)(2,1)}, u32[]{:S(2)}) copy-start(bf16[1,128,8192]{2,1,0:T(8,128)(2,1)} %x_ref.5) | copy-start | bytes 6291460
  0.7 8.3 %copy-start.1 = (bf16[1,128,8192]{2,1,0:T(8,128)(2,1)S(1)}, bf16[1,128,8192]{2,1,0:T(8,128)(2,1)}, u32[]{:S(2)}) copy-start(bf16[1,128,8192]{2,1,0:T(8,128)(2,1)} %g_ref.5) | copy-start | bytes 6291460
  7.6 6.1 %collective-permute-start = (f32[16,104,128]{2,1,0:T(8,128)}, f32[16,104,128]{2,1,0:T(8,128)S(1)}, u32[]{:S(2)}, u32[]{:S(2)}) collective-permute-start(f32[16,104,128]{2,1,0:T(8,128)} %ends_and_lags.2), channel_id=1, source_target_pairs={{0,4},{4,0},{8,12},{12,8},{16,20},{20,16},{24,28},{28,24},{32,36},... | collective-permute-start | bytes 2555912 | tf_op jit(solution)/shard_map/ppermute | solution.py:322
  15.0 1.0 %copy-start.3 = (f32[16,104,128]{2,1,0:T(8,128)}, f32[16,104,128]{2,1,0:T(8,128)S(1)}, u32[]{:S(2)}) copy-start(f32[16,104,128]{2,1,0:T(8,128)S(1)} %collective-permute-done.arrived_ref.near_ref) | copy-start | bytes 2555908
  16.0 21.1 %all-to-all-start = ((f32[16,88,128]{2,1,0:T(8,128)}), f32[16,88,128]{2,1,0:T(8,128)S(1)}, u32[]{:S(2)}, u32[]{:S(2)}) async-start(f32[16,88,128]{2,1,0:T(8,128)} %join_pair.1), calls=%async_computation | async-start | bytes 1441792 | tf_op jit(solution)/shard_map/all_to_all | solution.py:319
  38.0 19.2 %all-to-all-start.1 = ((f32[32,32,128]{2,1,0:T(8,128)}), f32[32,32,128]{2,1,0:T(8,128)S(1)}, u32[]{:S(2)}, u32[]{:S(2)}) async-start(f32[32,32,128]{2,1,0:T(8,128)} %carries.1), calls=%async_computation.1 | async-start | bytes 1048576 | tf_op jit(solution)/shard_map/all_to_all | solution.py:407
  45.5 11.6 %collective-permute-start.4 = (f32[16,104,128]{2,1,0:T(8,128)S(1)}, f32[16,104,128]{2,1,0:T(8,128)S(1)}, u32[]{:S(2)}, u32[]{:S(2)}) collective-permute-start(f32[16,104,128]{2,1,0:T(8,128)S(1)} %ends_and_lags.3.kept_ref), channel_id=1, source_target_pairs={{0,4},{4,0},{8,12},{12,8},{16,20},{20,16},{24,28},{28,24},{32,36},... | collective-permute-start | bytes 2555912 | tf_op jit(solution)/shard_map/ppermute | solution.py:322
  46.0 8.9 %collective-permute-start.3 = (f32[24,128]{1,0:T(8,128)S(1)}, f32[24,128]{1,0:T(8,128)S(1)}, u32[]{:S(2)}, u32[]{:S(2)}) collective-permute-start(f32[24,128]{1,0:T(8,128)S(1)} %gradient_sums.1.refs_0_), channel_id=1, source_target_pairs={{0,3},{1,0},{2,1},{3,2},{4,7},{5,4},{6,5},{7,6},{8,11},{9,8},{10,9... | collective-permute-start | bytes 36872 | tf_op jit(solution)/shard_map/ppermute | solution.py:416
  48.5 6.4 %collective-permute-start.2 = (f32[24,128]{1,0:T(8,128)S(1)}, f32[24,128]{1,0:T(8,128)S(1)}, u32[]{:S(2)}, u32[]{:S(2)}) collective-permute-start(f32[24,128]{1,0:T(8,128)S(1)} %gradient_sums.1.refs_0_), channel_id=1, source_target_pairs={{0,2},{1,3},{2,0},{3,1},{4,6},{5,7},{6,4},{7,5},{8,10},{9,11},{10,... | collective-permute-start | bytes 36872 | tf_op jit(solution)/shard_map/ppermute | solution.py:416
  49.1 5.9 %collective-permute-start.1 = (f32[24,128]{1,0:T(8,128)S(1)}, f32[24,128]{1,0:T(8,128)S(1)}, u32[]{:S(2)}, u32[]{:S(2)}) collective-permute-start(f32[24,128]{1,0:T(8,128)S(1)} %gradient_sums.1.refs_0_), channel_id=1, source_target_pairs={{0,1},{1,2},{2,3},{3,0},{4,5},{5,6},{6,7},{7,4},{8,9},{9,10},{10,1... | collective-permute-start | bytes 36872 | tf_op jit(solution)/shard_map/ppermute | solution.py:416
  57.2 6.8 %copy-start.8 = (f32[32,32,128]{2,1,0:T(8,128)}, f32[32,32,128]{2,1,0:T(8,128)S(1)}, u32[]{:S(2)}) copy-start(f32[32,32,128]{2,1,0:T(8,128)S(1)} %all-to-all-done.1) | copy-start | bytes 1572868
  57.2 6.8 %copy-start.9 = (f32[16,104,128]{2,1,0:T(8,128)}, f32[16,104,128]{2,1,0:T(8,128)S(1)}, u32[]{:S(2)}) copy-start(f32[16,104,128]{2,1,0:T(8,128)S(1)} %collective-permute-done.4.far_ref) | copy-start | bytes 2555908
  57.2 17.0 %all-to-all-start.2 = ((f32[32,24,128]{2,1,0:T(8,128)}), f32[32,24,128]{2,1,0:T(8,128)S(1)}, u32[]{:S(2)}, u32[]{:S(2)}) async-start(f32[32,24,128]{2,1,0:T(8,128)} %total.1), calls=%async_computation.2 | async-start | bytes 786432 | tf_op jit(solution)/shard_map/all_to_all | solution.py:436
  63.9 10.3 %copy-start.7 = (f32[8,512]{1,0:T(8,128)S(1)}, f32[8,512]{1,0:T(8,128)}, u32[]{:S(2)}) copy-start(f32[8,512]{1,0:T(8,128)} %log_ref.7) | copy-start | bytes 49156

commit v8 on v7

--- a/solution.py
+++ b/solution.py
@@ -164,9 +164,11 @@
     return dot(jnp.concatenate([high, low], 1), twice(place))
 
 
-def pair_kernel(core_ref, kept_ref, arrived_ref, res_ref, pair_ref):
+def pair_kernel(core_ref, kept_ref, arrived_ref, res_ref, pair_ref, mine_ref, near_ref):
     even = core_ref[0] == 0
     count = kept_ref.shape[0]
+    mine_ref[...] = kept_ref[:, : 4 * M, :]
+    near_ref[...] = arrived_ref[:, : 4 * M, :]
     weighted = ([], [])
     for s in range(count):
         for h in range(2):
@@ -347,7 +349,9 @@
     arrived = other_core(away)
     kept = ends_and_lags(core_scalar, x2, g2, pltpu.CompilerParams(vmem_limit_bytes=40 * 2**20))
     state_block = pl.BlockSpec((block, 11 * M, SPAN), lambda i, at: (i, 0, 0))
-    pair = pl.pallas_call(
+    edge_block = pl.BlockSpec((block, 4 * M, SPAN), lambda i, at: (i, 0, 0))
+    edge_shape = jax.ShapeDtypeStruct((pairs, 4 * M, SPAN), F32)
+    pair, mine, near = pl.pallas_call(
         pair_kernel,
         grid_spec=pltpu.PrefetchScalarGridSpec(
             num_scalar_prefetch=1,
@@ -357,13 +361,13 @@
                 pl.BlockSpec((block, 11 * M, SPAN), lambda i, at: (i, 0, 0)),
                 pl.BlockSpec((M, wide), lambda i, at: (0, at[0] * part + i)),
             ],
-            out_specs=state_block,
+            out_specs=[state_block, edge_block, edge_block],
         ),
-        out_shape=states_shape,
+        out_shape=[states_shape, edge_shape, edge_shape],
         compiler_params=little,
         name="join_pair",
     )(core_scalar, kept, arrived, residues)
-    pair, later_rates, later_res, kept = lax.optimization_barrier((pair, log_rates, residues, kept))
+    pair, later_rates, later_res = lax.optimization_barrier((pair, log_rates, residues))
     got = exchange(pair)
 
     decay_rate = jnp.exp(later_rates)
@@ -403,7 +407,7 @@
         compiler_params=little,
         name="carries",
     )(got, own_rate, own_res)
-    back, got, x3, g3, kept = lax.optimization_barrier((back, got, signal, out_grad, kept))
+    back, got, x3, g3, mine = lax.optimization_barrier((back, got, signal, out_grad, mine))
     carried = lax.all_to_all(back, "seq", 0, 0, tiled=True).reshape(pairs, 2, 4 * M, SPAN)
     sums = pl.pallas_call(
         functools.partial(sums_kernel, pairs, 1.0 / (rows * chunks * SPAN)),
@@ -414,7 +418,7 @@
         name="gradient_sums",
     )(own[None], got, own_rate, own_res)
     arriving = [lax.ppermute(sums, "batch", [(i, (i + k) % rows) for i in range(rows)]) for k in range(1, rows)]
-    arrived_far = other_core(kept)
+    far = other_core(mine)
     mixed_part, grad_part = convolutions(early, steps - early, x3, g3, mixed_part, grad_part)
 
     def total_kernel(*refs):
@@ -430,9 +434,7 @@
         compiler_params=little,
         name="total",
     )(sums, *arriving)
-    carried, total, mixed_part, grad_part, arrived_far = lax.optimization_barrier(
-        (carried, total, mixed_part, grad_part, arrived_far)
-    )
+    carried, total, mixed_part, grad_part, far = lax.optimization_barrier((carried, total, mixed_part, grad_part, far))
     everyone = lax.all_to_all(total, "seq", 0, 0, tiled=True)
 
     flat_block = pl.BlockSpec((SPAN, wide), lambda i, at: (0, i))
@@ -459,7 +461,7 @@
         compiler_params=params,
         cost_estimate=pl.CostEstimate(flops=work * 1600, bytes_accessed=work * 12, transcendentals=work),
         name="add_carries",
-    )(core_scalar, mixed_part, grad_part, rate_rows, log_rates, residues, carried, arrived, arrived_far)
+    )(core_scalar, mixed_part, grad_part, rate_rows, log_rates, residues, carried, near, far)
     grad_residues, grad_rates = pl.pallas_call(
         functools.partial(gather_kernel, pairs),
         out_shape=[jax.ShapeDtypeStruct(residues.shape, F32), jax.ShapeDtypeStruct(log_rates.shape, F32)],

time: 75.4 us -> 75.2 us (level)
  no operation moved by 1% of the time
where the time goes in v8:
time: 75.2 us; the launch traced here: 74.7 us
  Pallas kernels  39.8 us (53%)
  starting transfers between devices  27.5 us (37%)
  waiting for transfers between devices  3.97 us (5%)
  local copies, waits for them, and re-layouts  2.65 us (4%)
  between operations  0.83 us (1%)
    pallas_call x2, Pallas kernels, convolutions(): pl.pallas_call(second_kernel, grid=(count,), in_specs=kernel_blocks + [pl...  16.7 us
    pallas_call x2, Pallas kernels, ends_and_lags(): pl.pallas_call(first_kernel, grid_spec=pltpu.PrefetchScalarGridSpec(num_s...  11.6 us
    all_to_all x1, starting transfers between devices, exchange(): lax.all_to_all(values, 'seq', 0, 0, axis_index_groups=same_core, tiled=True)  7.85 us
    pallas_call x1, Pallas kernels, local(): pl.pallas_call(last_kernel, grid_spec=pltpu.PrefetchScalarGridSpec(num_sc...  7.78 us
    all_to_all x1, starting transfers between devices, local(): lax.all_to_all(back, 'seq', 0, 0, tiled=True).reshape(pairs, 2, 4 * M, SPAN)  7.53 us
    all_to_all x1, starting transfers between devices, local(): everyone = lax.all_to_all(total, 'seq', 0, 0, tiled=True)  6.71 us
    ppermute x3, starting transfers between devices, local(): lax.ppermute(sums, 'batch', [(i, (i + k) % rows) for i in range(rows)])  3.63 us
    all_to_all x1, waiting for transfers between devices, local(): everyone = lax.all_to_all(total, 'seq', 0, 0, tiled=True)  2.49 us
  transfers between devices with their start and end apart: 8, of which 2 were waited for; matrix products, arithmetic and copies ran while one was open for 3% of the time, Pallas kernels for 40%

profile of v8, /device:TPU:1, one launch (start us, length us, event | category | flops | bytes accessed | tf_op | source)
XLA Modules:
  0.0 74.7 jit_solution(9630280215775689747)
XLA Ops:
  0.6 0.0 copy-start.3
  0.6 0.0 copy-start.4
  0.7 0.0 copy-start.2
  0.7 0.0 copy-start.5
  0.7 0.0 copy-start
  0.7 0.0 copy-start.1
  0.7 6.9 %ends_and_lags.2 = f32[16,104,128]{2,1,0:T(8,128)} custom-call(s32[1]{0:T(128)S(6)} %sub.7.half_ref, bf16[1,128,8192]{2,1,0:T(8,128)(2,1)} %x_ref.5, bf16[1,128,8192]{2,1,0:T(8,128)(2,1)} %g_ref.5, f32[8,512]{1,0:T(8,128)} %log_ref.7, f32[8,8192]{1,0:T(8,128)} %res_ref.11, bf16[256,256]{1,0:T(8,128)(2,1)} %constant.35.clone.fwd_ref, ...), custom_call_target="tpu_custom_call" | custom-call | tf_op jit(solution)/shard_map/ends_and_lags/pallas_call | solution.py:327
  7.6 1.4 %collective-permute-start = (f32[16,104,128]{2,1,0:T(8,128)}, f32[16,104,128]{2,1,0:T(8,128)S(1)}, u32[]{:S(2)}, u32[]{:S(2)}) collective-permute-start(f32[16,104,128]{2,1,0:T(8,128)} %ends_and_lags.2), channel_id=1, source_target_pairs={{0,4},{4,0},{8,12},{12,8},{16,20},{20,16},{24,28},{28,24},{32,36},... | collective-permute-start | bytes 2555912 | tf_op jit(solution)/shard_map/ppermute | solution.py:324
  9.0 0.0 copy-done.3
  9.0 0.0 copy-done.4
  9.0 0.0 copy-done.2
  9.0 0.0 copy-done.5
  9.0 0.0 copy-done
  9.0 0.0 copy-done.1
  9.1 4.7 %ends_and_lags.3.kept_ref = f32[16,104,128]{2,1,0:T(8,128)S(1)} custom-call(s32[1]{0:T(128)} %bitcast.half_ref.core_ref, bf16[1,128,8192]{2,1,0:T(8,128)(2,1)S(1)} %copy-done, bf16[1,128,8192]{2,1,0:T(8,128)(2,1)S(1)} %copy-done.1, f32[8,512]{1,0:T(8,128)S(1)} %copy-done.5, f32[8,8192]{1,0:T(8,128)S(1)} %copy-done.2, bf16[256,256]{1,0:T(8,128)(2,1)S(1)} %copy-done.4, ...), custom_call_target="tpu_custom_call" | custom-call | tf_op jit(solution)/shard_map/ends_and_lags/pallas_call | solution.py:327
  13.7 0.0 collective-permute-done.arrived_ref
  13.7 1.3 %join_pair.1 = (f32[16,88,128]{2,1,0:T(8,128)}, f32[16,32,128]{2,1,0:T(8,128)S(1)}, f32[16,32,128]{2,1,0:T(8,128)S(1)}) custom-call(s32[1]{0:T(128)} %bitcast.half_ref.core_ref, f32[16,104,128]{2,1,0:T(8,128)S(1)} %ends_and_lags.3.kept_ref, f32[16,104,128]{2,1,0:T(8,128)S(1)} %collective-permute-done.arrived_ref, f32[8,8192]{1,0:T(8,128)S(1)} %copy-done.2), custom_call_target="tpu_custom_call" | custom-call | tf_op jit(solution)/shard_map/join_pair/pallas_call | solution.py:354
  15.0 0.0 copy-start.7
  15.0 0.7 copy-done.7
  15.7 7.9 %all-to-all-start = ((f32[16,88,128]{2,1,0:T(8,128)}), f32[16,88,128]{2,1,0:T(8,128)S(1)}, u32[]{:S(2)}, u32[]{:S(2)}) async-start(f32[16,88,128]{2,1,0:T(8,128)} %get-tuple-element.38), calls=%async_computation | async-start | bytes 1441792 | tf_op jit(solution)/shard_map/all_to_all | solution.py:321
  23.6 0.1 constant_dynamic-slice_fusion.1
  23.7 0.1 broadcast_in_dim.19
  23.8 0.1 reshape.16.rate_ref
  23.9 0.1 copy.12
  24.0 0.2 broadcast_in_dim.17
  24.2 0.7 broadcast_in_dim.18.rate_ref
  24.8 11.4 %local_convolutions.2 = (f32[128,8192]{1,0:T(8,128)}, f32[128,8192]{1,0:T(8,128)}) custom-call(bf16[1,128,8192]{2,1,0:T(8,128)(2,1)} %x_ref.5, bf16[1,128,8192]{2,1,0:T(8,128)(2,1)} %g_ref.5, f32[32,8,128]{2,1,0:T(8,128)} %broadcast_in_dim.18.rate_ref, f32[8,8192]{1,0:T(8,128)} %res_ref.11, bf16[256,256]{1,0:T(8,128)(2,1)} %constant.35.clone.fwd_ref, ...), custom_call_target="tpu_custom_call" | custom-call | flops 314572800 | bytes 2097152 | tf_op jit(solution)/shard_map/local_convolutions/pallas_call | solution.py:389
  36.3 0.7 constant_dynamic-slice_fusion.res_ref
  37.0 0.0 all-to-all-done.got_ref
  37.0 0.8 %carries.1 = f32[32,32,128]{2,1,0:T(8,128)} custom-call(f32[16,88,128]{2,1,0:T(8,128)S(1)} %all-to-all-done.got_ref, f32[8,256]{1,0:T(8,128)S(1)} %reshape.16.rate_ref, f32[8,256]{1,0:T(8,128)S(1)} %constant_dynamic-slice_fusion.res_ref), custom_call_target="tpu_custom_call" | custom-call | tf_op jit(solution)/shard_map/carries/pallas_call | solution.py:404
  37.8 7.5 %all-to-all-start.1 = ((f32[32,32,128]{2,1,0:T(8,128)}), f32[32,32,128]{2,1,0:T(8,128)S(1)}, u32[]{:S(2)}, u32[]{:S(2)}) async-start(f32[32,32,128]{2,1,0:T(8,128)} %carries.1), calls=%async_computation.1 | async-start | bytes 1048576 | tf_op jit(solution)/shard_map/all_to_all | solution.py:411
  45.4 0.3 collective-permute-start.4
  45.7 0.2 gradient_sums.1.refs_0_
  45.9 2.5 %collective-permute-start.3 = (f32[24,128]{1,0:T(8,128)S(1)}, f32[24,128]{1,0:T(8,128)S(1)}, u32[]{:S(2)}, u32[]{:S(2)}) collective-permute-start(f32[24,128]{1,0:T(8,128)S(1)} %gradient_sums.1.refs_0_), channel_id=1, source_target_pairs={{0,3},{1,0},{2,1},{3,2},{4,7},{5,4},{6,5},{7,6},{8,11},{9,8},{10,9... | collective-permute-start | bytes 36872 | tf_op jit(solution)/shard_map/ppermute | solution.py:420
  48.4 0.5 collective-permute-start.2
  48.9 0.6 collective-permute-start.1
  49.5 5.2 %local_convolutions.3 = (f32[128,8192]{1,0:T(8,128)}, f32[128,8192]{1,0:T(8,128)}) custom-call(bf16[1,128,8192]{2,1,0:T(8,128)(2,1)} %x_ref.5, bf16[1,128,8192]{2,1,0:T(8,128)(2,1)} %g_ref.5, f32[32,8,128]{2,1,0:T(8,128)} %broadcast_in_dim.18.rate_ref, f32[8,8192]{1,0:T(8,128)} %res_ref.11, ...), custom_call_target="tpu_custom_call", output_to_operand_aliasing={{0}: (6, {}), {1}: (7, {})} | custom-call | flops 314572800 | bytes 2097152 | tf_op jit(solution)/shard_map/local_convolutions/pallas_call | solution.py:389
  54.7 0.0 collective-permute-done.3.refs_3_
  54.7 0.0 collective-permute-done.2.refs_2_
  54.7 0.0 collective-permute-done.1.refs_1_
  54.7 0.8 %total.1 = f32[32,24,128]{2,1,0:T(8,128)} custom-call(f32[24,128]{1,0:T(8,128)S(1)} %gradient_sums.1.refs_0_, f32[24,128]{1,0:T(8,128)S(1)} %collective-permute-done.1.refs_1_, f32[24,128]{1,0:T(8,128)S(1)} %collective-permute-done.2.refs_2_, f32[24,128]{1,0:T(8,128)S(1)} %collective-permute-done.3.refs_3_), custom_call_target="tpu_custom_call" | custom-call | tf_op jit(solution)/shard_map/total/pallas_call | solution.py:431
  55.5 0.0 collective-permute-done.4.far_ref
  55.5 0.0 copy-start.9
  55.5 1.5 %all-to-all-done.1 = f32[32,32,128]{2,1,0:T(8,128)S(1)} async-done(((f32[32,32,128]{2,1,0:T(8,128)}), f32[32,32,128]{2,1,0:T(8,128)S(1)}, u32[]{:S(2)}, u32[]{:S(2)}) %all-to-all-start.1) | async-done | bytes 524320 | tf_op jit(solution)/shard_map/all_to_all | solution.py:411
  57.0 0.0 copy-start.8
  57.0 6.7 %all-to-all-start.2 = ((f32[32,24,128]{2,1,0:T(8,128)}), f32[32,24,128]{2,1,0:T(8,128)S(1)}, u32[]{:S(2)}, u32[]{:S(2)}) async-start(f32[32,24,128]{2,1,0:T(8,128)} %total.1), calls=%async_computation.2 | async-start | bytes 786432 | tf_op jit(solution)/shard_map/all_to_all | solution.py:438
  63.7 0.0 copy-done.9
  63.7 0.0 copy-done.8
  63.7 0.0 copy-start.6
  63.7 7.8 %add_carries.1 = (bf16[1,128,8192]{2,1,0:T(8,128)(2,1)}, bf16[1,128,8192]{2,1,0:T(8,128)(2,1)}) custom-call(s32[1]{0:T(128)} %bitcast.half_ref.core_ref, f32[128,8192]{1,0:T(8,128)} %get-tuple-element.54.mixed_ref, f32[128,8192]{1,0:T(8,128)} %get-tuple-element.55.grad_ref, f32[32,8,128]{2,1,0:T(8,128)} %broadcast_in_dim.18.rate_ref, f32[8,512]{1,0:T(8,128)} %log_ref.7, ...), custom_call_target="tpu_custom_call" | custom-call | flops 1677721600 | bytes 12582912 | tf_op jit(solution)/shard_map/add_carries/pallas_call | solution.py:443
  71.5 2.5 %all-to-all-done.2.all_ref = f32[32,24,128]{2,1,0:T(8,128)S(1)} async-done(((f32[32,24,128]{2,1,0:T(8,128)}), f32[32,24,128]{2,1,0:T(8,128)S(1)}, u32[]{:S(2)}, u32[]{:S(2)}) %all-to-all-start.2) | async-done | bytes 393248 | tf_op jit(solution)/shard_map/all_to_all | solution.py:438
  74.0 0.0 copy-done.6
  74.0 0.7 unpack.1
  (1 shorter events, 0.0 us)
Async XLA Ops:
  0.6 8.4 %copy-start.3 = (bf16[128,768]{1,0:T(8,128)(2,1)S(1)}, bf16[128,768]{1,0:T(8,128)(2,1)}, u32[]{:S(2)}) copy-start(bf16[128,768]{1,0:T(8,128)(2,1)} %constant.36.clone.inv_ref) | copy-start | bytes 589828
  0.6 8.4 %copy-start.4 = (bf16[256,256]{1,0:T(8,128)(2,1)S(1)}, bf16[256,256]{1,0:T(8,128)(2,1)}, u32[]{:S(2)}) copy-start(bf16[256,256]{1,0:T(8,128)(2,1)} %constant.35.clone.fwd_ref) | copy-start | bytes 393220
  0.7 8.4 %copy-start.2 = (f32[8,8192]{1,0:T(8,128)S(1)}, f32[8,8192]{1,0:T(8,128)}, u32[]{:S(2)}) copy-start(f32[8,8192]{1,0:T(8,128)} %res_ref.11) | copy-start | bytes 786436
  0.7 8.4 %copy-start.5 = (f32[8,512]{1,0:T(8,128)S(1)}, f32[8,512]{1,0:T(8,128)}, u32[]{:S(2)}) copy-start(f32[8,512]{1,0:T(8,128)} %log_ref.7) | copy-start | bytes 49156
  0.7 8.4 %copy-start = (bf16[1,128,8192]{2,1,0:T(8,128)(2,1)S(1)}, bf16[1,128,8192]{2,1,0:T(8,128)(2,1)}, u32[]{:S(2)}) copy-start(bf16[1,128,8192]{2,1,0:T(8,128)(2,1)} %x_ref.5) | copy-start | bytes 6291460
  0.7 8.3 %copy-start.1 = (bf16[1,128,8192]{2,1,0:T(8,128)(2,1)S(1)}, bf16[1,128,8192]{2,1,0:T(8,128)(2,1)}, u32[]{:S(2)}) copy-start(bf16[1,128,8192]{2,1,0:T(8,128)(2,1)} %g_ref.5) | copy-start | bytes 6291460
  7.6 6.1 %collective-permute-start = (f32[16,104,128]{2,1,0:T(8,128)}, f32[16,104,128]{2,1,0:T(8,128)S(1)}, u32[]{:S(2)}, u32[]{:S(2)}) collective-permute-start(f32[16,104,128]{2,1,0:T(8,128)} %ends_and_lags.2), channel_id=1, source_target_pairs={{0,4},{4,0},{8,12},{12,8},{16,20},{20,16},{24,28},{28,24},{32,36},... | collective-permute-start | bytes 2555912 | tf_op jit(solution)/shard_map/ppermute | solution.py:324
  15.0 0.7 copy-start.7
  15.7 21.3 %all-to-all-start = ((f32[16,88,128]{2,1,0:T(8,128)}), f32[16,88,128]{2,1,0:T(8,128)S(1)}, u32[]{:S(2)}, u32[]{:S(2)}) async-start(f32[16,88,128]{2,1,0:T(8,128)} %get-tuple-element.38), calls=%async_computation | async-start | bytes 1441792 | tf_op jit(solution)/shard_map/all_to_all | solution.py:321
  37.8 19.2 %all-to-all-start.1 = ((f32[32,32,128]{2,1,0:T(8,128)}), f32[32,32,128]{2,1,0:T(8,128)S(1)}, u32[]{:S(2)}, u32[]{:S(2)}) async-start(f32[32,32,128]{2,1,0:T(8,128)} %carries.1), calls=%async_computation.1 | async-start | bytes 1048576 | tf_op jit(solution)/shard_map/all_to_all | solution.py:411
  45.4 10.2 %collective-permute-start.4 = (f32[16,32,128]{2,1,0:T(8,128)S(1)}, f32[16,32,128]{2,1,0:T(8,128)S(1)}, u32[]{:S(2)}, u32[]{:S(2)}) collective-permute-start(f32[16,32,128]{2,1,0:T(8,128)S(1)} %get-tuple-element.53), channel_id=1, source_target_pairs={{0,4},{4,0},{8,12},{12,8},{16,20},{20,16},{24,28},{28,24},{32,36},... | collective-permute-start | bytes 786440 | tf_op jit(solution)/shard_map/ppermute | solution.py:324
  45.9 8.8 %collective-permute-start.3 = (f32[24,128]{1,0:T(8,128)S(1)}, f32[24,128]{1,0:T(8,128)S(1)}, u32[]{:S(2)}, u32[]{:S(2)}) collective-permute-start(f32[24,128]{1,0:T(8,128)S(1)} %gradient_sums.1.refs_0_), channel_id=1, source_target_pairs={{0,3},{1,0},{2,1},{3,2},{4,7},{5,4},{6,5},{7,6},{8,11},{9,8},{10,9... | collective-permute-start | bytes 36872 | tf_op jit(solution)/shard_map/ppermute | solution.py:420
  48.4 6.3 %collective-permute-start.2 = (f32[24,128]{1,0:T(8,128)S(1)}, f32[24,128]{1,0:T(8,128)S(1)}, u32[]{:S(2)}, u32[]{:S(2)}) collective-permute-start(f32[24,128]{1,0:T(8,128)S(1)} %gradient_sums.1.refs_0_), channel_id=1, source_target_pairs={{0,2},{1,3},{2,0},{3,1},{4,6},{5,7},{6,4},{7,5},{8,10},{9,11},{10,... | collective-permute-start | bytes 36872 | tf_op jit(solution)/shard_map/ppermute | solution.py:420
  48.9 5.8 %collective-permute-start.1 = (f32[24,128]{1,0:T(8,128)S(1)}, f32[24,128]{1,0:T(8,128)S(1)}, u32[]{:S(2)}, u32[]{:S(2)}) collective-permute-start(f32[24,128]{1,0:T(8,128)S(1)} %gradient_sums.1.refs_0_), channel_id=1, source_target_pairs={{0,1},{1,2},{2,3},{3,0},{4,5},{5,6},{6,7},{7,4},{8,9},{9,10},{10,1... | collective-permute-start | bytes 36872 | tf_op jit(solution)/shard_map/ppermute | solution.py:420
  55.5 8.2 %copy-start.9 = (f32[16,32,128]{2,1,0:T(8,128)}, f32[16,32,128]{2,1,0:T(8,128)S(1)}, u32[]{:S(2)}) copy-start(f32[16,32,128]{2,1,0:T(8,128)S(1)} %collective-permute-done.4.far_ref) | copy-start | bytes 786436
  57.0 6.7 %copy-start.8 = (f32[32,32,128]{2,1,0:T(8,128)}, f32[32,32,128]{2,1,0:T(8,128)S(1)}, u32[]{:S(2)}) copy-start(f32[32,32,128]{2,1,0:T(8,128)S(1)} %all-to-all-done.1) | copy-start | bytes 1572868
  57.0 17.0 %all-to-all-start.2 = ((f32[32,24,128]{2,1,0:T(8,128)}), f32[32,24,128]{2,1,0:T(8,128)S(1)}, u32[]{:S(2)}, u32[]{:S(2)}) async-start(f32[32,24,128]{2,1,0:T(8,128)} %total.1), calls=%async_computation.2 | async-start | bytes 786432 | tf_op jit(solution)/shard_map/all_to_all | solution.py:438
  63.7 10.3 %copy-start.6 = (f32[8,512]{1,0:T(8,128)S(1)}, f32[8,512]{1,0:T(8,128)}, u32[]{:S(2)}) copy-start(f32[8,512]{1,0:T(8,128)} %log_ref.7) | copy-start | bytes 49156

commit v9 on v8

--- a/solution.py
+++ b/solution.py
@@ -197,12 +197,12 @@
         pair_ref[s, rows, :] = kept_ref[s, rows, :] + arrived_ref[s, rows, :] + total[s * M : (s + 1) * M]
 
 
-def carry_kernel(pairs, got_ref, rate_ref, res_ref, back_ref):
+def carry_kernel(pairs, index_ref, got_ref, rate_ref, res_ref, back_ref):
     for h in range(2):
         cols = slice(h * SPAN, (h + 1) * SPAN)
         rate = rate_ref[:, cols]
         across = jnp.exp(-rate * (2 * SPAN))
-        handed = res_ref[:, cols] * jnp.exp(-rate)
+        handed = res_ref[:, pl.ds(pl.multiple_of(index_ref[0] * SLICE + h * SPAN, SPAN), SPAN)] * jnp.exp(-rate)
         state = jnp.zeros((M, SPAN), F32)
         adjoint = state
         for k in range(pairs):
@@ -222,7 +222,8 @@
     rate_sum = pltpu.roll(rate_sum, offset, 1)
     for h in range(2):
         cols = slice(h * SPAN, (h + 1) * SPAN)
-        rate, res = rate_ref[:, cols], res_ref[:, cols]
+        rate = rate_ref[:, cols]
+        res = res_ref[:, pl.ds(pl.multiple_of(index_ref[0] * SLICE + h * SPAN, SPAN), SPAN)]
         pole = jnp.exp(-rate)
         across = jnp.exp(-rate * (2 * SPAN))
 
@@ -367,13 +368,12 @@
         compiler_params=little,
         name="join_pair",
     )(core_scalar, kept, arrived, residues)
-    pair, later_rates, later_res = lax.optimization_barrier((pair, log_rates, residues))
+    pair, later_rates = lax.optimization_barrier((pair, log_rates))
     got = exchange(pair)
 
     decay_rate = jnp.exp(later_rates)
-    rate_rows = jnp.broadcast_to(decay_rate.T.reshape(chunks, 1, SPAN), (chunks, M, SPAN))
+    rate_rows = decay_rate.T.reshape(chunks, 1, SPAN)
     own_rate = jnp.repeat(lax.dynamic_slice_in_dim(decay_rate, own * GROUPS, GROUPS, 1), GROUP, axis=1)
-    own_res = lax.dynamic_slice_in_dim(later_res, own * SLICE, SLICE, 1)
 
     work = SPAN * channels
 
@@ -381,7 +381,7 @@
         kernel_blocks = [
             pl.BlockSpec((1, SPAN, wide), lambda i: (0, 0, at + i)),
             pl.BlockSpec((1, SPAN, wide), lambda i: (0, 0, at + i)),
-            pl.BlockSpec((block, M, SPAN), lambda i: (at + i, 0, 0)),
+            pl.BlockSpec((block, 1, SPAN), lambda i: (at + i, 0, 0)),
             pl.BlockSpec((M, wide), lambda i: (0, at + i)),
             whole(fwd),
             whole(inv),
@@ -404,9 +404,10 @@
     back = pl.pallas_call(
         functools.partial(carry_kernel, pairs),
         out_shape=jax.ShapeDtypeStruct((chunks, 4 * M, SPAN), F32),
+        in_specs=[smem, vmem, vmem, vmem],
         compiler_params=little,
         name="carries",
-    )(got, own_rate, own_res)
+    )(own[None], got, own_rate, residues)
     back, got, x3, g3, mine = lax.optimization_barrier((back, got, signal, out_grad, mine))
     carried = lax.all_to_all(back, "seq", 0, 0, tiled=True).reshape(pairs, 2, 4 * M, SPAN)
     sums = pl.pallas_call(
@@ -416,7 +417,7 @@
         compiler_params=little,
         cost_estimate=pl.CostEstimate(flops=10**10, bytes_accessed=10**7, transcendentals=0),
         name="gradient_sums",
-    )(own[None], got, own_rate, own_res)
+    )(own[None], got, own_rate, residues)
     arriving = [lax.ppermute(sums, "batch", [(i, (i + k) % rows) for i in range(rows)]) for k in range(1, rows)]
     far = other_core(mine)
     mixed_part, grad_part = convolutions(early, steps - early, x3, g3, mixed_part, grad_part)
@@ -448,7 +449,7 @@
             in_specs=[
                 flat_block,
                 flat_block,
-                pl.BlockSpec((block, M, SPAN), lambda i, at: (i, 0, 0)),
+                pl.BlockSpec((block, 1, SPAN), lambda i, at: (i, 0, 0)),
                 pl.BlockSpec((M, wide // GROUP), lambda i, at: (0, i)),
                 pl.BlockSpec((M, wide), lambda i, at: (0, i)),
                 pl.BlockSpec((block, None, 4 * M, SPAN), lambda i, at: (lax.rem(i, part), i // part, 0, 0)),

time: 75.2 us -> 75.6 us (level)
  starting transfers between devices: 27.5 us -> 29.9 us
  waiting for transfers between devices: 3.97 us -> 2.63 us
  local copies, waits for them, and re-layouts: 2.65 us -> 1.89 us
    ppermute x3, starting transfers between devices: 3.63 us -> 4.84 us  [local(): lax.ppermute(sums, 'batch', [(i, (i + k) % rows) for i in range(rows)])]
    all_to_all x1, waiting for transfers between devices: 1.46 us -> 0.26 us  [local(): lax.all_to_all(back, 'seq', 0, 0, tiled=True).reshape(pairs, 2, 4 * M, SPAN)]
    all_to_all x1, starting transfers between devices: 6.71 us -> 7.91 us  [local(): everyone = lax.all_to_all(total, 'seq', 0, 0, tiled=True)]
    broadcast_in_dim x2 -> x0, local copies, waits for them, and re-layouts: 0.82 us -> none  [local(): jnp.broadcast_to(decay_rate.T.reshape(chunks, 1, SPAN), (chunks, M, SPAN))]
    reshape x0 -> x1, local copies, waits for them, and re-layouts: none -> 0.76 us  [local(): rate_rows = decay_rate.T.reshape(chunks, 1, SPAN)]
  transfers between devices with their start and end apart: 8 -> 8, of which waited for: 2 -> 2; matrix products, arithmetic and copies ran while one was open for 3% -> 2% of each run, Pallas kernels for 40% -> 40%
where the time goes in v9:
time: 75.6 us; the launch traced here: 75.1 us
  Pallas kernels  39.9 us (53%)
  starting transfers between devices  29.9 us (40%)
  waiting for transfers between devices  2.63 us (3%)
  local copies, waits for them, and re-layouts  1.89 us (2%)
  between operations  0.83 us (1%)
    pallas_call x2, Pallas kernels, convolutions(): pl.pallas_call(second_kernel, grid=(count,), in_specs=kernel_blocks + [pl...  16.6 us
    pallas_call x2, Pallas kernels, ends_and_lags(): pl.pallas_call(first_kernel, grid_spec=pltpu.PrefetchScalarGridSpec(num_s...  11.6 us
    pallas_call x1, Pallas kernels, local(): pl.pallas_call(last_kernel, grid_spec=pltpu.PrefetchScalarGridSpec(num_sc...  7.92 us
    all_to_all x1, starting transfers between devices, local(): everyone = lax.all_to_all(total, 'seq', 0, 0, tiled=True)  7.91 us
    all_to_all x1, starting transfers between devices, exchange(): lax.all_to_all(values, 'seq', 0, 0, axis_index_groups=same_core, tiled=True)  7.85 us
    all_to_all x1, starting transfers between devices, local(): lax.all_to_all(back, 'seq', 0, 0, tiled=True).reshape(pairs, 2, 4 * M, SPAN)  7.56 us
    ppermute x3, starting transfers between devices, local(): lax.ppermute(sums, 'batch', [(i, (i + k) % rows) for i in range(rows)])  4.84 us
    all_to_all x1, waiting for transfers between devices, local(): everyone = lax.all_to_all(total, 'seq', 0, 0, tiled=True)  2.35 us
  transfers between devices with their start and end apart: 8, of which 2 were waited for; matrix products, arithmetic and copies ran while one was open for 2% of the time, Pallas kernels for 40%

profile of v9, /device:TPU:1, one launch (start us, length us, event | category | flops | bytes accessed | tf_op | source)
XLA Modules:
  0.0 75.1 jit_solution(14231659889513886108)
XLA Ops:
  0.6 0.0 copy-start.5
  0.6 0.0 copy-start.4
  0.7 0.0 copy-start
  0.7 0.0 copy-start.6
  0.7 0.0 copy-start.2
  0.7 0.0 copy-start.1
  0.7 6.9 %ends_and_lags.2 = f32[16,104,128]{2,1,0:T(8,128)} custom-call(s32[1]{0:T(128)S(6)} %sub.8.half_ref, bf16[1,128,8192]{2,1,0:T(8,128)(2,1)} %x_ref.5, bf16[1,128,8192]{2,1,0:T(8,128)(2,1)} %g_ref.5, f32[8,512]{1,0:T(8,128)} %log_ref.7, f32[8,8192]{1,0:T(8,128)} %res_ref.15, bf16[256,256]{1,0:T(8,128)(2,1)} %constant.31.clone.fwd_ref, ...), custom_call_target="tpu_custom_call" | custom-call | tf_op jit(solution)/shard_map/ends_and_lags/pallas_call | solution.py:328
  7.6 1.4 %collective-permute-start = (f32[16,104,128]{2,1,0:T(8,128)}, f32[16,104,128]{2,1,0:T(8,128)S(1)}, u32[]{:S(2)}, u32[]{:S(2)}) collective-permute-start(f32[16,104,128]{2,1,0:T(8,128)} %ends_and_lags.2), channel_id=1, source_target_pairs={{0,4},{4,0},{8,12},{12,8},{16,20},{20,16},{24,28},{28,24},{32,36},... | collective-permute-start | bytes 2555912 | tf_op jit(solution)/shard_map/ppermute | solution.py:325
  9.0 0.0 copy-done.5
  9.0 0.0 copy-done.4
  9.0 0.0 copy-done
  9.0 0.0 copy-done.6
  9.0 0.0 copy-done.2
  9.0 0.0 copy-done.1
  9.1 4.7 %ends_and_lags.3.kept_ref = f32[16,104,128]{2,1,0:T(8,128)S(1)} custom-call(s32[1]{0:T(128)} %bitcast.half_ref.core_ref, bf16[1,128,8192]{2,1,0:T(8,128)(2,1)S(1)} %copy-done, bf16[1,128,8192]{2,1,0:T(8,128)(2,1)S(1)} %copy-done.1, f32[8,512]{1,0:T(8,128)S(1)} %copy-done.6, f32[8,8192]{1,0:T(8,128)S(1)} %copy-done.2, bf16[256,256]{1,0:T(8,128)(2,1)S(1)} %copy-done.5, ...), custom_call_target="tpu_custom_call" | custom-call | tf_op jit(solution)/shard_map/ends_and_lags/pallas_call | solution.py:328
  13.7 0.0 copy-start.3
  13.7 0.0 collective-permute-done.arrived_ref
  13.7 1.3 %join_pair.1 = (f32[16,88,128]{2,1,0:T(8,128)}, f32[16,32,128]{2,1,0:T(8,128)S(1)}, f32[16,32,128]{2,1,0:T(8,128)S(1)}) custom-call(s32[1]{0:T(128)} %bitcast.half_ref.core_ref, f32[16,104,128]{2,1,0:T(8,128)S(1)} %ends_and_lags.3.kept_ref, f32[16,104,128]{2,1,0:T(8,128)S(1)} %collective-permute-done.arrived_ref, f32[8,8192]{1,0:T(8,128)S(1)} %copy-done.2), custom_call_target="tpu_custom_call" | custom-call | tf_op jit(solution)/shard_map/join_pair/pallas_call | solution.py:355
  15.0 0.0 copy-start.8
  15.0 0.7 copy-done.8
  15.7 7.9 %all-to-all-start = ((f32[16,88,128]{2,1,0:T(8,128)}), f32[16,88,128]{2,1,0:T(8,128)S(1)}, u32[]{:S(2)}, u32[]{:S(2)}) async-start(f32[16,88,128]{2,1,0:T(8,128)} %get-tuple-element.37), calls=%async_computation | async-start | bytes 1441792 | tf_op jit(solution)/shard_map/all_to_all | solution.py:322
  23.6 0.1 copy.13
  23.8 0.8 %reshape.17 = f32[32,1,128]{2,0,1:T(8,128)} reshape(f32[512,8]{1,0:T(8,128)S(1)} %copy.13) | data formatting | bytes 32768 | tf_op jit(solution)/shard_map/reshape | solution.py:375
  24.5 0.1 constant_dynamic-slice_fusion
  24.6 0.1 broadcast_in_dim.12
  24.7 0.1 reshape.18.rate_ref
  24.8 11.3 %local_convolutions.2 = (f32[128,8192]{1,0:T(8,128)}, f32[128,8192]{1,0:T(8,128)}) custom-call(bf16[1,128,8192]{2,1,0:T(8,128)(2,1)} %x_ref.5, bf16[1,128,8192]{2,1,0:T(8,128)(2,1)} %g_ref.5, f32[32,1,128]{2,1,0:T(1,128)} %bitcast.7, f32[8,8192]{1,0:T(8,128)} %res_ref.15, bf16[256,256]{1,0:T(8,128)(2,1)} %constant.31.clone.fwd_ref, ...), custom_call_target="tpu_custom_call" | custom-call | flops 314572800 | bytes 2097152 | tf_op jit(solution)/shard_map/local_convolutions/pallas_call | solution.py:389
  36.1 0.0 all-to-all-done.got_ref
  36.1 0.0 copy-done.3
  36.1 0.8 %carries.1 = f32[32,32,128]{2,1,0:T(8,128)} custom-call(s32[1]{0:T(128)} %bitcast.1.index_ref, f32[16,88,128]{2,1,0:T(8,128)S(1)} %all-to-all-done.got_ref, f32[8,256]{1,0:T(8,128)S(1)} %reshape.18.rate_ref, f32[8,8192]{1,0:T(8,128)S(1)} %copy-done.3), custom_call_target="tpu_custom_call" | custom-call | tf_op jit(solution)/shard_map/carries/pallas_call | solution.py:404
  37.0 7.6 %all-to-all-start.1 = ((f32[32,32,128]{2,1,0:T(8,128)}), f32[32,32,128]{2,1,0:T(8,128)S(1)}, u32[]{:S(2)}, u32[]{:S(2)}) async-start(f32[32,32,128]{2,1,0:T(8,128)} %carries.1), calls=%async_computation.1 | async-start | bytes 1048576 | tf_op jit(solution)/shard_map/all_to_all | solution.py:412
  44.5 0.3 collective-permute-start.4
  44.9 0.2 gradient_sums.1.refs_0_
  45.0 1.2 %collective-permute-start.1 = (f32[24,128]{1,0:T(8,128)S(1)}, f32[24,128]{1,0:T(8,128)S(1)}, u32[]{:S(2)}, u32[]{:S(2)}) collective-permute-start(f32[24,128]{1,0:T(8,128)S(1)} %gradient_sums.1.refs_0_), channel_id=1, source_target_pairs={{0,1},{1,2},{2,3},{3,0},{4,5},{5,6},{6,7},{7,4},{8,9},{9,10},{10,1... | collective-permute-start | bytes 36872 | tf_op jit(solution)/shard_map/ppermute | solution.py:421
  46.3 2.5 %collective-permute-start.2 = (f32[24,128]{1,0:T(8,128)S(1)}, f32[24,128]{1,0:T(8,128)S(1)}, u32[]{:S(2)}, u32[]{:S(2)}) collective-permute-start(f32[24,128]{1,0:T(8,128)S(1)} %gradient_sums.1.refs_0_), channel_id=1, source_target_pairs={{0,2},{1,3},{2,0},{3,1},{4,6},{5,7},{6,4},{7,5},{8,10},{9,11},{10,... | collective-permute-start | bytes 36872 | tf_op jit(solution)/shard_map/ppermute | solution.py:421
  48.7 1.1 %collective-permute-start.3 = (f32[24,128]{1,0:T(8,128)S(1)}, f32[24,128]{1,0:T(8,128)S(1)}, u32[]{:S(2)}, u32[]{:S(2)}) collective-permute-start(f32[24,128]{1,0:T(8,128)S(1)} %gradient_sums.1.refs_0_), channel_id=1, source_target_pairs={{0,3},{1,0},{2,1},{3,2},{4,7},{5,4},{6,5},{7,6},{8,11},{9,8},{10,9... | collective-permute-start | bytes 36872 | tf_op jit(solution)/shard_map/ppermute | solution.py:421
  49.9 5.2 %local_convolutions.3 = (f32[128,8192]{1,0:T(8,128)}, f32[128,8192]{1,0:T(8,128)}) custom-call(bf16[1,128,8192]{2,1,0:T(8,128)(2,1)} %x_ref.5, bf16[1,128,8192]{2,1,0:T(8,128)(2,1)} %g_ref.5, f32[32,1,128]{2,1,0:T(1,128)} %bitcast.8, f32[8,8192]{1,0:T(8,128)} %res_ref.15, ...), custom_call_target="tpu_custom_call", output_to_operand_aliasing={{0}: (6, {}), {1}: (7, {})} | custom-call | flops 314572800 | bytes 2097152 | tf_op jit(solution)/shard_map/local_convolutions/pallas_call | solution.py:389
  55.1 0.0 collective-permute-done.1.refs_1_
  55.1 0.0 collective-permute-done.2.refs_2_
  55.1 0.0 collective-permute-done.3.refs_3_
  55.1 0.8 %total.1 = f32[32,24,128]{2,1,0:T(8,128)} custom-call(f32[24,128]{1,0:T(8,128)S(1)} %gradient_sums.1.refs_0_, f32[24,128]{1,0:T(8,128)S(1)} %collective-permute-done.1.refs_1_, f32[24,128]{1,0:T(8,128)S(1)} %collective-permute-done.2.refs_2_, f32[24,128]{1,0:T(8,128)S(1)} %collective-permute-done.3.refs_3_), custom_call_target="tpu_custom_call" | custom-call | tf_op jit(solution)/shard_map/total/pallas_call | solution.py:432
  55.9 0.0 collective-permute-done.4.far_ref
  55.9 0.0 copy-start.10
  55.9 0.3 all-to-all-done.1
  56.2 0.0 copy-start.9
  56.2 7.9 %all-to-all-start.2 = ((f32[32,24,128]{2,1,0:T(8,128)}), f32[32,24,128]{2,1,0:T(8,128)S(1)}, u32[]{:S(2)}, u32[]{:S(2)}) async-start(f32[32,24,128]{2,1,0:T(8,128)} %total.1), calls=%async_computation.2 | async-start | bytes 786432 | tf_op jit(solution)/shard_map/all_to_all | solution.py:439
  64.1 0.0 copy-done.10
  64.1 0.0 copy-done.9
  64.1 0.0 copy-start.7
  64.1 7.9 %add_carries.1 = (bf16[1,128,8192]{2,1,0:T(8,128)(2,1)}, bf16[1,128,8192]{2,1,0:T(8,128)(2,1)}) custom-call(s32[1]{0:T(128)} %bitcast.half_ref.core_ref, f32[128,8192]{1,0:T(8,128)} %get-tuple-element.52.mixed_ref, f32[128,8192]{1,0:T(8,128)} %get-tuple-element.53.grad_ref, f32[32,1,128]{2,1,0:T(1,128)} %bitcast.9, f32[8,512]{1,0:T(8,128)} %log_ref.7, ...), custom_call_target="tpu_custom_call" | custom-call | flops 1677721600 | bytes 12582912 | tf_op jit(solution)/shard_map/add_carries/pallas_call | solution.py:444
  72.0 2.4 %all-to-all-done.2.all_ref = f32[32,24,128]{2,1,0:T(8,128)S(1)} async-done(((f32[32,24,128]{2,1,0:T(8,128)}), f32[32,24,128]{2,1,0:T(8,128)S(1)}, u32[]{:S(2)}, u32[]{:S(2)}) %all-to-all-start.2) | async-done | bytes 393248 | tf_op jit(solution)/shard_map/all_to_all | solution.py:439
  74.4 0.0 copy-done.7
  74.4 0.7 unpack.1
  (1 shorter events, 0.0 us)
Async XLA Ops:
  0.6 8.4 %copy-start.5 = (bf16[256,256]{1,0:T(8,128)(2,1)S(1)}, bf16[256,256]{1,0:T(8,128)(2,1)}, u32[]{:S(2)}) copy-start(bf16[256,256]{1,0:T(8,128)(2,1)} %constant.31.clone.fwd_ref) | copy-start | bytes 393220
  0.6 8.4 %copy-start.4 = (bf16[128,768]{1,0:T(8,128)(2,1)S(1)}, bf16[128,768]{1,0:T(8,128)(2,1)}, u32[]{:S(2)}) copy-start(bf16[128,768]{1,0:T(8,128)(2,1)} %constant.32.clone.inv_ref) | copy-start | bytes 589828
  0.7 8.4 %copy-start = (bf16[1,128,8192]{2,1,0:T(8,128)(2,1)S(1)}, bf16[1,128,8192]{2,1,0:T(8,128)(2,1)}, u32[]{:S(2)}) copy-start(bf16[1,128,8192]{2,1,0:T(8,128)(2,1)} %x_ref.5) | copy-start | bytes 6291460
  0.7 8.4 %copy-start.6 = (f32[8,512]{1,0:T(8,128)S(1)}, f32[8,512]{1,0:T(8,128)}, u32[]{:S(2)}) copy-start(f32[8,512]{1,0:T(8,128)} %log_ref.7) | copy-start | bytes 49156
  0.7 8.4 %copy-start.2 = (f32[8,8192]{1,0:T(8,128)S(1)}, f32[8,8192]{1,0:T(8,128)}, u32[]{:S(2)}) copy-start(f32[8,8192]{1,0:T(8,128)} %res_ref.15) | copy-start | bytes 786436
  0.7 8.3 %copy-start.1 = (bf16[1,128,8192]{2,1,0:T(8,128)(2,1)S(1)}, bf16[1,128,8192]{2,1,0:T(8,128)(2,1)}, u32[]{:S(2)}) copy-start(bf16[1,128,8192]{2,1,0:T(8,128)(2,1)} %g_ref.5) | copy-start | bytes 6291460
  7.6 6.1 %collective-permute-start = (f32[16,104,128]{2,1,0:T(8,128)}, f32[16,104,128]{2,1,0:T(8,128)S(1)}, u32[]{:S(2)}, u32[]{:S(2)}) collective-permute-start(f32[16,104,128]{2,1,0:T(8,128)} %ends_and_lags.2), channel_id=1, source_target_pairs={{0,4},{4,0},{8,12},{12,8},{16,20},{20,16},{24,28},{28,24},{32,36},... | collective-permute-start | bytes 2555912 | tf_op jit(solution)/shard_map/ppermute | solution.py:325
  13.7 22.4 %copy-start.3 = (f32[8,8192]{1,0:T(8,128)S(1)}, f32[8,8192]{1,0:T(8,128)}, u32[]{:S(2)}) copy-start(f32[8,8192]{1,0:T(8,128)} %res_ref.15) | copy-start | bytes 786436
  15.0 0.7 copy-start.8
  15.7 20.4 %all-to-all-start = ((f32[16,88,128]{2,1,0:T(8,128)}), f32[16,88,128]{2,1,0:T(8,128)S(1)}, u32[]{:S(2)}, u32[]{:S(2)}) async-start(f32[16,88,128]{2,1,0:T(8,128)} %get-tuple-element.37), calls=%async_computation | async-start | bytes 1441792 | tf_op jit(solution)/shard_map/all_to_all | solution.py:322
  37.0 19.2 %all-to-all-start.1 = ((f32[32,32,128]{2,1,0:T(8,128)}), f32[32,32,128]{2,1,0:T(8,128)S(1)}, u32[]{:S(2)}, u32[]{:S(2)}) async-start(f32[32,32,128]{2,1,0:T(8,128)} %carries.1), calls=%async_computation.1 | async-start | bytes 1048576 | tf_op jit(solution)/shard_map/all_to_all | solution.py:412
  44.5 11.4 %collective-permute-start.4 = (f32[16,32,128]{2,1,0:T(8,128)S(1)}, f32[16,32,128]{2,1,0:T(8,128)S(1)}, u32[]{:S(2)}, u32[]{:S(2)}) collective-permute-start(f32[16,32,128]{2,1,0:T(8,128)S(1)} %get-tuple-element.51), channel_id=1, source_target_pairs={{0,4},{4,0},{8,12},{12,8},{16,20},{20,16},{24,28},{28,24},{32,36},... | collective-permute-start | bytes 786440 | tf_op jit(solution)/shard_map/ppermute | solution.py:325
  45.0 10.1 %collective-permute-start.1 = (f32[24,128]{1,0:T(8,128)S(1)}, f32[24,128]{1,0:T(8,128)S(1)}, u32[]{:S(2)}, u32[]{:S(2)}) collective-permute-start(f32[24,128]{1,0:T(8,128)S(1)} %gradient_sums.1.refs_0_), channel_id=1, source_target_pairs={{0,1},{1,2},{2,3},{3,0},{4,5},{5,6},{6,7},{7,4},{8,9},{9,10},{10,1... | collective-permute-start | bytes 36872 | tf_op jit(solution)/shard_map/ppermute | solution.py:421
  46.3 8.8 %collective-permute-start.2 = (f32[24,128]{1,0:T(8,128)S(1)}, f32[24,128]{1,0:T(8,128)S(1)}, u32[]{:S(2)}, u32[]{:S(2)}) collective-permute-start(f32[24,128]{1,0:T(8,128)S(1)} %gradient_sums.1.refs_0_), channel_id=1, source_target_pairs={{0,2},{1,3},{2,0},{3,1},{4,6},{5,7},{6,4},{7,5},{8,10},{9,11},{10,... | collective-permute-start | bytes 36872 | tf_op jit(solution)/shard_map/ppermute | solution.py:421
  48.7 6.4 %collective-permute-start.3 = (f32[24,128]{1,0:T(8,128)S(1)}, f32[24,128]{1,0:T(8,128)S(1)}, u32[]{:S(2)}, u32[]{:S(2)}) collective-permute-start(f32[24,128]{1,0:T(8,128)S(1)} %gradient_sums.1.refs_0_), channel_id=1, source_target_pairs={{0,3},{1,0},{2,1},{3,2},{4,7},{5,4},{6,5},{7,6},{8,11},{9,8},{10,9... | collective-permute-start | bytes 36872 | tf_op jit(solution)/shard_map/ppermute | solution.py:421
  55.9 8.2 %copy-start.10 = (f32[16,32,128]{2,1,0:T(8,128)}, f32[16,32,128]{2,1,0:T(8,128)S(1)}, u32[]{:S(2)}) copy-start(f32[16,32,128]{2,1,0:T(8,128)S(1)} %collective-permute-done.4.far_ref) | copy-start | bytes 786436
  56.2 7.9 %copy-start.9 = (f32[32,32,128]{2,1,0:T(8,128)}, f32[32,32,128]{2,1,0:T(8,128)S(1)}, u32[]{:S(2)}) copy-start(f32[32,32,128]{2,1,0:T(8,128)S(1)} %all-to-all-done.1) | copy-start | bytes 1572868
  56.2 18.2 %all-to-all-start.2 = ((f32[32,24,128]{2,1,0:T(8,128)}), f32[32,24,128]{2,1,0:T(8,128)S(1)}, u32[]{:S(2)}, u32[]{:S(2)}) async-start(f32[32,24,128]{2,1,0:T(8,128)} %total.1), calls=%async_computation.2 | async-start | bytes 786432 | tf_op jit(solution)/shard_map/all_to_all | solution.py:439
  64.1 10.3 %copy-start.7 = (f32[8,512]{1,0:T(8,128)S(1)}, f32[8,512]{1,0:T(8,128)}, u32[]{:S(2)}) copy-start(f32[8,512]{1,0:T(8,128)} %log_ref.7) | copy-start | bytes 49156

commit v10 on v9

--- a/solution.py
+++ b/solution.py
@@ -418,7 +418,7 @@
         cost_estimate=pl.CostEstimate(flops=10**10, bytes_accessed=10**7, transcendentals=0),
         name="gradient_sums",
     )(own[None], got, own_rate, residues)
-    arriving = [lax.ppermute(sums, "batch", [(i, (i + k) % rows) for i in range(rows)]) for k in range(1, rows)]
+    arriving = [lax.ppermute(sums, "batch", [(i, (i + k) % rows) for i in range(rows)]) for k in range(rows - 1, 0, -1)]
     far = other_core(mine)
     mixed_part, grad_part = convolutions(early, steps - early, x3, g3, mixed_part, grad_part)
 

time: 75.6 us -> 74.4 us (0.984)
  starting transfers between devices: 29.9 us -> 27.5 us
  waiting for transfers between devices: 2.63 us -> 3.84 us
    all_to_all x1, waiting for transfers between devices: 0.26 us -> 1.47 us  [local(): lax.all_to_all(back, 'seq', 0, 0, tiled=True).reshape(pairs, 2, 4 * M, SPAN)]
    ppermute x3, starting transfers between devices: 4.84 us -> 3.63 us  [local(): lax.ppermute(sums, 'batch', [(i, (i + k) % rows) for i in range(rows)])]
    all_to_all x1, starting transfers between devices: 7.91 us -> 6.7 us  [local(): everyone = lax.all_to_all(total, 'seq', 0, 0, tiled=True)]
  transfers between devices with their start and end apart: 8 -> 8, of which waited for: 2 -> 2; matrix products, arithmetic and copies ran while one was open for 2% -> 2% of each run, Pallas kernels for 40% -> 41%
where the time goes in v10:
time: 74.4 us; the launch traced here: 73.9 us
  Pallas kernels  39.9 us (54%)
  starting transfers between devices  27.5 us (37%)
  waiting for transfers between devices  3.84 us (5%)
  local copies, waits for them, and re-layouts  1.89 us (3%)
  between operations  0.83 us (1%)
    pallas_call x2, Pallas kernels, convolutions(): pl.pallas_call(second_kernel, grid=(count,), in_specs=kernel_blocks + [pl...  16.6 us
    pallas_call x2, Pallas kernels, ends_and_lags(): pl.pallas_call(first_kernel, grid_spec=pltpu.PrefetchScalarGridSpec(num_s...  11.6 us
    pallas_call x1, Pallas kernels, local(): pl.pallas_call(last_kernel, grid_spec=pltpu.PrefetchScalarGridSpec(num_sc...  7.92 us
    all_to_all x1, starting transfers between devices, exchange(): lax.all_to_all(values, 'seq', 0, 0, axis_index_groups=same_core, tiled=True)  7.85 us
    all_to_all x1, starting transfers between devices, local(): lax.all_to_all(back, 'seq', 0, 0, tiled=True).reshape(pairs, 2, 4 * M, SPAN)  7.56 us
    all_to_all x1, starting transfers between devices, local(): everyone = lax.all_to_all(total, 'seq', 0, 0, tiled=True)  6.7 us
    ppermute x3, starting transfers between devices, local(): lax.ppermute(sums, 'batch', [(i, (i + k) % rows) for i in range(rows)])  3.63 us
    all_to_all x1, waiting for transfers between devices, local(): everyone = lax.all_to_all(total, 'seq', 0, 0, tiled=True)  2.35 us
  transfers between devices with their start and end apart: 8, of which 2 were waited for; matrix products, arithmetic and copies ran while one was open for 2% of the time, Pallas kernels for 41%

profile of v10, /device:TPU:1, one launch (start us, length us, event | category | flops | bytes accessed | tf_op | source)
XLA Modules:
  0.0 73.9 jit_solution(1572382841811406902)
XLA Ops:
  0.6 0.0 copy-start.5
  0.6 0.0 copy-start.4
  0.7 0.0 copy-start
  0.7 0.0 copy-start.6
  0.7 0.0 copy-start.2
  0.7 0.0 copy-start.1
  0.7 6.9 %ends_and_lags.2 = f32[16,104,128]{2,1,0:T(8,128)} custom-call(s32[1]{0:T(128)S(6)} %sub.8.half_ref, bf16[1,128,8192]{2,1,0:T(8,128)(2,1)} %x_ref.5, bf16[1,128,8192]{2,1,0:T(8,128)(2,1)} %g_ref.5, f32[8,512]{1,0:T(8,128)} %log_ref.7, f32[8,8192]{1,0:T(8,128)} %res_ref.15, bf16[256,256]{1,0:T(8,128)(2,1)} %constant.31.clone.fwd_ref, ...), custom_call_target="tpu_custom_call" | custom-call | tf_op jit(solution)/shard_map/ends_and_lags/pallas_call | solution.py:328
  7.6 1.4 %collective-permute-start = (f32[16,104,128]{2,1,0:T(8,128)}, f32[16,104,128]{2,1,0:T(8,128)S(1)}, u32[]{:S(2)}, u32[]{:S(2)}) collective-permute-start(f32[16,104,128]{2,1,0:T(8,128)} %ends_and_lags.2), channel_id=1, source_target_pairs={{0,4},{4,0},{8,12},{12,8},{16,20},{20,16},{24,28},{28,24},{32,36},... | collective-permute-start | bytes 2555912 | tf_op jit(solution)/shard_map/ppermute | solution.py:325
  9.0 0.0 copy-done.5
  9.0 0.0 copy-done.4
  9.0 0.0 copy-done
  9.0 0.0 copy-done.6
  9.0 0.0 copy-done.2
  9.0 0.0 copy-done.1
  9.1 4.7 %ends_and_lags.3.kept_ref = f32[16,104,128]{2,1,0:T(8,128)S(1)} custom-call(s32[1]{0:T(128)} %bitcast.half_ref.core_ref, bf16[1,128,8192]{2,1,0:T(8,128)(2,1)S(1)} %copy-done, bf16[1,128,8192]{2,1,0:T(8,128)(2,1)S(1)} %copy-done.1, f32[8,512]{1,0:T(8,128)S(1)} %copy-done.6, f32[8,8192]{1,0:T(8,128)S(1)} %copy-done.2, bf16[256,256]{1,0:T(8,128)(2,1)S(1)} %copy-done.5, ...), custom_call_target="tpu_custom_call" | custom-call | tf_op jit(solution)/shard_map/ends_and_lags/pallas_call | solution.py:328
  13.7 0.0 copy-start.3
  13.7 0.0 collective-permute-done.arrived_ref
  13.7 1.3 %join_pair.1 = (f32[16,88,128]{2,1,0:T(8,128)}, f32[16,32,128]{2,1,0:T(8,128)S(1)}, f32[16,32,128]{2,1,0:T(8,128)S(1)}) custom-call(s32[1]{0:T(128)} %bitcast.half_ref.core_ref, f32[16,104,128]{2,1,0:T(8,128)S(1)} %ends_and_lags.3.kept_ref, f32[16,104,128]{2,1,0:T(8,128)S(1)} %collective-permute-done.arrived_ref, f32[8,8192]{1,0:T(8,128)S(1)} %copy-done.2), custom_call_target="tpu_custom_call" | custom-call | tf_op jit(solution)/shard_map/join_pair/pallas_call | solution.py:355
  15.0 0.0 copy-start.8
  15.0 0.7 copy-done.8
  15.7 7.9 %all-to-all-start = ((f32[16,88,128]{2,1,0:T(8,128)}), f32[16,88,128]{2,1,0:T(8,128)S(1)}, u32[]{:S(2)}, u32[]{:S(2)}) async-start(f32[16,88,128]{2,1,0:T(8,128)} %get-tuple-element.37), calls=%async_computation | async-start | bytes 1441792 | tf_op jit(solution)/shard_map/all_to_all | solution.py:322
  23.6 0.1 copy.13
  23.8 0.8 %reshape.17 = f32[32,1,128]{2,0,1:T(8,128)} reshape(f32[512,8]{1,0:T(8,128)S(1)} %copy.13) | data formatting | bytes 32768 | tf_op jit(solution)/shard_map/reshape | solution.py:375
  24.5 0.1 constant_dynamic-slice_fusion
  24.6 0.1 broadcast_in_dim.12
  24.7 0.1 reshape.18.rate_ref
  24.8 11.3 %local_convolutions.2 = (f32[128,8192]{1,0:T(8,128)}, f32[128,8192]{1,0:T(8,128)}) custom-call(bf16[1,128,8192]{2,1,0:T(8,128)(2,1)} %x_ref.5, bf16[1,128,8192]{2,1,0:T(8,128)(2,1)} %g_ref.5, f32[32,1,128]{2,1,0:T(1,128)} %bitcast.7, f32[8,8192]{1,0:T(8,128)} %res_ref.15, bf16[256,256]{1,0:T(8,128)(2,1)} %constant.31.clone.fwd_ref, ...), custom_call_target="tpu_custom_call" | custom-call | flops 314572800 | bytes 2097152 | tf_op jit(solution)/shard_map/local_convolutions/pallas_call | solution.py:389
  36.1 0.0 all-to-all-done.got_ref
  36.1 0.0 copy-done.3
  36.1 0.8 %carries.1 = f32[32,32,128]{2,1,0:T(8,128)} custom-call(s32[1]{0:T(128)} %bitcast.1.index_ref, f32[16,88,128]{2,1,0:T(8,128)S(1)} %all-to-all-done.got_ref, f32[8,256]{1,0:T(8,128)S(1)} %reshape.18.rate_ref, f32[8,8192]{1,0:T(8,128)S(1)} %copy-done.3), custom_call_target="tpu_custom_call" | custom-call | tf_op jit(solution)/shard_map/carries/pallas_call | solution.py:404
  37.0 7.6 %all-to-all-start.1 = ((f32[32,32,128]{2,1,0:T(8,128)}), f32[32,32,128]{2,1,0:T(8,128)S(1)}, u32[]{:S(2)}, u32[]{:S(2)}) async-start(f32[32,32,128]{2,1,0:T(8,128)} %carries.1), calls=%async_computation.1 | async-start | bytes 1048576 | tf_op jit(solution)/shard_map/all_to_all | solution.py:412
  44.5 0.3 collective-permute-start.4
  44.9 0.2 gradient_sums.1.refs_0_
  45.0 2.5 %collective-permute-start.1 = (f32[24,128]{1,0:T(8,128)S(1)}, f32[24,128]{1,0:T(8,128)S(1)}, u32[]{:S(2)}, u32[]{:S(2)}) collective-permute-start(f32[24,128]{1,0:T(8,128)S(1)} %gradient_sums.1.refs_0_), channel_id=1, source_target_pairs={{0,3},{1,0},{2,1},{3,2},{4,7},{5,4},{6,5},{7,6},{8,11},{9,8},{10,9... | collective-permute-start | bytes 36872 | tf_op jit(solution)/shard_map/ppermute | solution.py:421
  47.5 0.5 collective-permute-start.2
  48.1 0.6 collective-permute-start.3
  48.7 5.2 %local_convolutions.3 = (f32[128,8192]{1,0:T(8,128)}, f32[128,8192]{1,0:T(8,128)}) custom-call(bf16[1,128,8192]{2,1,0:T(8,128)(2,1)} %x_ref.5, bf16[1,128,8192]{2,1,0:T(8,128)(2,1)} %g_ref.5, f32[32,1,128]{2,1,0:T(1,128)} %bitcast.8, f32[8,8192]{1,0:T(8,128)} %res_ref.15, ...), custom_call_target="tpu_custom_call", output_to_operand_aliasing={{0}: (6, {}), {1}: (7, {})} | custom-call | flops 314572800 | bytes 2097152 | tf_op jit(solution)/shard_map/local_convolutions/pallas_call | solution.py:389
  53.9 0.0 collective-permute-done.1.refs_1_
  53.9 0.0 collective-permute-done.2.refs_2_
  53.9 0.0 collective-permute-done.3.refs_3_
  53.9 0.8 %total.1 = f32[32,24,128]{2,1,0:T(8,128)} custom-call(f32[24,128]{1,0:T(8,128)S(1)} %gradient_sums.1.refs_0_, f32[24,128]{1,0:T(8,128)S(1)} %collective-permute-done.1.refs_1_, f32[24,128]{1,0:T(8,128)S(1)} %collective-permute-done.2.refs_2_, f32[24,128]{1,0:T(8,128)S(1)} %collective-permute-done.3.refs_3_), custom_call_target="tpu_custom_call" | custom-call | tf_op jit(solution)/shard_map/total/pallas_call | solution.py:432
  54.7 0.0 collective-permute-done.4.far_ref
  54.7 0.0 copy-start.10
  54.7 1.5 %all-to-all-done.1 = f32[32,32,128]{2,1,0:T(8,128)S(1)} async-done(((f32[32,32,128]{2,1,0:T(8,128)}), f32[32,32,128]{2,1,0:T(8,128)S(1)}, u32[]{:S(2)}, u32[]{:S(2)}) %all-to-all-start.1) | async-done | bytes 524320 | tf_op jit(solution)/shard_map/all_to_all | solution.py:412
  56.2 0.0 copy-start.9
  56.2 6.7 %all-to-all-start.2 = ((f32[32,24,128]{2,1,0:T(8,128)}), f32[32,24,128]{2,1,0:T(8,128)S(1)}, u32[]{:S(2)}, u32[]{:S(2)}) async-start(f32[32,24,128]{2,1,0:T(8,128)} %total.1), calls=%async_computation.2 | async-start | bytes 786432 | tf_op jit(solution)/shard_map/all_to_all | solution.py:439
  62.9 0.0 copy-done.10
  62.9 0.0 copy-done.9
  62.9 0.0 copy-start.7
  62.9 7.9 %add_carries.1 = (bf16[1,128,8192]{2,1,0:T(8,128)(2,1)}, bf16[1,128,8192]{2,1,0:T(8,128)(2,1)}) custom-call(s32[1]{0:T(128)} %bitcast.half_ref.core_ref, f32[128,8192]{1,0:T(8,128)} %get-tuple-element.52.mixed_ref, f32[128,8192]{1,0:T(8,128)} %get-tuple-element.53.grad_ref, f32[32,1,128]{2,1,0:T(1,128)} %bitcast.9, f32[8,512]{1,0:T(8,128)} %log_ref.7, ...), custom_call_target="tpu_custom_call" | custom-call | flops 1677721600 | bytes 12582912 | tf_op jit(solution)/shard_map/add_carries/pallas_call | solution.py:444
  70.8 2.4 %all-to-all-done.2.all_ref = f32[32,24,128]{2,1,0:T(8,128)S(1)} async-done(((f32[32,24,128]{2,1,0:T(8,128)}), f32[32,24,128]{2,1,0:T(8,128)S(1)}, u32[]{:S(2)}, u32[]{:S(2)}) %all-to-all-start.2) | async-done | bytes 393248 | tf_op jit(solution)/shard_map/all_to_all | solution.py:439
  73.2 0.0 copy-done.7
  73.2 0.7 unpack.1
  (1 shorter events, 0.0 us)
Async XLA Ops:
  0.6 8.4 %copy-start.5 = (bf16[256,256]{1,0:T(8,128)(2,1)S(1)}, bf16[256,256]{1,0:T(8,128)(2,1)}, u32[]{:S(2)}) copy-start(bf16[256,256]{1,0:T(8,128)(2,1)} %constant.31.clone.fwd_ref) | copy-start | bytes 393220
  0.6 8.4 %copy-start.4 = (bf16[128,768]{1,0:T(8,128)(2,1)S(1)}, bf16[128,768]{1,0:T(8,128)(2,1)}, u32[]{:S(2)}) copy-start(bf16[128,768]{1,0:T(8,128)(2,1)} %constant.32.clone.inv_ref) | copy-start | bytes 589828
  0.7 8.4 %copy-start = (bf16[1,128,8192]{2,1,0:T(8,128)(2,1)S(1)}, bf16[1,128,8192]{2,1,0:T(8,128)(2,1)}, u32[]{:S(2)}) copy-start(bf16[1,128,8192]{2,1,0:T(8,128)(2,1)} %x_ref.5) | copy-start | bytes 6291460
  0.7 8.4 %copy-start.6 = (f32[8,512]{1,0:T(8,128)S(1)}, f32[8,512]{1,0:T(8,128)}, u32[]{:S(2)}) copy-start(f32[8,512]{1,0:T(8,128)} %log_ref.7) | copy-start | bytes 49156
  0.7 8.4 %copy-start.2 = (f32[8,8192]{1,0:T(8,128)S(1)}, f32[8,8192]{1,0:T(8,128)}, u32[]{:S(2)}) copy-start(f32[8,8192]{1,0:T(8,128)} %res_ref.15) | copy-start | bytes 786436
  0.7 8.3 %copy-start.1 = (bf16[1,128,8192]{2,1,0:T(8,128)(2,1)S(1)}, bf16[1,128,8192]{2,1,0:T(8,128)(2,1)}, u32[]{:S(2)}) copy-start(bf16[1,128,8192]{2,1,0:T(8,128)(2,1)} %g_ref.5) | copy-start | bytes 6291460
  7.6 6.1 %collective-permute-start = (f32[16,104,128]{2,1,0:T(8,128)}, f32[16,104,128]{2,1,0:T(8,128)S(1)}, u32[]{:S(2)}, u32[]{:S(2)}) collective-permute-start(f32[16,104,128]{2,1,0:T(8,128)} %ends_and_lags.2), channel_id=1, source_target_pairs={{0,4},{4,0},{8,12},{12,8},{16,20},{20,16},{24,28},{28,24},{32,36},... | collective-permute-start | bytes 2555912 | tf_op jit(solution)/shard_map/ppermute | solution.py:325
  13.7 22.4 %copy-start.3 = (f32[8,8192]{1,0:T(8,128)S(1)}, f32[8,8192]{1,0:T(8,128)}, u32[]{:S(2)}) copy-start(f32[8,8192]{1,0:T(8,128)} %res_ref.15) | copy-start | bytes 786436
  15.0 0.7 copy-start.8
  15.7 20.4 %all-to-all-start = ((f32[16,88,128]{2,1,0:T(8,128)}), f32[16,88,128]{2,1,0:T(8,128)S(1)}, u32[]{:S(2)}, u32[]{:S(2)}) async-start(f32[16,88,128]{2,1,0:T(8,128)} %get-tuple-element.37), calls=%async_computation | async-start | bytes 1441792 | tf_op jit(solution)/shard_map/all_to_all | solution.py:322
  37.0 19.2 %all-to-all-start.1 = ((f32[32,32,128]{2,1,0:T(8,128)}), f32[32,32,128]{2,1,0:T(8,128)S(1)}, u32[]{:S(2)}, u32[]{:S(2)}) async-start(f32[32,32,128]{2,1,0:T(8,128)} %carries.1), calls=%async_computation.1 | async-start | bytes 1048576 | tf_op jit(solution)/shard_map/all_to_all | solution.py:412
  44.5 10.1 %collective-permute-start.4 = (f32[16,32,128]{2,1,0:T(8,128)S(1)}, f32[16,32,128]{2,1,0:T(8,128)S(1)}, u32[]{:S(2)}, u32[]{:S(2)}) collective-permute-start(f32[16,32,128]{2,1,0:T(8,128)S(1)} %get-tuple-element.51), channel_id=1, source_target_pairs={{0,4},{4,0},{8,12},{12,8},{16,20},{20,16},{24,28},{28,24},{32,36},... | collective-permute-start | bytes 786440 | tf_op jit(solution)/shard_map/ppermute | solution.py:325
  45.0 8.8 %collective-permute-start.1 = (f32[24,128]{1,0:T(8,128)S(1)}, f32[24,128]{1,0:T(8,128)S(1)}, u32[]{:S(2)}, u32[]{:S(2)}) collective-permute-start(f32[24,128]{1,0:T(8,128)S(1)} %gradient_sums.1.refs_0_), channel_id=1, source_target_pairs={{0,3},{1,0},{2,1},{3,2},{4,7},{5,4},{6,5},{7,6},{8,11},{9,8},{10,9... | collective-permute-start | bytes 36872 | tf_op jit(solution)/shard_map/ppermute | solution.py:421
  47.5 6.3 %collective-permute-start.2 = (f32[24,128]{1,0:T(8,128)S(1)}, f32[24,128]{1,0:T(8,128)S(1)}, u32[]{:S(2)}, u32[]{:S(2)}) collective-permute-start(f32[24,128]{1,0:T(8,128)S(1)} %gradient_sums.1.refs_0_), channel_id=1, source_target_pairs={{0,2},{1,3},{2,0},{3,1},{4,6},{5,7},{6,4},{7,5},{8,10},{9,11},{10,... | collective-permute-start | bytes 36872 | tf_op jit(solution)/shard_map/ppermute | solution.py:421
  48.1 5.8 %collective-permute-start.3 = (f32[24,128]{1,0:T(8,128)S(1)}, f32[24,128]{1,0:T(8,128)S(1)}, u32[]{:S(2)}, u32[]{:S(2)}) collective-permute-start(f32[24,128]{1,0:T(8,128)S(1)} %gradient_sums.1.refs_0_), channel_id=1, source_target_pairs={{0,1},{1,2},{2,3},{3,0},{4,5},{5,6},{6,7},{7,4},{8,9},{9,10},{10,1... | collective-permute-start | bytes 36872 | tf_op jit(solution)/shard_map/ppermute | solution.py:421
  54.7 8.2 %copy-start.10 = (f32[16,32,128]{2,1,0:T(8,128)}, f32[16,32,128]{2,1,0:T(8,128)S(1)}, u32[]{:S(2)}) copy-start(f32[16,32,128]{2,1,0:T(8,128)S(1)} %collective-permute-done.4.far_ref) | copy-start | bytes 786436
  56.2 6.7 %copy-start.9 = (f32[32,32,128]{2,1,0:T(8,128)}, f32[32,32,128]{2,1,0:T(8,128)S(1)}, u32[]{:S(2)}) copy-start(f32[32,32,128]{2,1,0:T(8,128)S(1)} %all-to-all-done.1) | copy-start | bytes 1572868
  56.2 17.0 %all-to-all-start.2 = ((f32[32,24,128]{2,1,0:T(8,128)}), f32[32,24,128]{2,1,0:T(8,128)S(1)}, u32[]{:S(2)}, u32[]{:S(2)}) async-start(f32[32,24,128]{2,1,0:T(8,128)} %total.1), calls=%async_computation.2 | async-start | bytes 786432 | tf_op jit(solution)/shard_map/all_to_all | solution.py:439
  62.9 10.3 %copy-start.7 = (f32[8,512]{1,0:T(8,128)S(1)}, f32[8,512]{1,0:T(8,128)}, u32[]{:S(2)}) copy-start(f32[8,512]{1,0:T(8,128)} %log_ref.7) | copy-start | bytes 49156
